TPU v7x, 32 devices: a whole 2x2x4 slice. The times are simulated.
32 devices in a mesh: row: 8 (over z, core), col: 4 (over y, x).
Axes of the slice: x: 2, y: 2, z: 4, core: 2. Of those that a mesh axis runs over, the one named last changes fastest.
Arguments:
- values: bfloat16 [16, 8, 128, 128], P('row', 'col'), as said below
- columns: int32 [16, 8], P('row', 'col'), may hold values from 0 to 15, as said below
Outputs:
- sign_blocks: float32 [16, 8, 128, 128], P('row', 'col')
Inputs may be any that keep to these rules, and one draw needn't show every extreme that they name: Block row i keeps 2 distinct block columns in each panel of 4 consecutive block columns, slot s lying in panel s // 2; slot (i // 4) * 2 of row i is its diagonal block; the pattern is symmetric: j is kept in row i exactly when i is kept in row j. `values`: the blocks are those of a symmetric matrix.
All inputs are finite; a program needn't handle non-finite values.
Results may differ from a plain program's by a relative error of at most 0.003.
Values may be sent and summed in bfloat16 or wider, within the bound.
No kernel may reach another device: no remote copies, remote signals or barrier semaphores. Data moves between devices by JAX's collectives and lax.ppermute only.
A program may use at most 64 MiB of HBM per device.

v0:
```python
import jax
import jax.numpy as jnp
from jax import lax
from jax.sharding import PartitionSpec as P


def select_blocks(panel_blocks, panel_slots, row_columns, targets):
    partner = jnp.take(panel_slots, row_columns, axis=0)
    width = partner.shape[2]
    match = partner[:, :, :, None] == targets[:, None, None, :]
    found = jnp.any(match, axis=2)
    where_slot = jnp.sum(
        jnp.where(match, jnp.arange(width, dtype=jnp.int32)[None, None, :, None], 0), axis=2
    )
    picked = panel_blocks[row_columns[:, :, None], where_slot]
    return jnp.where(found[:, :, :, None, None], picked, jnp.zeros((), picked.dtype))


def partial_product(row_blocks, row_columns, panel_blocks, panel_slots, targets):
    picked = select_blocks(panel_blocks, panel_slots, row_columns, targets)
    return jnp.einsum("bsxz,bstzy->btxy", row_blocks, picked, preferred_element_type=jnp.float32)


def gather_panel(blocks):
    return lax.all_gather(blocks, "row", axis=0, tiled=True)


def per_device(values, columns):
    rows_here, slots_here, block = (values.shape[0], values.shape[1], values.shape[2])
    row_ids = lax.axis_index("row") * rows_here + jnp.arange(rows_here, dtype=jnp.int32)
    on_diagonal = (columns == row_ids[:, None]).astype(jnp.float32)
    identity = on_diagonal[:, :, None, None] * jnp.eye(block, dtype=jnp.float32)[None, None, :, :]
    panel_blocks = lax.all_gather(values, "row", axis=0, tiled=True)
    panel_slots = lax.all_gather(columns, "row", axis=0, tiled=True)
    row_blocks = lax.all_gather(values, "col", axis=1, tiled=True)
    row_columns = lax.all_gather(columns, "col", axis=1, tiled=True)
    square = partial_product(row_blocks, row_columns, panel_blocks, panel_slots, columns)
    square_low = square.astype(jnp.bfloat16)
    square_panel = gather_panel(square_low)
    square_rows = lax.all_gather(square_low, "col", axis=1, tiled=True)
    fourth = partial_product(square_rows, row_columns, square_panel, panel_slots, columns)
    polynomial = (15.0 * identity - 10.0 * square_low.astype(jnp.float32) + 3.0 * fourth).astype(
        jnp.bfloat16
    )
    polynomial_panel = gather_panel(polynomial)
    updated = (
        partial_product(row_blocks, row_columns, polynomial_panel, panel_slots, columns) * 0.125
    )
    return updated


def solution(mesh):
    in_specs = (P("row", "col", None, None), P("row", "col"))
    out_specs = P("row", "col", None, None)
    return jax.shard_map(
        per_device, mesh=mesh, in_specs=in_specs, out_specs=out_specs, check_vma=False
    )
```

profile of v0, /device:TPU:0, one launch (start us, length us, event | category | flops | bytes accessed | tf_op | source)
XLA Modules:
  0.0 100.9 jit_solution(3661939698221606958)
XLA Ops:
  6.5 0.7 all-gather.6.cloned.1.call-update
  7.3 0.0 all-gather.8.cloned.1.call-start
  7.3 0.6 copy-done.1
  7.9 0.1 copy.41
  8.0 9.5 %all-gather.1 = s32[4,2,2]{2,1,0:T(2,128)S(1)} all-gather(s32[1,2,2]{2,1,0:T(2,128)S(1)} %bitcast.76), channel_id=1, replica_groups=mesh['row'=8,'col'=4] {'col'}, dimensions={0}, use_global_device_ids=true | all-gather | bytes 80 | tf_op jit(solution)/shard_map/all_gather | solution.py:36
  17.5 0.1 copy.60
  17.6 0.1 reshape.71
  17.7 12.0 %all-gather = s32[8,2,2]{2,1,0:T(2,128)S(1)} all-gather(s32[1,2,2]{2,1,0:T(2,128)S(1)} %bitcast.74), channel_id=1, replica_groups=mesh['row'=8,'col'=4] {'row'}, dimensions={0}, use_global_device_ids=true | all-gather | bytes 144 | tf_op jit(solution)/shard_map/all_gather | solution.py:34
  29.7 0.6 gather_fusion.3
  30.3 0.1 copy.62
  30.4 0.1 fusion.21
  30.5 0.1 copy.47
  30.6 0.1 reshape.47
  30.7 10.3 %all_gather.24 = bf16[2,8,128,128]{3,2,1,0:T(8,128)(2,1)S(1)} all-gather(bf16[2,2,128,128]{3,2,1,0:T(8,128)(2,1)S(1)} %copy-done), channel_id=1, replica_groups=mesh['row'=8,'col'=4] {'col'}, dimensions={1}, use_global_device_ids=true | all-gather | bytes 655360 | tf_op jit(solution)/shard_map/all_gather | solution.py:35
  41.0 0.1 compare_reduce_fusion
  41.1 2.0 %gather_fusion = bf16[32,128,128]{2,1,0:T(8,128)(2,1)S(1)} fusion(bf16[16,2,128,128]{3,2,1,0:T(8,128)(2,1)} %all-gather.6.cloned.1.call-done, s32[32]{0:T(128)S(1)} %reshape.47), kind=kCustom, calls=%fused_computation.1 | custom fusion | bytes 2097408 | tf_op jit(solution)/shard_map/gather | solution.py:15
  43.1 0.7 copy.48
  43.8 0.5 fusion.7
  44.2 0.8 copy.49
  45.0 0.0 all-gather.10.cloned.1.call-start
  45.1 0.1 compare_convert_fusion
  45.2 9.1 %all_gather.26 = bf16[2,8,128,128]{2,3,1,0:T(8,128)(2,1)S(1)} all-gather(bf16[2,2,128,128]{2,3,1,0:T(8,128)(2,1)S(1)} %fusion.7), channel_id=1, replica_groups=mesh['row'=8,'col'=4] {'col'}, dimensions={1}, use_global_device_ids=true | all-gather | bytes 655360 | tf_op jit(solution)/shard_map/all_gather | solution.py:40
  54.3 10.3 %all-gather.8.cloned.1.call-done = bf16[16,2,128,128]{3,2,1,0:T(8,128)(2,1)} async-done(((bf16[2,2,128,128]{3,2,1,0:T(8,128)(2,1)}), bf16[16,2,128,128]{3,2,1,0:T(8,128)(2,1)}) %all-gather.8.cloned.1.call-update) | async-done | bytes 1048592 | tf_op jit(solution)/shard_map/all_gather | solution.py:25
  64.5 2.0 %gather_fusion.1 = bf16[32,128,128]{2,1,0:T(8,128)(2,1)S(1)} fusion(bf16[16,2,128,128]{3,2,1,0:T(8,128)(2,1)} %all-gather.8.cloned.1.call-done, s32[32]{0:T(128)S(1)} %reshape.47), kind=kCustom, calls=%fused_computation.2 | custom fusion | bytes 2097408 | tf_op jit(solution)/shard_map/gather | solution.py:15
  66.5 0.7 copy.50
  67.2 0.5 fusion.6
  67.7 0.8 copy.52
  68.5 21.8 %all-gather.10.cloned.1.call-done = bf16[16,2,128,128]{3,2,1,0:T(8,128)(2,1)} async-done(((bf16[2,2,128,128]{3,2,1,0:T(8,128)(2,1)}), bf16[16,2,128,128]{3,2,1,0:T(8,128)(2,1)}) %all-gather.10.cloned.1.call-update) | async-done | bytes 1048592 | tf_op jit(solution)/shard_map/all_gather | solution.py:25
  90.3 2.0 %gather_fusion.2 = bf16[32,128,128]{2,1,0:T(8,128)(2,1)S(1)} fusion(bf16[16,2,128,128]{3,2,1,0:T(8,128)(2,1)} %all-gather.10.cloned.1.call-done, s32[32]{0:T(128)S(1)} %reshape.47), kind=kCustom, calls=%fused_computation.3 | custom fusion | bytes 2097408 | tf_op jit(solution)/shard_map/gather | solution.py:15
  92.3 0.7 copy.53
  93.0 0.5 fusion.1
  93.5 0.8 copy.54
  (15 shorter events, 0.1 us)
Async XLA Ops:
  6.5 24.1 %copy-start = (bf16[2,2,128,128]{3,2,1,0:T(8,128)(2,1)S(1)}, bf16[2,2,128,128]{3,2,1,0:T(8,128)(2,1)}, u32[]{:S(2)}) copy-start(bf16[2,2,128,128]{3,2,1,0:T(8,128)(2,1)} %param.4) | copy-start | bytes 393220
  6.5 34.5 %all-gather.6.cloned.1.call-start = ((), (), s32[]{:S(2)}) async-start(), calls=%async_computation | async-start | bytes 1179648 | tf_op jit(solution)/shard_map/all_gather | solution.py:33
  7.3 0.7 copy-start.1
  7.3 57.3 %all-gather.8.cloned.1.call-start = ((), (), s32[]{:S(2)}) async-start(), calls=%async_computation.1 | async-start | bytes 1179648 | tf_op jit(solution)/shard_map/all_gather | solution.py:25
  45.0 45.3 %all-gather.10.cloned.1.call-start = ((), (), s32[]{:S(2)}) async-start(), calls=%async_computation.2 | async-start | bytes 1179648 | tf_op jit(solution)/shard_map/all_gather | solution.py:25
Sparse Core Ops, SparseCore 0:
  9.0 24.7 all-gather.5
  45.2 19.3 all-gather.7
  68.6 21.6 all-gather.9
where the time goes:
time: 101 us
  blocking collectives  40.9 us (40%)
  waiting for transfers between devices  32.9 us (33%)
  between operations  13.2 us (13%)
  local copies, waits for them, and re-layouts  12.1 us (12%)
  matrix products  1.45 us (1%)
    all_gather x2, waiting for transfers between devices, gather_panel(): return lax.all_gather(blocks, 'row', axis=0, tiled=True)  32.1 us
    all_gather x1, blocking collectives, per_device(): panel_slots = lax.all_gather(columns, 'row', axis=0, tiled=True)  12 us
    all_gather x1, blocking collectives, per_device(): row_blocks = lax.all_gather(values, 'col', axis=1, tiled=True)  10.3 us
    all_gather x1, blocking collectives, per_device(): row_columns = lax.all_gather(columns, 'col', axis=1, tiled=True)  9.5 us
    all_gather x1, blocking collectives, per_device(): square_rows = lax.all_gather(square_low, 'col', axis=1, tiled=True)  9.07 us
    gather x6, local copies, waits for them, and re-layouts, select_blocks(): picked = panel_blocks[row_columns[:, :, None], where_slot]  8.01 us
  transfers between devices with their start and end apart: 3, of which 2 were waited for; matrix products, arithmetic and copies ran while one was open for 1% of the time, Pallas kernels for 0%

commit v1 on v0

--- a/solution.py
+++ b/solution.py
@@ -1,7 +1,13 @@
+import functools
+
 import jax
 import jax.numpy as jnp
 from jax import lax
+from jax.experimental import pallas as pl
+from jax.experimental.pallas import tpu as pltpu
 from jax.sharding import PartitionSpec as P
+
+REPLICA_LIMIT = 8 * 1024 * 1024
 
 
 def select_blocks(panel_blocks, panel_slots, row_columns, targets):
@@ -25,7 +31,7 @@
     return lax.all_gather(blocks, "row", axis=0, tiled=True)
 
 
-def per_device(values, columns):
+def per_device_panels(values, columns):
     rows_here, slots_here, block = (values.shape[0], values.shape[1], values.shape[2])
     row_ids = lax.axis_index("row") * rows_here + jnp.arange(rows_here, dtype=jnp.int32)
     on_diagonal = (columns == row_ids[:, None]).astype(jnp.float32)
@@ -49,6 +55,143 @@
     return updated
 
 
+def local_iteration(
+    rows, kept, rows_here, slots_here, place, columns, origin, blocks, out, xs, ys, qs, table, sem
+):
+    count = rows * kept
+    size = xs.shape[1]
+    copy = pltpu.make_async_copy(blocks, xs.at[pl.ds(0, count)], sem)
+    copy.start()
+
+    def clear(at, carry):
+        table[at] = count
+        return carry
+
+    def enter(at, carry):
+        table[lax.div(at, kept) * rows + columns[at]] = at
+        return carry
+
+    lax.fori_loop(0, rows * rows, clear, 0, unroll=8)
+    lax.fori_loop(0, count, enter, 0, unroll=8)
+    nothing = jnp.zeros((size, size), jnp.bfloat16)
+    xs[count] = nothing
+    ys[count] = nothing
+    qs[rows * slots_here] = nothing
+    row_here, panel = origin[0], origin[1]
+    copy.wait()
+
+    def wide(parts):
+        return jnp.concatenate(parts, axis=1)
+
+    def tall(parts):
+        return jnp.concatenate(parts, axis=0)
+
+    def dot(left, right):
+        return jnp.dot(left, right, preferred_element_type=jnp.float32)
+
+    def square(i, carry):
+        ks = [columns[i * kept + s] for s in range(kept)]
+        left = wide([xs[place(i * kept + s)] for s in range(kept)])
+        for first in range(0, kept, slots_here):
+            right = tall(
+                [
+                    wide(
+                        [xs[place(table[k * rows + ks[first + t]])] for t in range(slots_here)]
+                    )
+                    for k in ks
+                ]
+            )
+            product = dot(left, right).astype(jnp.bfloat16)
+            for t in range(slots_here):
+                ys[i * kept + first + t] = product[:, t * size : (t + 1) * size]
+        return carry
+
+    lax.fori_loop(0, rows, square, 0)
+
+    eye = (
+        lax.broadcasted_iota(jnp.int32, (size, size), 0)
+        == lax.broadcasted_iota(jnp.int32, (size, size), 1)
+    ).astype(jnp.float32)
+
+    def polynomial(i, carry):
+        ks = [columns[i * kept + s] for s in range(kept)]
+        first = i * kept + panel * slots_here
+        js = [columns[first + t] for t in range(slots_here)]
+        left = wide([ys[i * kept + s] for s in range(kept)])
+        right = tall([wide([ys[table[k * rows + j]] for j in js]) for k in ks])
+        fourth = dot(left, right)
+        for t in range(slots_here):
+            scale = jnp.where(js[t] == i, 15.0, 0.0)
+            low = ys[first + t].astype(jnp.float32)
+            value = scale * eye - 10.0 * low + 3.0 * fourth[:, t * size : (t + 1) * size]
+            qs[i * slots_here + t] = value.astype(jnp.bfloat16)
+        return carry
+
+    lax.fori_loop(0, rows, polynomial, 0)
+
+    for a in range(rows_here):
+        i = row_here + a
+        ks = [columns[i * kept + s] for s in range(kept)]
+        js = [columns[i * kept + panel * slots_here + t] for t in range(slots_here)]
+
+        def entry(k, j):
+            at = table[k * rows + j]
+            inside = k * slots_here + lax.rem(at, slots_here)
+            return jnp.where(at == count, rows * slots_here, inside)
+
+        left = wide([xs[place(i * kept + s)] for s in range(kept)])
+        right = tall([wide([qs[entry(k, j)] for j in js]) for k in ks])
+        updated = dot(left, right) * 0.125
+        for t in range(slots_here):
+            out[a, t] = updated[:, t * size : (t + 1) * size]
+
+
+def per_device_whole(values, columns):
+    rows_here, slots_here, size = values.shape[0], values.shape[1], values.shape[2]
+    panels = lax.axis_size("col")
+    rows = rows_here * lax.axis_size("row")
+    kept = slots_here * panels
+    blocks = lax.all_gather(values, ("row", "col"), axis=0, tiled=True)
+    blocks = blocks.reshape(rows * kept, size, size)
+    slots = lax.all_gather(columns, ("row", "col"), axis=0, tiled=False)
+    slots = slots.reshape(rows // rows_here, panels, rows_here, slots_here)
+    slots = slots.transpose(0, 2, 1, 3).reshape(rows * kept)
+    origin = jnp.stack([lax.axis_index("row") * rows_here, lax.axis_index("col")])
+
+    def place(at):
+        i, s = lax.div(at, kept), lax.rem(at, kept)
+        band = lax.div(i, rows_here) * panels + lax.div(s, slots_here)
+        return (band * rows_here + lax.rem(i, rows_here)) * slots_here + lax.rem(s, slots_here)
+
+    count = rows * kept
+    return pl.pallas_call(
+        functools.partial(local_iteration, rows, kept, rows_here, slots_here, place),
+        out_shape=jax.ShapeDtypeStruct(values.shape, jnp.float32),
+        in_specs=[
+            pl.BlockSpec(memory_space=pltpu.SMEM),
+            pl.BlockSpec(memory_space=pltpu.SMEM),
+            pl.BlockSpec(memory_space=pl.ANY),
+        ],
+        out_specs=pl.BlockSpec(memory_space=pltpu.VMEM),
+        scratch_shapes=[
+            pltpu.VMEM((count + 1, size, size), jnp.bfloat16),
+            pltpu.VMEM((count + 1, size, size), jnp.bfloat16),
+            pltpu.VMEM((rows * slots_here + 1, size, size), jnp.bfloat16),
+            pltpu.SMEM((rows * rows,), jnp.int32),
+            pltpu.SemaphoreType.DMA,
+        ],
+        compiler_params=pltpu.CompilerParams(vmem_limit_bytes=32 * 1024 * 1024),
+    )(slots, origin.astype(jnp.int32), blocks)
+
+
+def per_device(values, columns):
+    devices = lax.axis_size("row") * lax.axis_size("col")
+    whole = devices * values.size * values.dtype.itemsize
+    if whole <= REPLICA_LIMIT:
+        return per_device_whole(values, columns)
+    return per_device_panels(values, columns)
+
+
 def solution(mesh):
     in_specs = (P("row", "col", None, None), P("row", "col"))
     out_specs = P("row", "col", None, None)

time: 101 us -> 109 us (1.079)
  waiting for transfers between devices: 32.9 us -> 0.71 us
  blocking collectives: 40.9 us -> 70.1 us
  Pallas kernels: 0 us -> 21.8 us
  local copies, waits for them, and re-layouts: 12.1 us -> 2.74 us
  matrix products: 1.45 us -> 0 us
    all_gather x3 -> x1, waiting for transfers between devices: 32.1 us -> 0.01 us  [per_device_whole(): blocks = lax.all_gather(values, ('row', 'col'), axis=0, tiled=True)]
    all_gather x4 -> x1, blocking collectives: 40.9 us -> 70.1 us  [per_device_whole(): slots = lax.all_gather(columns, ('row', 'col'), axis=0, tiled=False)]
    pallas_call x0 -> x1, Pallas kernels: none -> 21.8 us  [per_device_whole(): pl.pallas_call(functools.partial(local_iteration, rows, kept, rows_here,...]
    gather x8 -> x0, local copies, waits for them, and re-layouts: 8.65 us -> none  [the longest x6 8.01 us: select_blocks(): picked = panel_blocks[row_columns[:, :, None], where_slot]]
    convert_element_type x2 -> x0, local copies, waits for them, and re-layouts: 1.54 us -> none  [the longest x1 0.77 us: per_device(): square_low = square.astype(jnp.bfloat16)]
    dot_general x3 -> x0, matrix products: 1.45 us -> none  [partial_product(): jnp.einsum('bsxz,bstzy->btxy', row_blocks, picked, preferred_element_type...]
    unnamed x6 -> x2, local copies, waits for them, and re-layouts: 0.8 us -> 2.19 us
  transfers between devices with their start and end apart: 3 -> 1, of which waited for: 2 -> 0; matrix products, arithmetic and copies ran while one was open for 1% -> 1% of each run, Pallas kernels for 0% -> 0%
where the time goes in v1:
time: 109 us
  blocking collectives  70.1 us (64%)
  Pallas kernels  21.8 us (20%)
  between operations  13.4 us (12%)
  local copies, waits for them, and re-layouts  2.74 us (3%)
    all_gather x1, blocking collectives, per_device_whole(): slots = lax.all_gather(columns, ('row', 'col'), axis=0, tiled=False)  70.1 us
    pallas_call x1, Pallas kernels, per_device_whole(): pl.pallas_call(functools.partial(local_iteration, rows, kept, rows_here,...  21.8 us
    unnamed x2, local copies, waits for them, and re-layouts  2.19 us
  transfers between devices with their start and end apart: 1, of which 0 were waited for; matrix products, arithmetic and copies ran while one was open for 1% of the time, Pallas kernels for 0%

profile of v1, /device:TPU:0, one launch (start us, length us, event | category | flops | bytes accessed | tf_op | source)
XLA Modules:
  0.0 108.9 jit_solution(3368971989525472187)
XLA Ops:
  6.5 0.0 all-gather.4.cloned.1.call-start
  6.5 0.7 all-gather.4.cloned.1.call-update
  7.3 70.1 %all-gather.1 = s32[32,2,2]{2,1,0:T(2,128)S(1)} all-gather(s32[1,2,2]{2,1,0:T(2,128)} %bitcast.9), channel_id=2, replica_groups=mesh['row'=8,'col'=4] {'row','col'}, dimensions={0}, use_global_device_ids=true | all-gather | bytes 528 | tf_op jit(solution)/shard_map/all_gather | solution.py:156
  77.4 0.2 copy.9
  77.6 0.2 copy.8
  77.8 0.1 reshape.10.columns
  78.0 0.1 pad_add_fusion.origin
  78.0 0.0 all-gather.4.cloned.1.call-done
  78.0 0.0 copy-start
  78.0 2.2 %copy-done = bf16[64,2,128,128]{3,2,1,0:T(8,128)(2,1)S(1)} copy-done((bf16[64,2,128,128]{3,2,1,0:T(8,128)(2,1)S(1)}, bf16[64,2,128,128]{3,2,1,0:T(8,128)(2,1)}, u32[]{:S(2)}) %copy-start) | copy-done | bytes 4194328
  80.2 21.8 %shard_map.28 = f32[2,2,128,128]{3,2,1,0:T(8,128)} custom-call(s32[128]{0:T(128)S(1)} %reshape.10.columns, s32[2]{0:T(128)S(1)} %pad_add_fusion.origin, bf16[128,128,128]{2,1,0:T(8,128)(2,1)S(1)} %bitcast.6), custom_call_target="tpu_custom_call" | custom-call | tf_op jit(solution)/shard_map/pallas_call | solution.py:167
Async XLA Ops:
  6.5 71.5 %all-gather.4.cloned.1.call-start = ((), (), s32[]{:S(2)}) async-start(), calls=%async_computation | async-start | bytes 4325376 | tf_op jit(solution)/shard_map/all_gather | solution.py:154
  78.0 2.2 %copy-start = (bf16[64,2,128,128]{3,2,1,0:T(8,128)(2,1)S(1)}, bf16[64,2,128,128]{3,2,1,0:T(8,128)(2,1)}, u32[]{:S(2)}) copy-start(bf16[64,2,128,128]{3,2,1,0:T(8,128)(2,1)} %all-gather.4.cloned.1.call-done) | copy-start | bytes 12582916
Sparse Core Ops, SparseCore 0:
  10.2 64.7 all-gather.3

commit v2 on v0

--- a/solution.py
+++ b/solution.py
@@ -1,8 +1,11 @@
+import functools
+
 import jax
 import jax.numpy as jnp
 from jax import lax
+from jax.experimental import pallas as pl
+from jax.experimental.pallas import tpu as pltpu
 from jax.sharding import PartitionSpec as P
-
 
 def select_blocks(panel_blocks, panel_slots, row_columns, targets):
     partner = jnp.take(panel_slots, row_columns, axis=0)
@@ -25,7 +28,7 @@
     return lax.all_gather(blocks, "row", axis=0, tiled=True)
 
 
-def per_device(values, columns):
+def per_device_panels(values, columns):
     rows_here, slots_here, block = (values.shape[0], values.shape[1], values.shape[2])
     row_ids = lax.axis_index("row") * rows_here + jnp.arange(rows_here, dtype=jnp.int32)
     on_diagonal = (columns == row_ids[:, None]).astype(jnp.float32)
@@ -49,6 +52,225 @@
     return updated
 
 
+def local_iteration(
+    parts, rows, kept, rows_here, slots_here, left_at, square_at, fourth_at, update_at, origin, *rest
+):
+    blocks, (out, xs, ys, qs, sem) = rest[:-5], rest[-5:]
+    per_piece, size = rows_here * slots_here, xs.shape[1]
+    core = origin[2]
+    copies = []
+    for block, (piece, sibling_part) in zip(blocks, parts):
+        side = 1 - core if sibling_part else core
+        for step in range(block.shape[0] // per_piece):
+            copies.append(
+                pltpu.make_async_copy(
+                    block.at[pl.ds(step * per_piece, per_piece)],
+                    xs.at[pl.ds(((piece + step) * 2 + side) * per_piece, per_piece)],
+                    sem.at[len(copies)],
+                )
+            )
+    for copy in copies:
+        copy.start()
+    received = 10 * 2 * per_piece
+    nothing = jnp.zeros((size, size), jnp.bfloat16)
+    xs[xs.shape[0] - 1] = nothing
+    ys[rows * kept] = nothing
+    qs[rows * slots_here] = nothing
+    row_here, panel = origin[0], origin[1]
+    for copy in copies:
+        copy.wait()
+
+    for number, piece in enumerate((0, 1, 2, 3, 5, 7, 9)):
+        for inside in range(2 * per_piece):
+            xs[received + number * 2 * per_piece + inside] = xs[
+                piece * 2 * per_piece + inside
+            ].T
+
+    def wide(parts):
+        return jnp.concatenate(parts, axis=1)
+
+    def tall(parts):
+        return jnp.concatenate(parts, axis=0)
+
+    def dot(left, right):
+        return jnp.dot(left, right, preferred_element_type=jnp.float32)
+
+    def square(i, carry):
+        left = wide([xs[left_at[i * kept + s]] for s in range(kept)])
+        for first in range(0, kept, slots_here):
+            right = tall(
+                [
+                    wide(
+                        [
+                            xs[square_at[(i * kept + s) * kept + first + t]]
+                            for t in range(slots_here)
+                        ]
+                    )
+                    for s in range(kept)
+                ]
+            )
+            product = dot(left, right).astype(jnp.bfloat16)
+            for t in range(slots_here):
+                ys[i * kept + first + t] = product[:, t * size : (t + 1) * size]
+        return carry
+
+    lax.fori_loop(0, rows, square, 0)
+
+    eye = (
+        lax.broadcasted_iota(jnp.int32, (size, size), 0)
+        == lax.broadcasted_iota(jnp.int32, (size, size), 1)
+    ).astype(jnp.float32)
+
+    def polynomial(i, carry):
+        first = i * kept + panel * slots_here
+        left = wide([ys[i * kept + s] for s in range(kept)])
+        right = tall(
+            [
+                wide(
+                    [ys[fourth_at[(i * kept + s) * slots_here + t]] for t in range(slots_here)]
+                )
+                for s in range(kept)
+            ]
+        )
+        fourth = dot(left, right)
+        for t in range(slots_here):
+            scale = origin[3 + i * slots_here + t].astype(jnp.float32)
+            low = ys[first + t].astype(jnp.float32)
+            value = scale * eye - 10.0 * low + 3.0 * fourth[:, t * size : (t + 1) * size]
+            qs[i * slots_here + t] = value.astype(jnp.bfloat16)
+        return carry
+
+    lax.fori_loop(0, rows, polynomial, 0)
+
+    for a in range(rows_here):
+        i = row_here + a
+        left = wide([xs[left_at[i * kept + s]] for s in range(kept)])
+        right = tall(
+            [
+                wide(
+                    [qs[update_at[(i * kept + s) * slots_here + t]] for t in range(slots_here)]
+                )
+                for s in range(kept)
+            ]
+        )
+        updated = dot(left, right) * 0.125
+        for t in range(slots_here):
+            out[a, t] = updated[:, t * size : (t + 1) * size]
+
+
+NEXT = (0, 2, 3, 1)
+
+
+def around(array, step, bands):
+    return lax.ppermute(array, "row", [(r, (r + 2 * step) % bands) for r in range(bands)])
+
+
+def across(array, flip):
+    return lax.ppermute(array, "col", [(c, c ^ flip) for c in range(4)])
+
+
+def sibling(array, bands):
+    return lax.ppermute(array, "row", [(r, r ^ 1) for r in range(bands)])
+
+
+def all_columns(columns, bands, z, c, core):
+    other = sibling(columns, bands)
+    lower = jnp.where(core == 0, columns, other)
+    upper = jnp.where(core == 0, other, columns)
+    mine = jnp.concatenate([lower, upper], axis=0)
+    line = [mine] + [around(mine, step, bands) for step in range(1, 4)]
+    line = jnp.stack(line)
+    line = line[(z - jnp.arange(4)) % 4]
+    line = line.reshape(4 * mine.shape[0], mine.shape[1])
+    plane = jnp.stack([line] + [across(line, flip) for flip in range(1, 4)])
+    plane = plane[c ^ jnp.arange(4)]
+    return plane.transpose(1, 0, 2).reshape(line.shape[0], -1)
+
+
+def address_tables(pattern, z, c, slots_here, per_chip):
+    rows, kept = pattern.shape
+    ids = jnp.arange(rows, dtype=jnp.int32)
+    match = pattern[:, :, None] == ids[None, None, :]
+    found = jnp.any(match, axis=1)
+    slot = jnp.sum(jnp.where(match, jnp.arange(kept, dtype=jnp.int32)[None, :, None], 0), axis=1)
+    natural = jnp.where(found, ids[:, None] * kept + slot, rows * kept)
+    half = slot % slots_here
+    inside = (ids[:, None] % 4) * slots_here + half
+    inside_t = inside.T
+    h = (ids // 4)[:, None]
+    g = (ids // 4)[None, :]
+    received, mirror = 10 * per_chip, 10 * per_chip + 4 * per_chip
+    own = ((z - h) % 4) * per_chip + inside
+    own_mirror = received + ((z - g) % 4) * per_chip + inside_t
+    flip_g, flip_h = g ^ c, h ^ c
+    diagonal = (4 + (flip_g - 1) * 2) * per_chip + inside
+    turn = jnp.array(NEXT, jnp.int32)
+    pair = (5 + (flip_g - 1) * 2) * per_chip + inside
+    pair_mirror = mirror + (flip_h - 1) * per_chip + inside_t
+    place = jnp.where(turn[flip_g] == (h ^ g), pair, pair_mirror)
+    place = jnp.where(h == g, diagonal, place)
+    place = jnp.where(h == c, own_mirror, place)
+    place = jnp.where(g == c, own, place)
+    place = jnp.where(found, place, mirror + 3 * per_chip)
+    in_panel = lax.dynamic_slice_in_dim(pattern, c * slots_here, slots_here, axis=1)
+    left_at = place[ids[:, None], pattern]
+    square_at = place[pattern[:, :, None], pattern[:, None, :]]
+    fourth_at = natural[pattern[:, :, None], in_panel[:, None, :]]
+    panel_at = jnp.where(found, ids[:, None] * slots_here + half, rows * slots_here)
+    update_at = panel_at[pattern[:, :, None], in_panel[:, None, :]]
+    on_diagonal = jnp.where(in_panel == ids[:, None], 15, 0)
+    return left_at, square_at, fourth_at, update_at, on_diagonal
+
+
+def per_device_whole(values, columns):
+    rows_here, slots_here, size = values.shape[0], values.shape[1], values.shape[2]
+    bands, panels = lax.axis_size("row"), lax.axis_size("col")
+    rows, kept = rows_here * bands, slots_here * panels
+    per_piece = rows_here * slots_here
+    band, c = lax.axis_index("row"), lax.axis_index("col")
+    z, core = band // 2, band % 2
+    mine = values.reshape(per_piece, size, size)
+    line = [mine] + [around(mine, step, bands) for step in range(1, 4)]
+    stacked = jnp.stack(line)
+
+    def pick(h):
+        return lax.dynamic_index_in_dim(stacked, (z - h) % 4, axis=0, keepdims=False)
+
+    plane = []
+    for flip in range(1, 4):
+        payload = jnp.concatenate([pick(c), pick(c ^ NEXT[flip])])
+        plane.append(across(payload, flip))
+    here = line + plane
+    there = [sibling(piece, bands) for piece in here]
+    pattern = all_columns(columns, bands, z, c, core)
+    tables = address_tables(pattern, z, c, slots_here, 2 * per_piece)
+    tables = [table.reshape(-1).astype(jnp.int32) for table in tables]
+    origin = jnp.concatenate([jnp.stack([band * rows_here, c, core]).astype(jnp.int32), tables.pop()])
+    parts = [(piece, part) for part in (False, True) for piece in (0, 1, 2, 3, 4, 6, 8)]
+    count = 17 * 2 * per_piece + 1
+    return pl.pallas_call(
+        functools.partial(local_iteration, parts, rows, kept, rows_here, slots_here),
+        out_shape=jax.ShapeDtypeStruct(values.shape, jnp.float32),
+        in_specs=[pl.BlockSpec(memory_space=pltpu.SMEM)] * 5
+        + [pl.BlockSpec(memory_space=pl.ANY)] * len(parts),
+        out_specs=pl.BlockSpec(memory_space=pltpu.VMEM),
+        scratch_shapes=[
+            pltpu.VMEM((count, size, size), jnp.bfloat16),
+            pltpu.VMEM((rows * kept + 1, size, size), jnp.bfloat16),
+            pltpu.VMEM((rows * slots_here + 1, size, size), jnp.bfloat16),
+            pltpu.SemaphoreType.DMA((20,)),
+        ],
+        compiler_params=pltpu.CompilerParams(vmem_limit_bytes=32 * 1024 * 1024),
+    )(*tables, origin, *here, *there)
+
+
+def per_device(values, columns):
+    bands, panels = lax.axis_size("row"), lax.axis_size("col")
+    if panels == 4 and bands == 8 and values.shape[0] == 2:
+        return per_device_whole(values, columns)
+    return per_device_panels(values, columns)
+
+
 def solution(mesh):
     in_specs = (P("row", "col", None, None), P("row", "col"))
     out_specs = P("row", "col", None, None)

time: 101 us -> 72.6 us (0.72)
  blocking collectives: 40.9 us -> 0 us
  starting transfers between devices: 0.08 us -> 22.2 us
  Pallas kernels: 0 us -> 17 us
  waiting for transfers between devices: 32.9 us -> 16 us
  between operations: 13.2 us -> 0.3 us
  local copies, waits for them, and re-layouts: 12.1 us -> 16.2 us
  matrix products: 1.45 us -> 0 us
    all_gather x4 -> x0, blocking collectives: 40.9 us -> none  [the longest x1 12 us: per_device(): panel_slots = lax.all_gather(columns, 'row', axis=0, tiled=True)]
    all_gather x3 -> x0, waiting for transfers between devices: 32.1 us -> none  [the longest x2 32.1 us: gather_panel(): return lax.all_gather(blocks, 'row', axis=0, tiled=True)]
    ppermute x0 -> x20, starting transfers between devices: none -> 22.2 us  [the longest x6 12.4 us: around(): lax.ppermute(array, 'row', [(r, (r + 2 * step) % bands) for r in range(ba...]
    pallas_call x0 -> x1, Pallas kernels: none -> 17 us  [per_device_whole(): pl.pallas_call(functools.partial(local_iteration, parts, rows, kept, rows...]
    ppermute x0 -> x20, waiting for transfers between devices: none -> 16 us  [the longest x6 7.65 us: around(): lax.ppermute(array, 'row', [(r, (r + 2 * step) % bands) for r in range(ba...]
    gather x8, local copies, waits for them, and re-layouts: 8.65 us -> 14 us  [the longest x1 7.07 us: address_tables(): square_at = place[pattern[:, :, None], pattern[:, None, :]]]
    convert_element_type x2 -> x0, local copies, waits for them, and re-layouts: 1.54 us -> none  [the longest x1 0.77 us: per_device(): square_low = square.astype(jnp.bfloat16)]
    dot_general x3 -> x0, matrix products: 1.45 us -> none  [partial_product(): jnp.einsum('bsxz,bstzy->btxy', row_blocks, picked, preferred_element_type...]
  transfers between devices with their start and end apart: 3 -> 20, of which waited for: 2 -> 9; matrix products, arithmetic and copies ran while one was open for 1% -> 23% of each run, Pallas kernels for 0% -> 0%
where the time goes in v2:
time: 72.6 us; the launch traced here: 72.5 us
  starting transfers between devices  22.2 us (31%)
  Pallas kernels  17 us (23%)
  local copies, waits for them, and re-layouts  16.2 us (22%)
  waiting for transfers between devices  16 us (22%)
  other arithmetic  0.81 us (1%)
    pallas_call x1, Pallas kernels, per_device_whole(): pl.pallas_call(functools.partial(local_iteration, parts, rows, kept, rows...  17 us
    ppermute x6, starting transfers between devices, around(): lax.ppermute(array, 'row', [(r, (r + 2 * step) % bands) for r in range(ba...  12.4 us
    ppermute x6, starting transfers between devices, across(): return lax.ppermute(array, 'col', [(c, c ^ flip) for c in range(4)])  8 us
    ppermute x6, waiting for transfers between devices, around(): lax.ppermute(array, 'row', [(r, (r + 2 * step) % bands) for r in range(ba...  7.65 us
    ppermute x6, waiting for transfers between devices, across(): return lax.ppermute(array, 'col', [(c, c ^ flip) for c in range(4)])  7.62 us
    gather x1, local copies, waits for them, and re-layouts, address_tables(): square_at = place[pattern[:, :, None], pattern[:, None, :]]  7.07 us
    gather x1, local copies, waits for them, and re-layouts, address_tables(): update_at = panel_at[pattern[:, :, None], in_panel[:, None, :]]  1.95 us
    gather x1, local copies, waits for them, and re-layouts, address_tables(): fourth_at = natural[pattern[:, :, None], in_panel[:, None, :]]  1.95 us
  transfers between devices with their start and end apart: 20, of which 9 were waited for; matrix products, arithmetic and copies ran while one was open for 23% of the time, Pallas kernels for 0%

profile of v2, /device:TPU:0, one launch (start us, length us, event | category | flops | bytes accessed | tf_op | source)
XLA Modules:
  0.0 72.5 jit_solution(6373182263324485306)
XLA Ops:
  0.0 0.5 collective-permute-start.13
  0.5 4.6 %collective-permute-start.9 = (bf16[4,128,128]{2,1,0:T(8,128)(2,1)}, bf16[4,128,128]{2,1,0:T(8,128)(2,1)S(1)}, u32[]{:S(2)}, u32[]{:S(2)}) collective-permute-start(bf16[4,128,128]{2,1,0:T(8,128)(2,1)} %bitcast.53), channel_id=1, source_target_pairs={{0,24},{4,28},{8,0},{12,4},{16,8},{20,12},{24,16},{28,20},{1,25},{... | collective-permute-start | bytes 393224 | tf_op jit(solution)/shard_map/ppermute | solution.py:165
  5.1 0.2 collective-permute-start
  5.5 0.6 copy-done.1
  6.1 0.7 gather_fusion.2
  6.9 0.4 collective-permute-start.3
  7.4 2.3 %collective-permute-start.2 = (s32[4,2]{1,0:T(4,128)S(1)}, s32[4,2]{1,0:T(4,128)S(1)}, u32[]{:S(2)}, u32[]{:S(2)}) collective-permute-start(s32[4,2]{1,0:T(4,128)S(1)} %pad_add_fusion.2), channel_id=1, source_target_pairs={{0,16},{4,20},{8,24},{12,28},{16,0},{20,4},{24,8},{28,12},{1,17},{... | collective-permute-start | bytes 104 | tf_op jit(solution)/shard_map/ppermute | solution.py:165
  9.7 2.0 %collective-permute-done.3 = s32[4,2]{1,0:T(4,128)S(1)} collective-permute-done((s32[4,2]{1,0:T(4,128)S(1)}, s32[4,2]{1,0:T(4,128)S(1)}, u32[]{:S(2)}, u32[]{:S(2)}) %collective-permute-start.3) | collective-permute-done | bytes 64 | tf_op jit(solution)/shard_map/ppermute | solution.py:165
  11.7 3.6 %collective-permute-start.1 = (s32[4,2]{1,0:T(4,128)S(1)}, s32[4,2]{1,0:T(4,128)S(1)}, u32[]{:S(2)}, u32[]{:S(2)}) collective-permute-start(s32[4,2]{1,0:T(4,128)S(1)} %pad_add_fusion.2), channel_id=1, source_target_pairs={{0,8},{4,12},{8,16},{12,20},{16,24},{20,28},{24,0},{28,4},{1,9},{5... | collective-permute-start | bytes 104 | tf_op jit(solution)/shard_map/ppermute | solution.py:165
  15.5 2.0 %collective-permute-done.1 = s32[4,2]{1,0:T(4,128)S(1)} collective-permute-done((s32[4,2]{1,0:T(4,128)S(1)}, s32[4,2]{1,0:T(4,128)S(1)}, u32[]{:S(2)}, u32[]{:S(2)}) %collective-permute-start.1) | collective-permute-done | bytes 64 | tf_op jit(solution)/shard_map/ppermute | solution.py:165
  17.6 0.6 gather_fusion
  18.3 2.4 %collective-permute-start.6 = (s32[16,2]{0,1:T(2,128)S(1)}, s32[16,2]{0,1:T(2,128)S(1)}, u32[]{:S(2)}, u32[]{:S(2)}) collective-permute-start(s32[16,2]{0,1:T(2,128)S(1)} %reshape.352), channel_id=1, source_target_pairs={{0,3},{1,2},{2,1},{3,0},{4,7},{5,6},{6,5},{7,4},{8,11},{9,10},{10,... | collective-permute-start | bytes 392 | tf_op jit(solution)/shard_map/ppermute | solution.py:169
  20.8 0.5 collective-permute-start.5
  21.3 1.4 %collective-permute-done.6 = s32[16,2]{0,1:T(2,128)S(1)} collective-permute-done((s32[16,2]{0,1:T(2,128)S(1)}, s32[16,2]{0,1:T(2,128)S(1)}, u32[]{:S(2)}, u32[]{:S(2)}) %collective-permute-start.6) | collective-permute-done | bytes 160 | tf_op jit(solution)/shard_map/ppermute | solution.py:169
  22.7 1.5 %collective-permute-start.4 = (s32[16,2]{0,1:T(2,128)S(1)}, s32[16,2]{0,1:T(2,128)S(1)}, u32[]{:S(2)}, u32[]{:S(2)}) collective-permute-start(s32[16,2]{0,1:T(2,128)S(1)} %reshape.352), channel_id=1, source_target_pairs={{0,1},{1,0},{2,3},{3,2},{4,5},{5,4},{6,7},{7,6},{8,9},{9,8},{10,11... | collective-permute-start | bytes 392 | tf_op jit(solution)/shard_map/ppermute | solution.py:169
  24.4 1.4 %collective-permute-start.7 = (bf16[4,128,128]{2,1,0:T(8,128)(2,1)S(1)}, bf16[4,128,128]{2,1,0:T(8,128)(2,1)S(1)}, u32[]{:S(2)}, u32[]{:S(2)}) collective-permute-start(bf16[4,128,128]{2,1,0:T(8,128)(2,1)S(1)} %bitcast.55), channel_id=1, source_target_pairs={{0,8},{4,12},{8,16},{12,20},{16,24},{20,28},{24,0},{28,4},{1,9},{5... | collective-permute-start | bytes 393224 | tf_op jit(solution)/shard_map/ppermute | solution.py:165
  25.7 0.6 collective-permute-done.4
  26.3 0.6 gather_fusion.1
  27.5 3.6 %collective-permute-done.7.rest_1_ = bf16[4,128,128]{2,1,0:T(8,128)(2,1)S(1)} collective-permute-done((bf16[4,128,128]{2,1,0:T(8,128)(2,1)S(1)}, bf16[4,128,128]{2,1,0:T(8,128)(2,1)S(1)}, u32[]{:S(2)}, u32[]{:S(2)}) %collective-permute-start.7) | collective-permute-done | bytes 131104 | tf_op jit(solution)/shard_map/ppermute | solution.py:165
  31.3 1.4 %collective-permute-start.12 = (bf16[8,128,128]{2,1,0:T(8,128)(2,1)S(1)}, bf16[8,128,128]{2,1,0:T(8,128)(2,1)S(1)}, u32[]{:S(2)}, u32[]{:S(2)}) collective-permute-start(bf16[8,128,128]{2,1,0:T(8,128)(2,1)S(1)} %get-tuple-element.9), channel_id=1, source_target_pairs={{0,3},{1,2},{2,1},{3,0},{4,7},{5,6},{6,5},{7,4},{8,11},{9,10},{10,... | collective-permute-start | bytes 786440 | tf_op jit(solution)/shard_map/ppermute | solution.py:169
  32.8 0.6 collective-permute-start.11
  33.4 1.5 %collective-permute-start.10 = (bf16[8,128,128]{2,1,0:T(8,128)(2,1)S(1)}, bf16[8,128,128]{2,1,0:T(8,128)(2,1)S(1)}, u32[]{:S(2)}, u32[]{:S(2)}) collective-permute-start(bf16[8,128,128]{2,1,0:T(8,128)(2,1)S(1)} %get-tuple-element.11), channel_id=1, source_target_pairs={{0,1},{1,0},{2,3},{3,2},{4,5},{5,4},{6,7},{7,6},{8,9},{9,8},{10,11... | collective-permute-start | bytes 786440 | tf_op jit(solution)/shard_map/ppermute | solution.py:169
  35.2 0.6 collective-permute-start.15
  35.8 0.7 collective-permute-done.16.rest_10_
  36.6 2.8 %collective-permute-done.12.rest_6_ = bf16[8,128,128]{2,1,0:T(8,128)(2,1)S(1)} collective-permute-done((bf16[8,128,128]{2,1,0:T(8,128)(2,1)S(1)}, bf16[8,128,128]{2,1,0:T(8,128)(2,1)S(1)}, u32[]{:S(2)}, u32[]{:S(2)}) %collective-permute-start.12) | collective-permute-done | bytes 262176 | tf_op jit(solution)/shard_map/ppermute | solution.py:169
  39.4 2.7 %collective-permute-done.11.rest_5_ = bf16[8,128,128]{2,1,0:T(8,128)(2,1)S(1)} collective-permute-done((bf16[8,128,128]{2,1,0:T(8,128)(2,1)S(1)}, bf16[8,128,128]{2,1,0:T(8,128)(2,1)S(1)}, u32[]{:S(2)}, u32[]{:S(2)}) %collective-permute-start.11) | collective-permute-done | bytes 262176 | tf_op jit(solution)/shard_map/ppermute | solution.py:169
  42.1 0.5 collective-permute-start.17
  43.0 1.9 %gather_fusion.6 = s32[256]{0:T(256)S(1)} fusion(s32[16,16]{1,0:T(8,128)S(1)} %get-tuple-element.12, s32[256]{0:T(256)S(1)} %reshape.396), kind=kCustom, calls=%fused_computation.6 | custom fusion | bytes 4096 | tf_op jit(solution)/shard_map/gather | solution.py:220
  45.0 1.9 %gather_fusion.5 = s32[256]{0:T(256)S(1)} fusion(s32[16,16]{1,0:T(8,128)S(1)} %get-tuple-element.13, s32[256]{0:T(256)S(1)} %reshape.396), kind=kCustom, calls=%fused_computation.5 | custom fusion | bytes 4096 | tf_op jit(solution)/shard_map/gather | solution.py:218
  47.1 1.3 %gather_fusion.3 = s32[128]{0:T(128)S(1)} fusion(s32[16,16]{1,0:T(8,128)S(1)} %get-tuple-element.14, s32[128]{0:T(128)S(1)} %reshape.384), kind=kCustom, calls=%fused_computation.3 | custom fusion | bytes 2048 | tf_op jit(solution)/shard_map/gather | solution.py:216
  48.3 7.1 %gather_fusion.4 = s32[1024]{0:T(1024)S(1)} fusion(s32[16,16]{1,0:T(8,128)S(1)} %get-tuple-element.14, s32[1024]{0:T(1024)S(1)} %reshape.390), kind=kCustom, calls=%fused_computation.4 | custom fusion | bytes 16384 | tf_op jit(solution)/shard_map/gather | solution.py:217
  55.5 17.0 %shard_map.37 = f32[2,2,128,128]{3,2,1,0:T(8,128)} custom-call(s32[128]{0:T(128)S(1)} %gather_fusion.3, s32[1024]{0:T(1024)S(1)} %gather_fusion.4, s32[256]{0:T(256)S(1)} %gather_fusion.5, s32[256]{0:T(256)S(1)} %gather_fusion.6, s32[35]{0:T(128)S(1)} %pad_add_fusion.3.origin, bf16[4,128,128]{2,1,0:T(8,128)(2,1)S(1)} %bitcast.57, ...), custom_call_target="tpu_custom_call" | custom-call | tf_op jit(solution)/shard_map/pallas_call | solution.py:251
  (68 shorter events, 2.7 us)
Async XLA Ops:
  0.0 5.1 %copy-start.2 = (s32[2,2]{1,0:T(2,128)S(1)}, s32[2,2]{1,0:T(2,128)}, u32[]{:S(2)}) copy-start(s32[2,2]{1,0:T(2,128)} %param.4) | copy-start | bytes 52
  0.0 35.2 %collective-permute-start.13 = (bf16[4,128,128]{2,1,0:T(8,128)(2,1)}, bf16[4,128,128]{2,1,0:T(8,128)(2,1)S(1)}, u32[]{:S(2)}, u32[]{:S(2)}) collective-permute-start(bf16[4,128,128]{2,1,0:T(8,128)(2,1)} %bitcast.52), channel_id=1, source_target_pairs={{0,4},{4,0},{8,12},{12,8},{16,20},{20,16},{24,28},{28,24},{1,5},{5... | collective-permute-start | bytes 393224 | tf_op jit(solution)/shard_map/ppermute | solution.py:173
  0.5 27.0 %collective-permute-start.9 = (bf16[4,128,128]{2,1,0:T(8,128)(2,1)}, bf16[4,128,128]{2,1,0:T(8,128)(2,1)S(1)}, u32[]{:S(2)}, u32[]{:S(2)}) collective-permute-start(bf16[4,128,128]{2,1,0:T(8,128)(2,1)} %bitcast.53), channel_id=1, source_target_pairs={{0,24},{4,28},{8,0},{12,4},{16,8},{20,12},{24,16},{28,20},{1,25},{... | collective-permute-start | bytes 393224 | tf_op jit(solution)/shard_map/ppermute | solution.py:165
  5.1 22.4 %collective-permute-start.8 = (bf16[4,128,128]{2,1,0:T(8,128)(2,1)}, bf16[4,128,128]{2,1,0:T(8,128)(2,1)S(1)}, u32[]{:S(2)}, u32[]{:S(2)}) collective-permute-start(bf16[4,128,128]{2,1,0:T(8,128)(2,1)} %bitcast.54), channel_id=1, source_target_pairs={{0,16},{4,20},{8,24},{12,28},{16,0},{20,4},{24,8},{28,12},{1,17},{... | collective-permute-start | bytes 393224 | tf_op jit(solution)/shard_map/ppermute | solution.py:165
  5.1 1.7 %collective-permute-start = (s32[2,2]{1,0:T(2,128)S(1)}, s32[2,2]{1,0:T(2,128)S(1)}, u32[]{:S(2)}, u32[]{:S(2)}) collective-permute-start(s32[2,2]{1,0:T(2,128)S(1)} %copy-done.2), channel_id=1, source_target_pairs={{0,4},{4,0},{8,12},{12,8},{16,20},{20,16},{24,28},{28,24},{1,5},{5... | collective-permute-start | bytes 56 | tf_op jit(solution)/shard_map/ppermute | solution.py:173
  5.5 0.7 copy-start.1
  6.1 18.2 %copy-start = (bf16[2,2,128,128]{3,2,1,0:T(8,128)(2,1)S(1)}, bf16[2,2,128,128]{3,2,1,0:T(8,128)(2,1)}, u32[]{:S(2)}) copy-start(bf16[2,2,128,128]{3,2,1,0:T(8,128)(2,1)} %param.3) | copy-start | bytes 393220
  6.9 4.8 %collective-permute-start.3 = (s32[4,2]{1,0:T(4,128)S(1)}, s32[4,2]{1,0:T(4,128)S(1)}, u32[]{:S(2)}, u32[]{:S(2)}) collective-permute-start(s32[4,2]{1,0:T(4,128)S(1)} %pad_add_fusion.2), channel_id=1, source_target_pairs={{0,24},{4,28},{8,0},{12,4},{16,8},{20,12},{24,16},{28,20},{1,25},{... | collective-permute-start | bytes 104 | tf_op jit(solution)/shard_map/ppermute | solution.py:165
  7.4 8.0 %collective-permute-start.2 = (s32[4,2]{1,0:T(4,128)S(1)}, s32[4,2]{1,0:T(4,128)S(1)}, u32[]{:S(2)}, u32[]{:S(2)}) collective-permute-start(s32[4,2]{1,0:T(4,128)S(1)} %pad_add_fusion.2), channel_id=1, source_target_pairs={{0,16},{4,20},{8,24},{12,28},{16,0},{20,4},{24,8},{28,12},{1,17},{... | collective-permute-start | bytes 104 | tf_op jit(solution)/shard_map/ppermute | solution.py:165
  11.7 5.8 %collective-permute-start.1 = (s32[4,2]{1,0:T(4,128)S(1)}, s32[4,2]{1,0:T(4,128)S(1)}, u32[]{:S(2)}, u32[]{:S(2)}) collective-permute-start(s32[4,2]{1,0:T(4,128)S(1)} %pad_add_fusion.2), channel_id=1, source_target_pairs={{0,8},{4,12},{8,16},{12,20},{16,24},{20,28},{24,0},{28,4},{1,9},{5... | collective-permute-start | bytes 104 | tf_op jit(solution)/shard_map/ppermute | solution.py:165
  18.3 4.5 %collective-permute-start.6 = (s32[16,2]{0,1:T(2,128)S(1)}, s32[16,2]{0,1:T(2,128)S(1)}, u32[]{:S(2)}, u32[]{:S(2)}) collective-permute-start(s32[16,2]{0,1:T(2,128)S(1)} %reshape.352), channel_id=1, source_target_pairs={{0,3},{1,2},{2,1},{3,0},{4,7},{5,6},{6,5},{7,4},{8,11},{9,10},{10,... | collective-permute-start | bytes 392 | tf_op jit(solution)/shard_map/ppermute | solution.py:169
  20.8 3.6 %collective-permute-start.5 = (s32[16,2]{0,1:T(2,128)S(1)}, s32[16,2]{0,1:T(2,128)S(1)}, u32[]{:S(2)}, u32[]{:S(2)}) collective-permute-start(s32[16,2]{0,1:T(2,128)S(1)} %reshape.352), channel_id=1, source_target_pairs={{0,2},{1,3},{2,0},{3,1},{4,6},{5,7},{6,4},{7,5},{8,10},{9,11},{10,... | collective-permute-start | bytes 392 | tf_op jit(solution)/shard_map/ppermute | solution.py:169
  22.7 3.6 %collective-permute-start.4 = (s32[16,2]{0,1:T(2,128)S(1)}, s32[16,2]{0,1:T(2,128)S(1)}, u32[]{:S(2)}, u32[]{:S(2)}) collective-permute-start(s32[16,2]{0,1:T(2,128)S(1)} %reshape.352), channel_id=1, source_target_pairs={{0,1},{1,0},{2,3},{3,2},{4,5},{5,4},{6,7},{7,6},{8,9},{9,8},{10,11... | collective-permute-start | bytes 392 | tf_op jit(solution)/shard_map/ppermute | solution.py:169
  24.4 6.8 %collective-permute-start.7 = (bf16[4,128,128]{2,1,0:T(8,128)(2,1)S(1)}, bf16[4,128,128]{2,1,0:T(8,128)(2,1)S(1)}, u32[]{:S(2)}, u32[]{:S(2)}) collective-permute-start(bf16[4,128,128]{2,1,0:T(8,128)(2,1)S(1)} %bitcast.55), channel_id=1, source_target_pairs={{0,8},{4,12},{8,16},{12,20},{16,24},{20,28},{24,0},{28,4},{1,9},{5... | collective-permute-start | bytes 393224 | tf_op jit(solution)/shard_map/ppermute | solution.py:165
  31.3 8.0 %collective-permute-start.12 = (bf16[8,128,128]{2,1,0:T(8,128)(2,1)S(1)}, bf16[8,128,128]{2,1,0:T(8,128)(2,1)S(1)}, u32[]{:S(2)}, u32[]{:S(2)}) collective-permute-start(bf16[8,128,128]{2,1,0:T(8,128)(2,1)S(1)} %get-tuple-element.9), channel_id=1, source_target_pairs={{0,3},{1,2},{2,1},{3,0},{4,7},{5,6},{6,5},{7,4},{8,11},{9,10},{10,... | collective-permute-start | bytes 786440 | tf_op jit(solution)/shard_map/ppermute | solution.py:169
  32.8 9.3 %collective-permute-start.11 = (bf16[8,128,128]{2,1,0:T(8,128)(2,1)S(1)}, bf16[8,128,128]{2,1,0:T(8,128)(2,1)S(1)}, u32[]{:S(2)}, u32[]{:S(2)}) collective-permute-start(bf16[8,128,128]{2,1,0:T(8,128)(2,1)S(1)} %get-tuple-element.10), channel_id=1, source_target_pairs={{0,2},{1,3},{2,0},{3,1},{4,6},{5,7},{6,4},{7,5},{8,10},{9,11},{10,... | collective-permute-start | bytes 786440 | tf_op jit(solution)/shard_map/ppermute | solution.py:169
  33.4 8.6 %collective-permute-start.10 = (bf16[8,128,128]{2,1,0:T(8,128)(2,1)S(1)}, bf16[8,128,128]{2,1,0:T(8,128)(2,1)S(1)}, u32[]{:S(2)}, u32[]{:S(2)}) collective-permute-start(bf16[8,128,128]{2,1,0:T(8,128)(2,1)S(1)} %get-tuple-element.11), channel_id=1, source_target_pairs={{0,1},{1,0},{2,3},{3,2},{4,5},{5,4},{6,7},{7,6},{8,9},{9,8},{10,11... | collective-permute-start | bytes 786440 | tf_op jit(solution)/shard_map/ppermute | solution.py:169
  35.1 1.4 %collective-permute-start.16 = (bf16[4,128,128]{2,1,0:T(8,128)(2,1)S(1)}, bf16[4,128,128]{2,1,0:T(8,128)(2,1)S(1)}, u32[]{:S(2)}, u32[]{:S(2)}) collective-permute-start(bf16[4,128,128]{2,1,0:T(8,128)(2,1)S(1)} %collective-permute-done.9.rest_3_), channel_id=1, source_target_pairs={{0,4},{4,0},{8,12},{12,8},{16,20},{20,16},{24,28},{28,24},{1,5},{5... | collective-permute-start | bytes 393224 | tf_op jit(solution)/shard_map/ppermute | solution.py:173
  35.2 20.3 %collective-permute-start.15 = (bf16[4,128,128]{2,1,0:T(8,128)(2,1)S(1)}, bf16[4,128,128]{2,1,0:T(8,128)(2,1)S(1)}, u32[]{:S(2)}, u32[]{:S(2)}) collective-permute-start(bf16[4,128,128]{2,1,0:T(8,128)(2,1)S(1)} %collective-permute-done.8.rest_2_), channel_id=1, source_target_pairs={{0,4},{4,0},{8,12},{12,8},{16,20},{20,16},{24,28},{28,24},{1,5},{5... | collective-permute-start | bytes 393224 | tf_op jit(solution)/shard_map/ppermute | solution.py:173
  36.4 19.1 %collective-permute-start.14 = (bf16[4,128,128]{2,1,0:T(8,128)(2,1)S(1)}, bf16[4,128,128]{2,1,0:T(8,128)(2,1)S(1)}, u32[]{:S(2)}, u32[]{:S(2)}) collective-permute-start(bf16[4,128,128]{2,1,0:T(8,128)(2,1)S(1)} %collective-permute-done.7.rest_1_), channel_id=1, source_target_pairs={{0,4},{4,0},{8,12},{12,8},{16,20},{20,16},{24,28},{28,24},{1,5},{5... | collective-permute-start | bytes 393224 | tf_op jit(solution)/shard_map/ppermute | solution.py:173
  39.4 16.1 %collective-permute-start.19 = (bf16[8,128,128]{2,1,0:T(8,128)(2,1)S(1)}, bf16[8,128,128]{2,1,0:T(8,128)(2,1)S(1)}, u32[]{:S(2)}, u32[]{:S(2)}) collective-permute-start(bf16[8,128,128]{2,1,0:T(8,128)(2,1)S(1)} %collective-permute-done.12.rest_6_), channel_id=1, source_target_pairs={{0,4},{4,0},{8,12},{12,8},{16,20},{20,16},{24,28},{28,24},{1,5},{5... | collective-permute-start | bytes 786440 | tf_op jit(solution)/shard_map/ppermute | solution.py:173
  42.0 13.5 %collective-permute-start.18 = (bf16[8,128,128]{2,1,0:T(8,128)(2,1)S(1)}, bf16[8,128,128]{2,1,0:T(8,128)(2,1)S(1)}, u32[]{:S(2)}, u32[]{:S(2)}) collective-permute-start(bf16[8,128,128]{2,1,0:T(8,128)(2,1)S(1)} %collective-permute-done.11.rest_5_), channel_id=1, source_target_pairs={{0,4},{4,0},{8,12},{12,8},{16,20},{20,16},{24,28},{28,24},{1,5},{5... | collective-permute-start | bytes 786440 | tf_op jit(solution)/shard_map/ppermute | solution.py:173
  42.1 13.5 %collective-permute-start.17 = (bf16[8,128,128]{2,1,0:T(8,128)(2,1)S(1)}, bf16[8,128,128]{2,1,0:T(8,128)(2,1)S(1)}, u32[]{:S(2)}, u32[]{:S(2)}) collective-permute-start(bf16[8,128,128]{2,1,0:T(8,128)(2,1)S(1)} %collective-permute-done.10.rest_4_), channel_id=1, source_target_pairs={{0,4},{4,0},{8,12},{12,8},{16,20},{20,16},{24,28},{28,24},{1,5},{5... | collective-permute-start | bytes 786440 | tf_op jit(solution)/shard_map/ppermute | solution.py:173

commit v3 on v0

--- a/solution.py
+++ b/solution.py
@@ -1,8 +1,9 @@
 import jax
 import jax.numpy as jnp
 from jax import lax
+from jax.experimental import pallas as pl
+from jax.experimental.pallas import tpu as pltpu
 from jax.sharding import PartitionSpec as P
-
 
 def select_blocks(panel_blocks, panel_slots, row_columns, targets):
     partner = jnp.take(panel_slots, row_columns, axis=0)
@@ -25,7 +26,7 @@
     return lax.all_gather(blocks, "row", axis=0, tiled=True)
 
 
-def per_device(values, columns):
+def per_device_panels(values, columns):
     rows_here, slots_here, block = (values.shape[0], values.shape[1], values.shape[2])
     row_ids = lax.axis_index("row") * rows_here + jnp.arange(rows_here, dtype=jnp.int32)
     on_diagonal = (columns == row_ids[:, None]).astype(jnp.float32)
@@ -49,6 +50,236 @@
     return updated
 
 
+NEXT = (0, 2, 3, 1)
+TILE = 16
+
+
+def around(array, step, bands):
+    return lax.ppermute(array, "row", [(r, (r + 2 * step) % bands) for r in range(bands)])
+
+
+def across(array, flip):
+    return lax.ppermute(array, "col", [(c, c ^ flip) for c in range(4)])
+
+
+def sibling(array, bands):
+    return lax.ppermute(array, "row", [(r, r ^ 1) for r in range(bands)])
+
+
+def next_flip(flip):
+    return jnp.where(flip == 3, 1, flip + 1)
+
+
+def local_iteration(
+    origin, line, line_there, *rest
+):
+    here, there = rest[:3], rest[3:6]
+    out, xs, ys, qs, numbers, pattern, table, near, used, sem = rest[6:]
+    rows, kept, slots, size = 16, 8, 2, 128
+    band, c = origin[0], origin[1]
+    z, core = lax.div(band, 2), lax.rem(band, 2)
+    chunk = 4 * size + TILE
+
+    pieces = []
+    for source, side in ((line, core), (line_there, 1 - core)):
+        for step in range(4):
+            pieces.append((source, step * chunk, step * 8 + side * 4))
+    for group, side in ((here, core), (there, 1 - core)):
+        for flip in range(3):
+            for part in range(2):
+                pieces.append(
+                    (group[flip], part * chunk, (4 + flip * 2 + part) * 8 + side * 4)
+                )
+
+    total = jnp.zeros((TILE, size), jnp.float32)
+    for source, first, _ in pieces:
+        total += source[first + 4 * size : first + chunk, :].astype(jnp.float32)
+    numbers[...] = total[0:8].astype(jnp.int32)
+    copy = pltpu.make_async_copy(numbers, pattern, sem)
+    copy.start()
+
+    nothing = jnp.zeros((size, size), jnp.bfloat16)
+    empty = 17 * 8
+    xs[empty] = nothing
+    ys[rows * kept] = nothing
+    qs[rows * slots] = nothing
+    blank = empty + rows * kept * 256
+
+    def clear(at, carry):
+        table[at] = blank
+        return carry
+
+    lax.fori_loop(0, rows * rows, clear, 0, unroll=16)
+
+    for source, first, place in pieces:
+        for b in range(4):
+            xs[place + b] = source[first + b * size : first + (b + 1) * size, :]
+    for number, piece in enumerate((0, 1, 2, 3, 5, 7, 9)):
+        for b in range(8):
+            xs[80 + number * 8 + b] = xs[piece * 8 + b].T
+    copy.wait()
+
+    def enter(i, j, place, slot):
+        table[i * rows + j] = place + (i * kept + slot) * 256
+        near[i * kept + slot] = j
+
+    def known(h, g, base, mirror):
+        if mirror is not None:
+            for local in range(4):
+                used[local] = 0
+        for il in range(4):
+            for t in range(slots):
+                i = 4 * h + il
+                j = pattern[0, ((h * 2 + il // 2) * 4 + g) * 4 + (il % 2) * slots + t]
+                enter(i, j, base + il * slots + t, g * slots + t)
+                if mirror is not None:
+                    local = j - 4 * g
+                    taken = used[local]
+                    used[local] = taken + 1
+                    enter(j, i, mirror + il * slots + t, h * slots + taken)
+
+    for h in range(4):
+        flip = h ^ c
+        own = lax.rem(z - h + 4, 4) * 8
+        base = jnp.where(flip == 0, own, (4 + (flip - 1) * 2) * 8)
+        known(h, h, base, None)
+    for first in range(4):
+        for second in range(first + 1, 4):
+            flip_first, flip_second = first ^ c, second ^ c
+            straight = (flip_second == 0) | (
+                (flip_first != 0) & (next_flip(flip_second) == (first ^ second))
+            )
+            h = jnp.where(straight, first, second)
+            g = first + second - h
+            flip = g ^ c
+            own = lax.rem(z - h + 4, 4) * 8
+            base = jnp.where(flip == 0, own, (5 + (flip - 1) * 2) * 8)
+            mirror = 80 + jnp.where(flip == 0, own, (4 + flip - 1) * 8)
+            known(h, g, base, mirror)
+
+    def wide(parts):
+        return jnp.concatenate(parts, axis=1)
+
+    def tall(parts):
+        return jnp.concatenate(parts, axis=0)
+
+    def dot(left, right):
+        return jnp.dot(left, right, preferred_element_type=jnp.float32)
+
+    def x_at(k, j):
+        return table[k * rows + j] & 255
+
+    def y_at(k, j):
+        return lax.shift_right_logical(table[k * rows + j], 8)
+
+    for home in range(4):
+
+        def square(i, carry):
+            ks = [near[i * kept + s] for s in range(kept)]
+            left = wide([xs[x_at(i, k)] for k in ks])
+            for p in range(home, 4):
+                js = ks[p * slots : (p + 1) * slots]
+                right = tall([wide([xs[x_at(k, j)] for j in js]) for k in ks])
+                product = dot(left, right).astype(jnp.bfloat16)
+                for t in range(slots):
+                    block = product[:, t * size : (t + 1) * size]
+                    ys[i * kept + p * slots + t] = block
+                    if p > home:
+                        ys[y_at(js[t], i)] = block.T
+            return carry
+
+        lax.fori_loop(home * 4, home * 4 + 4, square, 0)
+
+    eye = (
+        lax.broadcasted_iota(jnp.int32, (size, size), 0)
+        == lax.broadcasted_iota(jnp.int32, (size, size), 1)
+    ).astype(jnp.float32)
+
+    def polynomial(i, carry):
+        ks = [near[i * kept + s] for s in range(kept)]
+        js = [near[i * kept + c * slots + t] for t in range(slots)]
+        left = wide([ys[i * kept + s] for s in range(kept)])
+        right = tall([wide([ys[y_at(k, j)] for j in js]) for k in ks])
+        fourth = dot(left, right)
+        for t in range(slots):
+            scale = jnp.where(js[t] == i, 15.0, 0.0)
+            low = ys[i * kept + c * slots + t].astype(jnp.float32)
+            value = scale * eye - 10.0 * low + 3.0 * fourth[:, t * size : (t + 1) * size]
+            qs[i * slots + t] = value.astype(jnp.bfloat16)
+        return carry
+
+    lax.fori_loop(0, rows, polynomial, 0)
+
+    for a in range(2):
+        i = band * 2 + a
+        ks = [near[i * kept + s] for s in range(kept)]
+        js = [near[i * kept + c * slots + t] for t in range(slots)]
+
+        def q_at(k, j):
+            at = y_at(k, j)
+            return lax.shift_right_logical(at, 3) * slots + (at & 1)
+
+        left = wide([xs[x_at(i, k)] for k in ks])
+        right = tall([wide([qs[q_at(k, j)] for j in js]) for k in ks])
+        updated = dot(left, right) * 0.125
+        for t in range(slots):
+            out[a, t] = updated[:, t * size : (t + 1) * size]
+
+
+def per_device_whole(values, columns):
+    bands = lax.axis_size("row")
+    size = values.shape[2]
+    band, c = lax.axis_index("row"), lax.axis_index("col")
+    z = band // 2
+    lane = lax.broadcasted_iota(jnp.int32, (TILE, size), 1)
+    line_number = lax.broadcasted_iota(jnp.int32, (TILE, size), 0)
+    first = (band * 4 + c) * 4
+    tile = jnp.zeros((TILE, size), jnp.int32)
+    for m in range(4):
+        here = (lane == first + m) & (line_number == 0)
+        tile = jnp.where(here, columns[m // 2, m % 2], tile)
+    mine = jnp.concatenate([values.reshape(4 * size, size), tile.astype(jnp.bfloat16)])
+    line = jnp.concatenate([mine] + [around(mine, step, bands) for step in range(1, 4)])
+    stacked = line.reshape(4, *mine.shape)
+
+    def pick(h):
+        return lax.dynamic_index_in_dim(stacked, (z - h) % 4, axis=0, keepdims=False)
+
+    here = []
+    for flip in range(1, 4):
+        payload = jnp.concatenate([pick(c), pick(c ^ NEXT[flip])])
+        here.append(across(payload, flip))
+    line_there = sibling(line, bands)
+    there = [sibling(piece, bands) for piece in here]
+    origin = jnp.stack([band, c]).astype(jnp.int32)
+    return pl.pallas_call(
+        local_iteration,
+        out_shape=jax.ShapeDtypeStruct(values.shape, jnp.float32),
+        in_specs=[pl.BlockSpec(memory_space=pltpu.SMEM)]
+        + [pl.BlockSpec(memory_space=pltpu.VMEM)] * 8,
+        out_specs=pl.BlockSpec(memory_space=pltpu.VMEM),
+        scratch_shapes=[
+            pltpu.VMEM((17 * 8 + 1, size, size), jnp.bfloat16),
+            pltpu.VMEM((129, size, size), jnp.bfloat16),
+            pltpu.VMEM((33, size, size), jnp.bfloat16),
+            pltpu.VMEM((8, size), jnp.int32),
+            pltpu.SMEM((8, size), jnp.int32),
+            pltpu.SMEM((256,), jnp.int32),
+            pltpu.SMEM((128,), jnp.int32),
+            pltpu.SMEM((4,), jnp.int32),
+            pltpu.SemaphoreType.DMA,
+        ],
+        compiler_params=pltpu.CompilerParams(vmem_limit_bytes=32 * 1024 * 1024),
+    )(origin, line, line_there, *here, *there)
+
+
+def per_device(values, columns):
+    sizes = (lax.axis_size("row"), lax.axis_size("col"), *values.shape)
+    if sizes == (8, 4, 2, 2, 128, 128):
+        return per_device_whole(values, columns)
+    return per_device_panels(values, columns)
+
+
 def solution(mesh):
     in_specs = (P("row", "col", None, None), P("row", "col"))
     out_specs = P("row", "col", None, None)

time: 101 us -> 51.5 us (0.51)
  blocking collectives: 40.9 us -> 0 us
  Pallas kernels: 0 us -> 13.8 us
  between operations: 13.2 us -> 0.07 us
  waiting for transfers between devices: 32.9 us -> 20.5 us
  starting transfers between devices: 0.08 us -> 11 us
  local copies, waits for them, and re-layouts: 12.1 us -> 2.43 us
  other arithmetic: 0.29 us -> 2.82 us
  matrix products: 1.45 us -> 0 us
    all_gather x4 -> x0, blocking collectives: 40.9 us -> none  [the longest x1 12 us: per_device(): panel_slots = lax.all_gather(columns, 'row', axis=0, tiled=True)]
    all_gather x3 -> x0, waiting for transfers between devices: 32.1 us -> none  [the longest x2 32.1 us: gather_panel(): return lax.all_gather(blocks, 'row', axis=0, tiled=True)]
    ppermute x0 -> x10, waiting for transfers between devices: none -> 20.5 us  [the longest x3 11.6 us: across(): return lax.ppermute(array, 'col', [(c, c ^ flip) for c in range(4)])]
    pallas_call x0 -> x1, Pallas kernels: none -> 13.8 us  [per_device_whole(): pl.pallas_call(local_iteration, out_shape=jax.ShapeDtypeStruct(values.sha...]
    ppermute x0 -> x10, starting transfers between devices: none -> 11 us  [the longest x3 7.01 us: around(): lax.ppermute(array, 'row', [(r, (r + 2 * step) % bands) for r in range(ba...]
    gather x8 -> x0, local copies, waits for them, and re-layouts: 8.65 us -> none  [the longest x6 8.01 us: select_blocks(): picked = panel_blocks[row_columns[:, :, None], where_slot]]
    unnamed x0 -> x1, other arithmetic: none -> 2.64 us
    convert_element_type x2 -> x0, local copies, waits for them, and re-layouts: 1.54 us -> none  [the longest x1 0.77 us: per_device(): square_low = square.astype(jnp.bfloat16)]
  transfers between devices with their start and end apart: 3 -> 10, of which waited for: 2 -> 7; matrix products, arithmetic and copies ran while one was open for 1% -> 0% of each run, Pallas kernels for 0% -> 0%
where the time goes in v3:
time: 51.5 us; the launch traced here: 50.6 us
  waiting for transfers between devices  20.5 us (40%)
  Pallas kernels  13.8 us (27%)
  starting transfers between devices  11 us (21%)
  other arithmetic  2.82 us (5%)
  local copies, waits for them, and re-layouts  2.43 us (5%)
    pallas_call x1, Pallas kernels, per_device_whole(): pl.pallas_call(local_iteration, out_shape=jax.ShapeDtypeStruct(values.sha...  13.8 us
    ppermute x3, waiting for transfers between devices, across(): return lax.ppermute(array, 'col', [(c, c ^ flip) for c in range(4)])  11.6 us
    ppermute x3, waiting for transfers between devices, around(): lax.ppermute(array, 'row', [(r, (r + 2 * step) % bands) for r in range(ba...  7.54 us
    ppermute x3, starting transfers between devices, around(): lax.ppermute(array, 'row', [(r, (r + 2 * step) % bands) for r in range(ba...  7.01 us
    ppermute x3, starting transfers between devices, across(): return lax.ppermute(array, 'col', [(c, c ^ flip) for c in range(4)])  3.55 us
    unnamed x1, other arithmetic  2.64 us
    unnamed x7, local copies, waits for them, and re-layouts  1.7 us
    ppermute x4, waiting for transfers between devices, sibling(): return lax.ppermute(array, 'row', [(r, r ^ 1) for r in range(bands)])  1.35 us
  transfers between devices with their start and end apart: 10, of which 7 were waited for; matrix products, arithmetic and copies ran while one was open for 0% of the time, Pallas kernels for 0%

profile of v3, /device:TPU:0, one launch (start us, length us, event | category | flops | bytes accessed | tf_op | source)
XLA Modules:
  0.0 50.6 jit_solution(16821632816945078688)
XLA Ops:
  0.0 0.0 copy-start.1
  0.0 0.7 %copy-done.1 = s32[2,2]{1,0:T(2,128)S(1)} copy-done((s32[2,2]{1,0:T(2,128)S(1)}, s32[2,2]{1,0:T(2,128)}, u32[]{:S(2)}) %copy-start.1) | copy-done | bytes 40
  0.7 0.7 %fusion = (s32[1,1]{1,0:T(1,128)}, s32[1,1]{1,0:T(1,128)}, s32[1,1]{1,0:T(1,128)}, s32[1,1]{1,0:T(1,128)}) fusion(s32[2,2]{1,0:T(2,128)S(1)} %copy-done.1), kind=kLoop, calls=%fused_computation.20 | loop fusion | bytes 32 | tf_op jit(solution)/shard_map/slice | solution.py:240
  1.3 0.0 copy-start
  1.4 1.0 %constant_dynamic-update-slice_fusion.4 = bf16[2112,128]{1,0:T(8,128)(2,1)S(1)} fusion(bf16[512,128]{1,0:T(8,128)(2,1)} %bitcast.17), kind=kLoop, calls=%fused_computation.12 | loop fusion | bytes 262144
  2.4 2.6 %constant_dynamic-update-slice_fusion.3 = (bf16[2112,128]{1,0:T(8,128)(2,1)S(1)}, bf16[16,128]{1,0:T(8,128)(2,1)S(1)}) fusion(bf16[2112,128]{1,0:T(8,128)(2,1)S(1)} %constant_dynamic-update-slice_fusion.4, s32[]{:T(128)} %bitcast.6, pred[128]{0:T(512)(128)(4,1)S(1)} %get-tuple-element.18, s32[]{:T(128)} %bitcast.5, pred[128]{0:T(512)(128)(4,1)S(1)} %get-tuple-element.19, ...), kind=kLoop, calls=%fused_computation.11 | loop fusion | flops 18432 | bytes 10768
  5.0 0.0 copy-done
  5.0 3.1 %collective-permute-start = (bf16[528,128]{1,0:T(8,128)(2,1)S(1)}, bf16[528,128]{1,0:T(8,128)(2,1)S(1)}, u32[]{:S(2)}, u32[]{:S(2)}) collective-permute-start(bf16[528,128]{1,0:T(8,128)(2,1)S(1)} %pad_maximum_fusion.3), channel_id=1, source_target_pairs={{0,8},{4,12},{8,16},{12,20},{16,24},{20,28},{24,0},{28,4},{1,9},{5... | collective-permute-start | bytes 405512 | tf_op jit(solution)/shard_map/ppermute | solution.py:58
  8.1 2.6 %collective-permute-start.1 = (bf16[528,128]{1,0:T(8,128)(2,1)S(1)}, bf16[528,128]{1,0:T(8,128)(2,1)S(1)}, u32[]{:S(2)}, u32[]{:S(2)}) collective-permute-start(bf16[528,128]{1,0:T(8,128)(2,1)S(1)} %pad_maximum_fusion.3), channel_id=1, source_target_pairs={{0,16},{4,20},{8,24},{12,28},{16,0},{20,4},{24,8},{28,12},{1,17},{... | collective-permute-start | bytes 405512 | tf_op jit(solution)/shard_map/ppermute | solution.py:58
  10.7 1.3 %collective-permute-start.2 = (bf16[528,128]{1,0:T(8,128)(2,1)S(1)}, bf16[528,128]{1,0:T(8,128)(2,1)S(1)}, u32[]{:S(2)}, u32[]{:S(2)}) collective-permute-start(bf16[528,128]{1,0:T(8,128)(2,1)S(1)} %pad_maximum_fusion.3), channel_id=1, source_target_pairs={{0,24},{4,28},{8,0},{12,4},{16,8},{20,12},{24,16},{28,20},{1,25},{... | collective-permute-start | bytes 405512 | tf_op jit(solution)/shard_map/ppermute | solution.py:58
  12.0 2.6 %collective-permute-done = bf16[528,128]{1,0:T(8,128)(2,1)S(1)} collective-permute-done((bf16[528,128]{1,0:T(8,128)(2,1)S(1)}, bf16[528,128]{1,0:T(8,128)(2,1)S(1)}, u32[]{:S(2)}, u32[]{:S(2)}) %collective-permute-start) | collective-permute-done | bytes 135200 | tf_op jit(solution)/shard_map/ppermute | solution.py:58
  14.7 4.9 %collective-permute-done.1 = bf16[528,128]{1,0:T(8,128)(2,1)S(1)} collective-permute-done((bf16[528,128]{1,0:T(8,128)(2,1)S(1)}, bf16[528,128]{1,0:T(8,128)(2,1)S(1)}, u32[]{:S(2)}, u32[]{:S(2)}) %collective-permute-start.1) | collective-permute-done | bytes 135200 | tf_op jit(solution)/shard_map/ppermute | solution.py:58
  19.6 0.0 collective-permute-done.2
  19.7 0.1 pad_maximum_fusion
  19.8 2.5 %collective-permute-start.6 = (bf16[1056,128]{1,0:T(8,128)(2,1)S(1)}, bf16[1056,128]{1,0:T(8,128)(2,1)S(1)}, u32[]{:S(2)}, u32[]{:S(2)}) collective-permute-start(bf16[1056,128]{1,0:T(8,128)(2,1)S(1)} %get-tuple-element.11), channel_id=1, source_target_pairs={{0,3},{1,2},{2,1},{3,0},{4,7},{5,6},{6,5},{7,4},{8,11},{9,10},{10,... | collective-permute-start | bytes 811016 | tf_op jit(solution)/shard_map/ppermute | solution.py:62
  22.3 0.5 %collective-permute-start.5 = (bf16[1056,128]{1,0:T(8,128)(2,1)S(1)}, bf16[1056,128]{1,0:T(8,128)(2,1)S(1)}, u32[]{:S(2)}, u32[]{:S(2)}) collective-permute-start(bf16[1056,128]{1,0:T(8,128)(2,1)S(1)} %get-tuple-element.12), channel_id=1, source_target_pairs={{0,2},{1,3},{2,0},{3,1},{4,6},{5,7},{6,4},{7,5},{8,10},{9,11},{10,... | collective-permute-start | bytes 811016 | tf_op jit(solution)/shard_map/ppermute | solution.py:62
  22.8 0.5 %collective-permute-start.4 = (bf16[1056,128]{1,0:T(8,128)(2,1)S(1)}, bf16[1056,128]{1,0:T(8,128)(2,1)S(1)}, u32[]{:S(2)}, u32[]{:S(2)}) collective-permute-start(bf16[1056,128]{1,0:T(8,128)(2,1)S(1)} %get-tuple-element.13), channel_id=1, source_target_pairs={{0,1},{1,0},{2,3},{3,2},{4,5},{5,4},{6,7},{7,6},{8,9},{9,8},{10,11... | collective-permute-start | bytes 811016 | tf_op jit(solution)/shard_map/ppermute | solution.py:62
  23.3 0.0 collective-permute-start.3
  23.3 6.8 %collective-permute-done.6.rest_2_ = bf16[1056,128]{1,0:T(8,128)(2,1)S(1)} collective-permute-done((bf16[1056,128]{1,0:T(8,128)(2,1)S(1)}, bf16[1056,128]{1,0:T(8,128)(2,1)S(1)}, u32[]{:S(2)}, u32[]{:S(2)}) %collective-permute-start.6) | collective-permute-done | bytes 270368 | tf_op jit(solution)/shard_map/ppermute | solution.py:62
  30.1 0.0 collective-permute-start.9
  30.2 4.7 %collective-permute-done.5.rest_1_ = bf16[1056,128]{1,0:T(8,128)(2,1)S(1)} collective-permute-done((bf16[1056,128]{1,0:T(8,128)(2,1)S(1)}, bf16[1056,128]{1,0:T(8,128)(2,1)S(1)}, u32[]{:S(2)}, u32[]{:S(2)}) %collective-permute-start.5) | collective-permute-done | bytes 270368 | tf_op jit(solution)/shard_map/ppermute | solution.py:62
  34.9 0.0 collective-permute-start.8
  34.9 0.1 collective-permute-done.4.rest_0_
  35.0 0.4 collective-permute-start.7
  35.4 0.1 pad_add_fusion.origin
  35.4 0.0 collective-permute-done.9.rest_5_
  35.4 1.0 %collective-permute-done.8.rest_4_ = bf16[1056,128]{1,0:T(8,128)(2,1)S(1)} collective-permute-done((bf16[1056,128]{1,0:T(8,128)(2,1)S(1)}, bf16[1056,128]{1,0:T(8,128)(2,1)S(1)}, u32[]{:S(2)}, u32[]{:S(2)}) %collective-permute-start.8) | collective-permute-done | bytes 270368 | tf_op jit(solution)/shard_map/ppermute | solution.py:66
  36.4 0.4 collective-permute-done.7.rest_3_
  36.8 0.0 collective-permute-done.3.line_there
  36.8 13.8 %shard_map.28 = f32[2,2,128,128]{3,2,1,0:T(8,128)} custom-call(s32[2]{0:T(128)S(1)} %pad_add_fusion.origin, bf16[2112,128]{1,0:T(8,128)(2,1)S(1)} %constant_dynamic-update-slice_fusion.line, bf16[2112,128]{1,0:T(8,128)(2,1)S(1)} %collective-permute-done.3.line_there, bf16[1056,128]{1,0:T(8,128)(2,1)S(1)} %collective-permute-done.4.rest_0_, ...), custom_call_target="tpu_custom_call" | custom-call | tf_op jit(solution)/shard_map/pallas_call | solution.py:255
  (8 shorter events, 0.1 us)
Async XLA Ops:
  0.0 0.7 %copy-start.1 = (s32[2,2]{1,0:T(2,128)S(1)}, s32[2,2]{1,0:T(2,128)}, u32[]{:S(2)}) copy-start(s32[2,2]{1,0:T(2,128)} %param.3) | copy-start | bytes 52
  1.3 3.7 %copy-start = (bf16[2,2,128,128]{3,2,1,0:T(8,128)(2,1)S(1)}, bf16[2,2,128,128]{3,2,1,0:T(8,128)(2,1)}, u32[]{:S(2)}) copy-start(bf16[2,2,128,128]{3,2,1,0:T(8,128)(2,1)} %param.2) | copy-start | bytes 393220
  5.0 9.6 %collective-permute-start = (bf16[528,128]{1,0:T(8,128)(2,1)S(1)}, bf16[528,128]{1,0:T(8,128)(2,1)S(1)}, u32[]{:S(2)}, u32[]{:S(2)}) collective-permute-start(bf16[528,128]{1,0:T(8,128)(2,1)S(1)} %pad_maximum_fusion.3), channel_id=1, source_target_pairs={{0,8},{4,12},{8,16},{12,20},{16,24},{20,28},{24,0},{28,4},{1,9},{5... | collective-permute-start | bytes 405512 | tf_op jit(solution)/shard_map/ppermute | solution.py:58
  8.1 11.5 %collective-permute-start.1 = (bf16[528,128]{1,0:T(8,128)(2,1)S(1)}, bf16[528,128]{1,0:T(8,128)(2,1)S(1)}, u32[]{:S(2)}, u32[]{:S(2)}) collective-permute-start(bf16[528,128]{1,0:T(8,128)(2,1)S(1)} %pad_maximum_fusion.3), channel_id=1, source_target_pairs={{0,16},{4,20},{8,24},{12,28},{16,0},{20,4},{24,8},{28,12},{1,17},{... | collective-permute-start | bytes 405512 | tf_op jit(solution)/shard_map/ppermute | solution.py:58
  10.7 8.9 %collective-permute-start.2 = (bf16[528,128]{1,0:T(8,128)(2,1)S(1)}, bf16[528,128]{1,0:T(8,128)(2,1)S(1)}, u32[]{:S(2)}, u32[]{:S(2)}) collective-permute-start(bf16[528,128]{1,0:T(8,128)(2,1)S(1)} %pad_maximum_fusion.3), channel_id=1, source_target_pairs={{0,24},{4,28},{8,0},{12,4},{16,8},{20,12},{24,16},{28,20},{1,25},{... | collective-permute-start | bytes 405512 | tf_op jit(solution)/shard_map/ppermute | solution.py:58
  19.8 10.4 %collective-permute-start.6 = (bf16[1056,128]{1,0:T(8,128)(2,1)S(1)}, bf16[1056,128]{1,0:T(8,128)(2,1)S(1)}, u32[]{:S(2)}, u32[]{:S(2)}) collective-permute-start(bf16[1056,128]{1,0:T(8,128)(2,1)S(1)} %get-tuple-element.11), channel_id=1, source_target_pairs={{0,3},{1,2},{2,1},{3,0},{4,7},{5,6},{6,5},{7,4},{8,11},{9,10},{10,... | collective-permute-start | bytes 811016 | tf_op jit(solution)/shard_map/ppermute | solution.py:62
  22.3 12.6 %collective-permute-start.5 = (bf16[1056,128]{1,0:T(8,128)(2,1)S(1)}, bf16[1056,128]{1,0:T(8,128)(2,1)S(1)}, u32[]{:S(2)}, u32[]{:S(2)}) collective-permute-start(bf16[1056,128]{1,0:T(8,128)(2,1)S(1)} %get-tuple-element.12), channel_id=1, source_target_pairs={{0,2},{1,3},{2,0},{3,1},{4,6},{5,7},{6,4},{7,5},{8,10},{9,11},{10,... | collective-permute-start | bytes 811016 | tf_op jit(solution)/shard_map/ppermute | solution.py:62
  22.8 12.1 %collective-permute-start.4 = (bf16[1056,128]{1,0:T(8,128)(2,1)S(1)}, bf16[1056,128]{1,0:T(8,128)(2,1)S(1)}, u32[]{:S(2)}, u32[]{:S(2)}) collective-permute-start(bf16[1056,128]{1,0:T(8,128)(2,1)S(1)} %get-tuple-element.13), channel_id=1, source_target_pairs={{0,1},{1,0},{2,3},{3,2},{4,5},{5,4},{6,7},{7,6},{8,9},{9,8},{10,11... | collective-permute-start | bytes 811016 | tf_op jit(solution)/shard_map/ppermute | solution.py:62
  23.3 13.5 %collective-permute-start.3 = (bf16[2112,128]{1,0:T(8,128)(2,1)S(1)}, bf16[2112,128]{1,0:T(8,128)(2,1)S(1)}, u32[]{:S(2)}, u32[]{:S(2)}) collective-permute-start(bf16[2112,128]{1,0:T(8,128)(2,1)S(1)} %constant_dynamic-update-slice_fusion.line), channel_id=1, source_target_pairs={{0,4},{4,0},{8,12},{12,8},{16,20},{20,16},{24,28},{28,24},{1,5},{5... | collective-permute-start | bytes 1622024 | tf_op jit(solution)/shard_map/ppermute | solution.py:66
  30.1 5.3 %collective-permute-start.9 = (bf16[1056,128]{1,0:T(8,128)(2,1)S(1)}, bf16[1056,128]{1,0:T(8,128)(2,1)S(1)}, u32[]{:S(2)}, u32[]{:S(2)}) collective-permute-start(bf16[1056,128]{1,0:T(8,128)(2,1)S(1)} %collective-permute-done.6.rest_2_), channel_id=1, source_target_pairs={{0,4},{4,0},{8,12},{12,8},{16,20},{20,16},{24,28},{28,24},{1,5},{5... | collective-permute-start | bytes 811016 | tf_op jit(solution)/shard_map/ppermute | solution.py:66
  34.9 1.5 %collective-permute-start.8 = (bf16[1056,128]{1,0:T(8,128)(2,1)S(1)}, bf16[1056,128]{1,0:T(8,128)(2,1)S(1)}, u32[]{:S(2)}, u32[]{:S(2)}) collective-permute-start(bf16[1056,128]{1,0:T(8,128)(2,1)S(1)} %collective-permute-done.5.rest_1_), channel_id=1, source_target_pairs={{0,4},{4,0},{8,12},{12,8},{16,20},{20,16},{24,28},{28,24},{1,5},{5... | collective-permute-start | bytes 811016 | tf_op jit(solution)/shard_map/ppermute | solution.py:66
  35.0 1.8 %collective-permute-start.7 = (bf16[1056,128]{1,0:T(8,128)(2,1)S(1)}, bf16[1056,128]{1,0:T(8,128)(2,1)S(1)}, u32[]{:S(2)}, u32[]{:S(2)}) collective-permute-start(bf16[1056,128]{1,0:T(8,128)(2,1)S(1)} %collective-permute-done.4.rest_0_), channel_id=1, source_target_pairs={{0,4},{4,0},{8,12},{12,8},{16,20},{20,16},{24,28},{28,24},{1,5},{5... | collective-permute-start | bytes 811016 | tf_op jit(solution)/shard_map/ppermute | solution.py:66

commit v4 on v3

--- a/solution.py
+++ b/solution.py
@@ -70,30 +70,30 @@
     return jnp.where(flip == 3, 1, flip + 1)
 
 
-def local_iteration(
-    origin, line, line_there, *rest
-):
-    here, there = rest[:3], rest[3:6]
-    out, xs, ys, qs, numbers, pattern, table, near, used, sem = rest[6:]
+def local_iteration(origin, *rest):
+    lines, planes = rest[:4], rest[4:16]
+    out, xs, ys, qs, numbers, pattern, x_table, y_table, near, sem = rest[16:]
     rows, kept, slots, size = 16, 8, 2, 128
     band, c = origin[0], origin[1]
     z, core = lax.div(band, 2), lax.rem(band, 2)
-    chunk = 4 * size + TILE
+    half = slots * size
 
     pieces = []
-    for source, side in ((line, core), (line_there, 1 - core)):
-        for step in range(4):
-            pieces.append((source, step * chunk, step * 8 + side * 4))
-    for group, side in ((here, core), (there, 1 - core)):
-        for flip in range(3):
-            for part in range(2):
-                pieces.append(
-                    (group[flip], part * chunk, (4 + flip * 2 + part) * 8 + side * 4)
-                )
-
     total = jnp.zeros((TILE, size), jnp.float32)
-    for source, first, _ in pieces:
-        total += source[first + 4 * size : first + chunk, :].astype(jnp.float32)
+    for a in range(2):
+        long = half + a * TILE
+        for source, side in ((lines[a], core), (lines[2 + a], 1 - core)):
+            for step in range(4):
+                pieces.append((source, step * long, step * 8 + side * 4 + a * 2))
+                if a == 1:
+                    total += source[step * long + half : step * long + long, :].astype(jnp.float32)
+        for group, side in ((planes[a * 3 : a * 3 + 3], core), (planes[6 + a * 3 : 9 + a * 3], 1 - core)):
+            for flip in range(3):
+                for part in range(2):
+                    place = (4 + flip * 2 + part) * 8 + side * 4 + a * 2
+                    pieces.append((group[flip], part * half, place))
+                if a == 1:
+                    total += group[flip][2 * half : 2 * half + TILE, :].astype(jnp.float32)
     numbers[...] = total[0:8].astype(jnp.int32)
     copy = pltpu.make_async_copy(numbers, pattern, sem)
     copy.start()
@@ -103,59 +103,50 @@
     xs[empty] = nothing
     ys[rows * kept] = nothing
     qs[rows * slots] = nothing
-    blank = empty + rows * kept * 256
 
     def clear(at, carry):
-        table[at] = blank
+        x_table[at] = empty
+        y_table[at] = rows * kept
         return carry
 
     lax.fori_loop(0, rows * rows, clear, 0, unroll=16)
 
     for source, first, place in pieces:
-        for b in range(4):
+        for b in range(slots):
             xs[place + b] = source[first + b * size : first + (b + 1) * size, :]
     for number, piece in enumerate((0, 1, 2, 3, 5, 7, 9)):
         for b in range(8):
             xs[80 + number * 8 + b] = xs[piece * 8 + b].T
     copy.wait()
 
-    def enter(i, j, place, slot):
-        table[i * rows + j] = place + (i * kept + slot) * 256
-        near[i * kept + slot] = j
-
-    def known(h, g, base, mirror):
-        if mirror is not None:
-            for local in range(4):
-                used[local] = 0
+    def entries(h, g):
         for il in range(4):
             for t in range(slots):
-                i = 4 * h + il
                 j = pattern[0, ((h * 2 + il // 2) * 4 + g) * 4 + (il % 2) * slots + t]
-                enter(i, j, base + il * slots + t, g * slots + t)
-                if mirror is not None:
-                    local = j - 4 * g
-                    taken = used[local]
-                    used[local] = taken + 1
-                    enter(j, i, mirror + il * slots + t, h * slots + taken)
+                yield 4 * h + il, j, il * slots + t, g * slots + t
 
     for h in range(4):
-        flip = h ^ c
-        own = lax.rem(z - h + 4, 4) * 8
-        base = jnp.where(flip == 0, own, (4 + (flip - 1) * 2) * 8)
-        known(h, h, base, None)
-    for first in range(4):
-        for second in range(first + 1, 4):
-            flip_first, flip_second = first ^ c, second ^ c
-            straight = (flip_second == 0) | (
-                (flip_first != 0) & (next_flip(flip_second) == (first ^ second))
-            )
-            h = jnp.where(straight, first, second)
-            g = first + second - h
+        for g in range(4):
             flip = g ^ c
             own = lax.rem(z - h + 4, 4) * 8
-            base = jnp.where(flip == 0, own, (5 + (flip - 1) * 2) * 8)
-            mirror = 80 + jnp.where(flip == 0, own, (4 + flip - 1) * 8)
-            known(h, g, base, mirror)
+            if h == g:
+                base = jnp.where(flip == 0, own, (4 + (flip - 1) * 2) * 8)
+            else:
+                straight = (flip == 0) | (((h ^ c) != 0) & (next_flip(flip) == (h ^ g)))
+                base = jnp.where(flip == 0, own, (5 + (flip - 1) * 2) * 8)
+                mirror = 80 + jnp.where(flip == 0, own, (3 + flip) * 8)
+            for i, j, number, slot in entries(h, g):
+                near[i * kept + slot] = j
+                y_table[i * rows + j] = i * kept + slot
+                if h == g:
+                    x_table[i * rows + j] = base + number
+            if h != g:
+
+                @pl.when(straight)
+                def _():
+                    for i, j, number, slot in entries(h, g):
+                        x_table[i * rows + j] = base + number
+                        x_table[j * rows + i] = mirror + number
 
     def wide(parts):
         return jnp.concatenate(parts, axis=1)
@@ -167,25 +158,24 @@
         return jnp.dot(left, right, preferred_element_type=jnp.float32)
 
     def x_at(k, j):
-        return table[k * rows + j] & 255
+        return x_table[k * rows + j]
 
     def y_at(k, j):
-        return lax.shift_right_logical(table[k * rows + j], 8)
+        return y_table[k * rows + j]
 
     for home in range(4):
 
         def square(i, carry):
             ks = [near[i * kept + s] for s in range(kept)]
             left = wide([xs[x_at(i, k)] for k in ks])
-            for p in range(home, 4):
-                js = ks[p * slots : (p + 1) * slots]
-                right = tall([wide([xs[x_at(k, j)] for j in js]) for k in ks])
-                product = dot(left, right).astype(jnp.bfloat16)
-                for t in range(slots):
-                    block = product[:, t * size : (t + 1) * size]
-                    ys[i * kept + p * slots + t] = block
-                    if p > home:
-                        ys[y_at(js[t], i)] = block.T
+            js = ks[home * slots :]
+            right = tall([wide([xs[x_at(k, j)] for j in js]) for k in ks])
+            product = dot(left, right).astype(jnp.bfloat16)
+            for t, j in enumerate(js):
+                block = product[:, t * size : (t + 1) * size]
+                ys[i * kept + home * slots + t] = block
+                if t >= slots:
+                    ys[y_at(j, i)] = block.T
             return carry
 
         lax.fori_loop(home * 4, home * 4 + 4, square, 0)
@@ -238,25 +228,30 @@
     for m in range(4):
         here = (lane == first + m) & (line_number == 0)
         tile = jnp.where(here, columns[m // 2, m % 2], tile)
-    mine = jnp.concatenate([values.reshape(4 * size, size), tile.astype(jnp.bfloat16)])
-    line = jnp.concatenate([mine] + [around(mine, step, bands) for step in range(1, 4)])
-    stacked = line.reshape(4, *mine.shape)
-
-    def pick(h):
-        return lax.dynamic_index_in_dim(stacked, (z - h) % 4, axis=0, keepdims=False)
-
-    here = []
-    for flip in range(1, 4):
-        payload = jnp.concatenate([pick(c), pick(c ^ NEXT[flip])])
-        here.append(across(payload, flip))
-    line_there = sibling(line, bands)
+    halves = values.reshape(2, 2 * size, size)
+    mine = (halves[0], jnp.concatenate([halves[1], tile.astype(jnp.bfloat16)]))
+
+    def from_line(line, h):
+        return lax.dynamic_index_in_dim(line, (z - h) % 4, axis=0, keepdims=False)
+
+    lines = [
+        jnp.stack([half] + [around(half, step, bands) for step in range(1, 4)]) for half in mine
+    ]
+    here, lines_there = [], []
+    for a, line in enumerate(lines):
+        tail = [jnp.sum(line[:, 2 * size :], axis=0)] if a else []
+        for flip in range(1, 4):
+            parts = [from_line(line, h)[: 2 * size] for h in (c, c ^ NEXT[flip])]
+            here.append(across(jnp.concatenate(parts + tail), flip))
+        lines_there.append(sibling(line.reshape(-1, size), bands))
     there = [sibling(piece, bands) for piece in here]
+    lines = [line.reshape(-1, size) for line in lines]
     origin = jnp.stack([band, c]).astype(jnp.int32)
     return pl.pallas_call(
         local_iteration,
         out_shape=jax.ShapeDtypeStruct(values.shape, jnp.float32),
         in_specs=[pl.BlockSpec(memory_space=pltpu.SMEM)]
-        + [pl.BlockSpec(memory_space=pltpu.VMEM)] * 8,
+        + [pl.BlockSpec(memory_space=pltpu.VMEM)] * 16,
         out_specs=pl.BlockSpec(memory_space=pltpu.VMEM),
         scratch_shapes=[
             pltpu.VMEM((17 * 8 + 1, size, size), jnp.bfloat16),
@@ -265,12 +260,12 @@
             pltpu.VMEM((8, size), jnp.int32),
             pltpu.SMEM((8, size), jnp.int32),
             pltpu.SMEM((256,), jnp.int32),
+            pltpu.SMEM((256,), jnp.int32),
             pltpu.SMEM((128,), jnp.int32),
-            pltpu.SMEM((4,), jnp.int32),
             pltpu.SemaphoreType.DMA,
         ],
         compiler_params=pltpu.CompilerParams(vmem_limit_bytes=32 * 1024 * 1024),
-    )(origin, line, line_there, *here, *there)
+    )(origin, *lines, *lines_there, *here, *there)
 
 
 def per_device(values, columns):

time: 51.5 us -> 47.8 us (0.928); the launches traced: 50.6 us -> 47.6 us
  waiting for transfers between devices: 20.5 us -> 6.84 us
  starting transfers between devices: 11 us -> 21.6 us
    ppermute x3 -> x6, waiting for transfers between devices: 7.54 us -> 0.02 us  [around(): lax.ppermute(array, 'row', [(r, (r + 2 * step) % bands) for r in range(ba...]
    ppermute x3 -> x6, waiting for transfers between devices: 11.6 us -> 5.81 us  [across(): return lax.ppermute(array, 'col', [(c, c ^ flip) for c in range(4)])]
    ppermute x3 -> x6, starting transfers between devices: 7.01 us -> 11.9 us  [around(): lax.ppermute(array, 'row', [(r, (r + 2 * step) % bands) for r in range(ba...]
    ppermute x3 -> x6, starting transfers between devices: 3.55 us -> 8.09 us  [across(): return lax.ppermute(array, 'col', [(c, c ^ flip) for c in range(4)])]
    convert_element_type x0 -> x1, other arithmetic: none -> 2.69 us  [per_device_whole(): mine = (halves[0], jnp.concatenate([halves[1], tile.astype(jnp.bfloat16)]))]
    unnamed x1 -> x0, other arithmetic: 2.64 us -> none
    ppermute x4 -> x8, starting transfers between devices: 0.44 us -> 1.6 us  [sibling(): return lax.ppermute(array, 'row', [(r, r ^ 1) for r in range(bands)])]
    unnamed x7 -> x2, local copies, waits for them, and re-layouts: 1.7 us -> 0.67 us
  transfers between devices with their start and end apart: 10 -> 20, of which waited for: 7 -> 8; matrix products, arithmetic and copies ran while one was open for 0% -> 8% of each run, Pallas kernels for 0% -> 0%
where the time goes in v4:
time: 47.8 us; the launch traced here: 47.6 us
  starting transfers between devices  21.6 us (45%)
  Pallas kernels  13.8 us (29%)
  waiting for transfers between devices  6.84 us (14%)
  other arithmetic  2.94 us (6%)
  local copies, waits for them, and re-layouts  2.28 us (5%)
    pallas_call x1, Pallas kernels, per_device_whole(): pl.pallas_call(local_iteration, out_shape=jax.ShapeDtypeStruct(values.sha...  13.8 us
    ppermute x6, starting transfers between devices, around(): lax.ppermute(array, 'row', [(r, (r + 2 * step) % bands) for r in range(ba...  11.9 us
    ppermute x6, starting transfers between devices, across(): return lax.ppermute(array, 'col', [(c, c ^ flip) for c in range(4)])  8.09 us
    ppermute x6, waiting for transfers between devices, across(): return lax.ppermute(array, 'col', [(c, c ^ flip) for c in range(4)])  5.81 us
    convert_element_type x1, other arithmetic, per_device_whole(): mine = (halves[0], jnp.concatenate([halves[1], tile.astype(jnp.bfloat16)]))  2.69 us
    ppermute x8, starting transfers between devices, sibling(): return lax.ppermute(array, 'row', [(r, r ^ 1) for r in range(bands)])  1.6 us
    ppermute x8, waiting for transfers between devices, sibling(): return lax.ppermute(array, 'row', [(r, r ^ 1) for r in range(bands)])  1.02 us
  transfers between devices with their start and end apart: 20, of which 8 were waited for; matrix products, arithmetic and copies ran while one was open for 8% of the time, Pallas kernels for 0%

profile of v4, /device:TPU:0, one launch (start us, length us, event | category | flops | bytes accessed | tf_op | source)
XLA Modules:
  0.0 47.6 jit_solution(5771956506859607061)
XLA Ops:
  0.0 0.9 %fusion.1 = (bf16[1,2,128,128]{3,2,1,0:T(8,128)(2,1)S(1)}, bf16[1,2,128,128]{3,2,1,0:T(8,128)(2,1)S(1)}) fusion(bf16[2,2,128,128]{3,2,1,0:T(8,128)(2,1)} %param.2), kind=kLoop, calls=%fused_computation.29 | loop fusion | bytes 262144 | tf_op jit(solution)/shard_map/slice | solution.py:232
  0.9 5.1 %collective-permute-start.2 = (bf16[256,128]{1,0:T(8,128)(2,1)S(1)}, bf16[256,128]{1,0:T(8,128)(2,1)S(1)}, u32[]{:S(2)}, u32[]{:S(2)}) collective-permute-start(bf16[256,128]{1,0:T(8,128)(2,1)S(1)} %bitcast.40), channel_id=1, source_target_pairs={{0,24},{4,28},{8,0},{12,4},{16,8},{20,12},{24,16},{28,20},{1,25},{... | collective-permute-start | bytes 196616 | tf_op jit(solution)/shard_map/ppermute | solution.py:58
  6.0 1.0 %collective-permute-start = (bf16[256,128]{1,0:T(8,128)(2,1)S(1)}, bf16[256,128]{1,0:T(8,128)(2,1)S(1)}, u32[]{:S(2)}, u32[]{:S(2)}) collective-permute-start(bf16[256,128]{1,0:T(8,128)(2,1)S(1)} %bitcast.42), channel_id=1, source_target_pairs={{0,8},{4,12},{8,16},{12,20},{16,24},{20,28},{24,0},{28,4},{1,9},{5... | collective-permute-start | bytes 196616 | tf_op jit(solution)/shard_map/ppermute | solution.py:58
  7.0 0.7 %copy-done = s32[2,2]{1,0:T(2,128)S(1)} copy-done((s32[2,2]{1,0:T(2,128)S(1)}, s32[2,2]{1,0:T(2,128)}, u32[]{:S(2)}) %copy-start) | copy-done | bytes 40
  7.7 0.7 %fusion.2 = (s32[1,1]{1,0:T(1,128)}, s32[1,1]{1,0:T(1,128)}, s32[1,1]{1,0:T(1,128)}, s32[1,1]{1,0:T(1,128)}) fusion(s32[2,2]{1,0:T(2,128)S(1)} %copy-done), kind=kLoop, calls=%fused_computation.30 | loop fusion | bytes 32 | tf_op jit(solution)/shard_map/slice | solution.py:230
  8.4 2.7 %select_convert_fusion = bf16[16,128]{1,0:T(8,128)(2,1)S(1)} fusion(s32[]{:T(128)} %bitcast.12, s32[]{:T(128)} %bitcast.11, s32[]{:T(128)} %bitcast.10, s32[]{:T(128)} %bitcast.9, pred[128]{0:T(512)(128)(4,1)S(1)} %get-tuple-element.27, pred[128]{0:T(512)(128)(4,1)S(1)} %get-tuple-element.28, pred[128]{0:T(512)(128)(4,1)S(1)} %get-tuple-element.29, ...), kind=kLoop, calls=%fused_computation.21 | loop fusion | flops 18432 | bytes 4640 | tf_op jit(solution)/shard_map/convert_element_type | solution.py:232
  11.1 2.0 %collective-permute-start.4 = (bf16[272,128]{1,0:T(8,128)(2,1)S(1)}, bf16[272,128]{1,0:T(8,128)(2,1)S(1)}, u32[]{:S(2)}, u32[]{:S(2)}) collective-permute-start(bf16[272,128]{1,0:T(8,128)(2,1)S(1)} %get-tuple-element.19), channel_id=1, source_target_pairs={{0,16},{4,20},{8,24},{12,28},{16,0},{20,4},{24,8},{28,12},{1,17},{... | collective-permute-start | bytes 208904 | tf_op jit(solution)/shard_map/ppermute | solution.py:58
  13.0 1.5 %collective-permute-start.3 = (bf16[272,128]{1,0:T(8,128)(2,1)S(1)}, bf16[272,128]{1,0:T(8,128)(2,1)S(1)}, u32[]{:S(2)}, u32[]{:S(2)}) collective-permute-start(bf16[272,128]{1,0:T(8,128)(2,1)S(1)} %get-tuple-element.19), channel_id=1, source_target_pairs={{0,8},{4,12},{8,16},{12,20},{16,24},{20,28},{24,0},{28,4},{1,9},{5... | collective-permute-start | bytes 208904 | tf_op jit(solution)/shard_map/ppermute | solution.py:58
  14.5 2.4 %collective-permute-start.5 = (bf16[272,128]{1,0:T(8,128)(2,1)S(1)}, bf16[272,128]{1,0:T(8,128)(2,1)S(1)}, u32[]{:S(2)}, u32[]{:S(2)}) collective-permute-start(bf16[272,128]{1,0:T(8,128)(2,1)S(1)} %get-tuple-element.19), channel_id=1, source_target_pairs={{0,24},{4,28},{8,0},{12,4},{16,8},{20,12},{24,16},{28,20},{1,25},{... | collective-permute-start | bytes 208904 | tf_op jit(solution)/shard_map/ppermute | solution.py:58
  16.9 0.0 collective-permute-done.1
  16.9 0.0 collective-permute-done
  17.0 2.5 %collective-permute-start.10 = (bf16[512,128]{1,0:T(8,128)(2,1)S(1)}, bf16[512,128]{1,0:T(8,128)(2,1)S(1)}, u32[]{:S(2)}, u32[]{:S(2)}) collective-permute-start(bf16[512,128]{1,0:T(8,128)(2,1)S(1)} %get-tuple-element.20), channel_id=1, source_target_pairs={{0,3},{1,2},{2,1},{3,0},{4,7},{5,6},{6,5},{7,4},{8,11},{9,10},{10,... | collective-permute-start | bytes 393224 | tf_op jit(solution)/shard_map/ppermute | solution.py:62
  19.5 0.5 %collective-permute-start.9 = (bf16[512,128]{1,0:T(8,128)(2,1)S(1)}, bf16[512,128]{1,0:T(8,128)(2,1)S(1)}, u32[]{:S(2)}, u32[]{:S(2)}) collective-permute-start(bf16[512,128]{1,0:T(8,128)(2,1)S(1)} %get-tuple-element.21), channel_id=1, source_target_pairs={{0,2},{1,3},{2,0},{3,1},{4,6},{5,7},{6,4},{7,5},{8,10},{9,11},{10,... | collective-permute-start | bytes 393224 | tf_op jit(solution)/shard_map/ppermute | solution.py:62
  20.2 2.5 %collective-permute-start.13 = (bf16[528,128]{1,0:T(8,128)(2,1)S(1)}, bf16[528,128]{1,0:T(8,128)(2,1)S(1)}, u32[]{:S(2)}, u32[]{:S(2)}) collective-permute-start(bf16[528,128]{1,0:T(8,128)(2,1)S(1)} %get-tuple-element.15), channel_id=1, source_target_pairs={{0,3},{1,2},{2,1},{3,0},{4,7},{5,6},{6,5},{7,4},{8,11},{9,10},{10,... | collective-permute-start | bytes 405512 | tf_op jit(solution)/shard_map/ppermute | solution.py:62
  22.6 0.5 %collective-permute-start.12 = (bf16[528,128]{1,0:T(8,128)(2,1)S(1)}, bf16[528,128]{1,0:T(8,128)(2,1)S(1)}, u32[]{:S(2)}, u32[]{:S(2)}) collective-permute-start(bf16[528,128]{1,0:T(8,128)(2,1)S(1)} %get-tuple-element.16), channel_id=1, source_target_pairs={{0,2},{1,3},{2,0},{3,1},{4,6},{5,7},{6,4},{7,5},{8,10},{9,11},{10,... | collective-permute-start | bytes 405512 | tf_op jit(solution)/shard_map/ppermute | solution.py:62
  23.1 0.6 %collective-permute-start.8 = (bf16[512,128]{1,0:T(8,128)(2,1)S(1)}, bf16[512,128]{1,0:T(8,128)(2,1)S(1)}, u32[]{:S(2)}, u32[]{:S(2)}) collective-permute-start(bf16[512,128]{1,0:T(8,128)(2,1)S(1)} %get-tuple-element.22), channel_id=1, source_target_pairs={{0,1},{1,0},{2,3},{3,2},{4,5},{5,4},{6,7},{7,6},{8,9},{9,8},{10,11... | collective-permute-start | bytes 393224 | tf_op jit(solution)/shard_map/ppermute | solution.py:62
  23.7 0.6 %collective-permute-done.10.rest_6_ = bf16[512,128]{1,0:T(8,128)(2,1)S(1)} collective-permute-done((bf16[512,128]{1,0:T(8,128)(2,1)S(1)}, bf16[512,128]{1,0:T(8,128)(2,1)S(1)}, u32[]{:S(2)}, u32[]{:S(2)}) %collective-permute-start.10) | collective-permute-done | bytes 131104 | tf_op jit(solution)/shard_map/ppermute | solution.py:62
  24.4 1.5 %collective-permute-start.11 = (bf16[528,128]{1,0:T(8,128)(2,1)S(1)}, bf16[528,128]{1,0:T(8,128)(2,1)S(1)}, u32[]{:S(2)}, u32[]{:S(2)}) collective-permute-start(bf16[528,128]{1,0:T(8,128)(2,1)S(1)} %get-tuple-element.17), channel_id=1, source_target_pairs={{0,1},{1,0},{2,3},{3,2},{4,5},{5,4},{6,7},{7,6},{8,9},{9,8},{10,11... | collective-permute-start | bytes 405512 | tf_op jit(solution)/shard_map/ppermute | solution.py:62
  25.9 2.9 %collective-permute-done.9.rest_5_ = bf16[512,128]{1,0:T(8,128)(2,1)S(1)} collective-permute-done((bf16[512,128]{1,0:T(8,128)(2,1)S(1)}, bf16[512,128]{1,0:T(8,128)(2,1)S(1)}, u32[]{:S(2)}, u32[]{:S(2)}) %collective-permute-start.9) | collective-permute-done | bytes 131104 | tf_op jit(solution)/shard_map/ppermute | solution.py:62
  28.8 1.4 %collective-permute-done.8.rest_4_ = bf16[512,128]{1,0:T(8,128)(2,1)S(1)} collective-permute-done((bf16[512,128]{1,0:T(8,128)(2,1)S(1)}, bf16[512,128]{1,0:T(8,128)(2,1)S(1)}, u32[]{:S(2)}, u32[]{:S(2)}) %collective-permute-start.8) | collective-permute-done | bytes 131104 | tf_op jit(solution)/shard_map/ppermute | solution.py:62
  30.2 0.5 %collective-permute-start.15 = (bf16[512,128]{1,0:T(8,128)(2,1)S(1)}, bf16[512,128]{1,0:T(8,128)(2,1)S(1)}, u32[]{:S(2)}, u32[]{:S(2)}) collective-permute-start(bf16[512,128]{1,0:T(8,128)(2,1)S(1)} %collective-permute-done.9.rest_5_), channel_id=1, source_target_pairs={{0,4},{4,0},{8,12},{12,8},{16,20},{20,16},{24,28},{28,24},{1,5},{5... | collective-permute-start | bytes 393224 | tf_op jit(solution)/shard_map/ppermute | solution.py:66
  30.7 0.1 collective-permute-start.14
  30.8 0.9 %collective-permute-done.11.rest_7_ = bf16[528,128]{1,0:T(8,128)(2,1)S(1)} collective-permute-done((bf16[528,128]{1,0:T(8,128)(2,1)S(1)}, bf16[528,128]{1,0:T(8,128)(2,1)S(1)}, u32[]{:S(2)}, u32[]{:S(2)}) %collective-permute-start.11) | collective-permute-done | bytes 135200 | tf_op jit(solution)/shard_map/ppermute | solution.py:62
  31.6 0.5 %collective-permute-start.19 = (bf16[528,128]{1,0:T(8,128)(2,1)S(1)}, bf16[528,128]{1,0:T(8,128)(2,1)S(1)}, u32[]{:S(2)}, u32[]{:S(2)}) collective-permute-start(bf16[528,128]{1,0:T(8,128)(2,1)S(1)} %collective-permute-done.13.rest_9_), channel_id=1, source_target_pairs={{0,4},{4,0},{8,12},{12,8},{16,20},{20,16},{24,28},{28,24},{1,5},{5... | collective-permute-start | bytes 405512 | tf_op jit(solution)/shard_map/ppermute | solution.py:66
  32.2 0.1 collective-permute-start.18
  32.2 0.4 collective-permute-start.17
  32.7 0.1 pad_add_fusion.origin
  32.7 0.4 collective-permute-done.6.rest_2_
  33.2 0.2 collective-permute-done.19.rest_15_
  33.4 0.2 collective-permute-done.18.rest_14_
  33.6 0.2 collective-permute-done.17.rest_13_
  33.8 13.8 %shard_map.28 = f32[2,2,128,128]{3,2,1,0:T(8,128)} custom-call(s32[2]{0:T(128)S(1)} %pad_add_fusion.origin, bf16[1024,128]{1,0:T(8,128)(2,1)S(1)} %bitcast.38, bf16[1088,128]{1,0:T(8,128)(2,1)S(1)} %bitcast.36, bf16[1024,128]{1,0:T(8,128)(2,1)S(1)} %collective-permute-done.6.rest_2_, bf16[1088,128]{1,0:T(8,128)(2,1)S(1)} %collective-permute-done.7.rest_3_, ...), custom_call_target="tpu_custom_call" | custom-call | tf_op jit(solution)/shard_map/pallas_call | solution.py:250
  (26 shorter events, 0.3 us)
Async XLA Ops:
  0.9 13.6 %collective-permute-start.2 = (bf16[256,128]{1,0:T(8,128)(2,1)S(1)}, bf16[256,128]{1,0:T(8,128)(2,1)S(1)}, u32[]{:S(2)}, u32[]{:S(2)}) collective-permute-start(bf16[256,128]{1,0:T(8,128)(2,1)S(1)} %bitcast.40), channel_id=1, source_target_pairs={{0,24},{4,28},{8,0},{12,4},{16,8},{20,12},{24,16},{28,20},{1,25},{... | collective-permute-start | bytes 196616 | tf_op jit(solution)/shard_map/ppermute | solution.py:58
  6.0 10.9 %collective-permute-start.1 = (bf16[256,128]{1,0:T(8,128)(2,1)S(1)}, bf16[256,128]{1,0:T(8,128)(2,1)S(1)}, u32[]{:S(2)}, u32[]{:S(2)}) collective-permute-start(bf16[256,128]{1,0:T(8,128)(2,1)S(1)} %bitcast.41), channel_id=1, source_target_pairs={{0,16},{4,20},{8,24},{12,28},{16,0},{20,4},{24,8},{28,12},{1,17},{... | collective-permute-start | bytes 196616 | tf_op jit(solution)/shard_map/ppermute | solution.py:58
  6.0 10.9 %collective-permute-start = (bf16[256,128]{1,0:T(8,128)(2,1)S(1)}, bf16[256,128]{1,0:T(8,128)(2,1)S(1)}, u32[]{:S(2)}, u32[]{:S(2)}) collective-permute-start(bf16[256,128]{1,0:T(8,128)(2,1)S(1)} %bitcast.42), channel_id=1, source_target_pairs={{0,8},{4,12},{8,16},{12,20},{16,24},{20,28},{24,0},{28,4},{1,9},{5... | collective-permute-start | bytes 196616 | tf_op jit(solution)/shard_map/ppermute | solution.py:58
  7.0 0.7 %copy-start = (s32[2,2]{1,0:T(2,128)S(1)}, s32[2,2]{1,0:T(2,128)}, u32[]{:S(2)}) copy-start(s32[2,2]{1,0:T(2,128)} %param.3) | copy-start | bytes 52
  11.1 9.0 %collective-permute-start.4 = (bf16[272,128]{1,0:T(8,128)(2,1)S(1)}, bf16[272,128]{1,0:T(8,128)(2,1)S(1)}, u32[]{:S(2)}, u32[]{:S(2)}) collective-permute-start(bf16[272,128]{1,0:T(8,128)(2,1)S(1)} %get-tuple-element.19), channel_id=1, source_target_pairs={{0,16},{4,20},{8,24},{12,28},{16,0},{20,4},{24,8},{28,12},{1,17},{... | collective-permute-start | bytes 208904 | tf_op jit(solution)/shard_map/ppermute | solution.py:58
  13.0 7.0 %collective-permute-start.3 = (bf16[272,128]{1,0:T(8,128)(2,1)S(1)}, bf16[272,128]{1,0:T(8,128)(2,1)S(1)}, u32[]{:S(2)}, u32[]{:S(2)}) collective-permute-start(bf16[272,128]{1,0:T(8,128)(2,1)S(1)} %get-tuple-element.19), channel_id=1, source_target_pairs={{0,8},{4,12},{8,16},{12,20},{16,24},{20,28},{24,0},{28,4},{1,9},{5... | collective-permute-start | bytes 208904 | tf_op jit(solution)/shard_map/ppermute | solution.py:58
  14.5 5.5 %collective-permute-start.5 = (bf16[272,128]{1,0:T(8,128)(2,1)S(1)}, bf16[272,128]{1,0:T(8,128)(2,1)S(1)}, u32[]{:S(2)}, u32[]{:S(2)}) collective-permute-start(bf16[272,128]{1,0:T(8,128)(2,1)S(1)} %get-tuple-element.19), channel_id=1, source_target_pairs={{0,24},{4,28},{8,0},{12,4},{16,8},{20,12},{24,16},{28,20},{1,25},{... | collective-permute-start | bytes 208904 | tf_op jit(solution)/shard_map/ppermute | solution.py:58
  17.0 7.4 %collective-permute-start.10 = (bf16[512,128]{1,0:T(8,128)(2,1)S(1)}, bf16[512,128]{1,0:T(8,128)(2,1)S(1)}, u32[]{:S(2)}, u32[]{:S(2)}) collective-permute-start(bf16[512,128]{1,0:T(8,128)(2,1)S(1)} %get-tuple-element.20), channel_id=1, source_target_pairs={{0,3},{1,2},{2,1},{3,0},{4,7},{5,6},{6,5},{7,4},{8,11},{9,10},{10,... | collective-permute-start | bytes 393224 | tf_op jit(solution)/shard_map/ppermute | solution.py:62
  19.5 9.3 %collective-permute-start.9 = (bf16[512,128]{1,0:T(8,128)(2,1)S(1)}, bf16[512,128]{1,0:T(8,128)(2,1)S(1)}, u32[]{:S(2)}, u32[]{:S(2)}) collective-permute-start(bf16[512,128]{1,0:T(8,128)(2,1)S(1)} %get-tuple-element.21), channel_id=1, source_target_pairs={{0,2},{1,3},{2,0},{3,1},{4,6},{5,7},{6,4},{7,5},{8,10},{9,11},{10,... | collective-permute-start | bytes 393224 | tf_op jit(solution)/shard_map/ppermute | solution.py:62
  20.2 10.0 %collective-permute-start.13 = (bf16[528,128]{1,0:T(8,128)(2,1)S(1)}, bf16[528,128]{1,0:T(8,128)(2,1)S(1)}, u32[]{:S(2)}, u32[]{:S(2)}) collective-permute-start(bf16[528,128]{1,0:T(8,128)(2,1)S(1)} %get-tuple-element.15), channel_id=1, source_target_pairs={{0,3},{1,2},{2,1},{3,0},{4,7},{5,6},{6,5},{7,4},{8,11},{9,10},{10,... | collective-permute-start | bytes 405512 | tf_op jit(solution)/shard_map/ppermute | solution.py:62
  22.6 8.1 %collective-permute-start.12 = (bf16[528,128]{1,0:T(8,128)(2,1)S(1)}, bf16[528,128]{1,0:T(8,128)(2,1)S(1)}, u32[]{:S(2)}, u32[]{:S(2)}) collective-permute-start(bf16[528,128]{1,0:T(8,128)(2,1)S(1)} %get-tuple-element.16), channel_id=1, source_target_pairs={{0,2},{1,3},{2,0},{3,1},{4,6},{5,7},{6,4},{7,5},{8,10},{9,11},{10,... | collective-permute-start | bytes 405512 | tf_op jit(solution)/shard_map/ppermute | solution.py:62
  23.1 7.0 %collective-permute-start.8 = (bf16[512,128]{1,0:T(8,128)(2,1)S(1)}, bf16[512,128]{1,0:T(8,128)(2,1)S(1)}, u32[]{:S(2)}, u32[]{:S(2)}) collective-permute-start(bf16[512,128]{1,0:T(8,128)(2,1)S(1)} %get-tuple-element.22), channel_id=1, source_target_pairs={{0,1},{1,0},{2,3},{3,2},{4,5},{5,4},{6,7},{7,6},{8,9},{9,8},{10,11... | collective-permute-start | bytes 393224 | tf_op jit(solution)/shard_map/ppermute | solution.py:62
  24.4 7.3 %collective-permute-start.11 = (bf16[528,128]{1,0:T(8,128)(2,1)S(1)}, bf16[528,128]{1,0:T(8,128)(2,1)S(1)}, u32[]{:S(2)}, u32[]{:S(2)}) collective-permute-start(bf16[528,128]{1,0:T(8,128)(2,1)S(1)} %get-tuple-element.17), channel_id=1, source_target_pairs={{0,1},{1,0},{2,3},{3,2},{4,5},{5,4},{6,7},{7,6},{8,9},{9,8},{10,11... | collective-permute-start | bytes 405512 | tf_op jit(solution)/shard_map/ppermute | solution.py:62
  28.8 5.0 %collective-permute-start.7 = (bf16[1088,128]{1,0:T(8,128)(2,1)S(1)}, bf16[1088,128]{1,0:T(8,128)(2,1)S(1)}, u32[]{:S(2)}, u32[]{:S(2)}) collective-permute-start(bf16[1088,128]{1,0:T(8,128)(2,1)S(1)} %bitcast.35), channel_id=1, source_target_pairs={{0,4},{4,0},{8,12},{12,8},{16,20},{20,16},{24,28},{28,24},{1,5},{5... | collective-permute-start | bytes 835592 | tf_op jit(solution)/shard_map/ppermute | solution.py:66
  30.2 1.5 %collective-permute-start.16 = (bf16[512,128]{1,0:T(8,128)(2,1)S(1)}, bf16[512,128]{1,0:T(8,128)(2,1)S(1)}, u32[]{:S(2)}, u32[]{:S(2)}) collective-permute-start(bf16[512,128]{1,0:T(8,128)(2,1)S(1)} %collective-permute-done.10.rest_6_), channel_id=1, source_target_pairs={{0,4},{4,0},{8,12},{12,8},{16,20},{20,16},{24,28},{28,24},{1,5},{5... | collective-permute-start | bytes 393224 | tf_op jit(solution)/shard_map/ppermute | solution.py:66
  30.2 2.0 %collective-permute-start.15 = (bf16[512,128]{1,0:T(8,128)(2,1)S(1)}, bf16[512,128]{1,0:T(8,128)(2,1)S(1)}, u32[]{:S(2)}, u32[]{:S(2)}) collective-permute-start(bf16[512,128]{1,0:T(8,128)(2,1)S(1)} %collective-permute-done.9.rest_5_), channel_id=1, source_target_pairs={{0,4},{4,0},{8,12},{12,8},{16,20},{20,16},{24,28},{28,24},{1,5},{5... | collective-permute-start | bytes 393224 | tf_op jit(solution)/shard_map/ppermute | solution.py:66
  30.7 1.5 %collective-permute-start.14 = (bf16[512,128]{1,0:T(8,128)(2,1)S(1)}, bf16[512,128]{1,0:T(8,128)(2,1)S(1)}, u32[]{:S(2)}, u32[]{:S(2)}) collective-permute-start(bf16[512,128]{1,0:T(8,128)(2,1)S(1)} %collective-permute-done.8.rest_4_), channel_id=1, source_target_pairs={{0,4},{4,0},{8,12},{12,8},{16,20},{20,16},{24,28},{28,24},{1,5},{5... | collective-permute-start | bytes 393224 | tf_op jit(solution)/shard_map/ppermute | solution.py:66
  31.6 1.5 %collective-permute-start.6 = (bf16[1024,128]{1,0:T(8,128)(2,1)S(1)}, bf16[1024,128]{1,0:T(8,128)(2,1)S(1)}, u32[]{:S(2)}, u32[]{:S(2)}) collective-permute-start(bf16[1024,128]{1,0:T(8,128)(2,1)S(1)} %bitcast.37), channel_id=1, source_target_pairs={{0,4},{4,0},{8,12},{12,8},{16,20},{20,16},{24,28},{28,24},{1,5},{5... | collective-permute-start | bytes 786440 | tf_op jit(solution)/shard_map/ppermute | solution.py:66
  31.6 1.7 %collective-permute-start.19 = (bf16[528,128]{1,0:T(8,128)(2,1)S(1)}, bf16[528,128]{1,0:T(8,128)(2,1)S(1)}, u32[]{:S(2)}, u32[]{:S(2)}) collective-permute-start(bf16[528,128]{1,0:T(8,128)(2,1)S(1)} %collective-permute-done.13.rest_9_), channel_id=1, source_target_pairs={{0,4},{4,0},{8,12},{12,8},{16,20},{20,16},{24,28},{28,24},{1,5},{5... | collective-permute-start | bytes 405512 | tf_op jit(solution)/shard_map/ppermute | solution.py:66
  32.2 1.4 %collective-permute-start.18 = (bf16[528,128]{1,0:T(8,128)(2,1)S(1)}, bf16[528,128]{1,0:T(8,128)(2,1)S(1)}, u32[]{:S(2)}, u32[]{:S(2)}) collective-permute-start(bf16[528,128]{1,0:T(8,128)(2,1)S(1)} %collective-permute-done.12.rest_8_), channel_id=1, source_target_pairs={{0,4},{4,0},{8,12},{12,8},{16,20},{20,16},{24,28},{28,24},{1,5},{5... | collective-permute-start | bytes 405512 | tf_op jit(solution)/shard_map/ppermute | solution.py:66
  32.2 1.5 %collective-permute-start.17 = (bf16[528,128]{1,0:T(8,128)(2,1)S(1)}, bf16[528,128]{1,0:T(8,128)(2,1)S(1)}, u32[]{:S(2)}, u32[]{:S(2)}) collective-permute-start(bf16[528,128]{1,0:T(8,128)(2,1)S(1)} %collective-permute-done.11.rest_7_), channel_id=1, source_target_pairs={{0,4},{4,0},{8,12},{12,8},{16,20},{20,16},{24,28},{28,24},{1,5},{5... | collective-permute-start | bytes 405512 | tf_op jit(solution)/shard_map/ppermute | solution.py:66

commit v5 on v4

--- a/solution.py
+++ b/solution.py
@@ -50,7 +50,6 @@
     return updated
 
 
-NEXT = (0, 2, 3, 1)
 TILE = 16
 
 
@@ -58,8 +57,8 @@
     return lax.ppermute(array, "row", [(r, (r + 2 * step) % bands) for r in range(bands)])
 
 
-def across(array, flip):
-    return lax.ppermute(array, "col", [(c, c ^ flip) for c in range(4)])
+def exchange(array):
+    return lax.all_to_all(array, "col", 0, 0, tiled=False)
 
 
 def sibling(array, bands):
@@ -67,12 +66,26 @@
 
 
 def next_flip(flip):
-    return jnp.where(flip == 3, 1, flip + 1)
+    return jnp.where(flip == 3, 1, jnp.where(flip == 0, 0, flip + 1))
+
+
+def make_payloads(place, columns, values, first, second):
+    size = values.shape[2]
+    lane = lax.broadcasted_iota(jnp.int32, (TILE, size), 1)
+    line = lax.broadcasted_iota(jnp.int32, (TILE, size), 0)
+    tile = jnp.zeros((TILE, size), jnp.int32)
+    for m in range(4):
+        here = (lane == place[0] + m) & (line == 0)
+        tile = jnp.where(here, columns[m // 2, m % 2], tile)
+    for t in range(2):
+        first[t * size : (t + 1) * size, :] = values[0, t]
+        second[t * size : (t + 1) * size, :] = values[1, t]
+    first[2 * size :, :] = tile.astype(jnp.float32).astype(jnp.bfloat16)
 
 
 def local_iteration(origin, *rest):
-    lines, planes = rest[:4], rest[4:16]
-    out, xs, ys, qs, numbers, pattern, x_table, y_table, near, sem = rest[16:]
+    lines, planes = rest[:4], rest[4:8]
+    out, xs, ys, qs, numbers, pattern, x_table, y_table, near, sem = rest[8:]
     rows, kept, slots, size = 16, 8, 2, 128
     band, c = origin[0], origin[1]
     z, core = lax.div(band, 2), lax.rem(band, 2)
@@ -80,20 +93,28 @@
 
     pieces = []
     total = jnp.zeros((TILE, size), jnp.float32)
+
+    def add_tile(source, first):
+        rows_at = pl.ds(pl.multiple_of(first, TILE), TILE)
+        return total + source[rows_at, :].astype(jnp.float32)
+
     for a in range(2):
-        long = half + a * TILE
-        for source, side in ((lines[a], core), (lines[2 + a], 1 - core)):
+        tail = 0 if a else TILE
+        for group, side in ((0, core), (2, 1 - core)):
+            source = lines[group + a]
             for step in range(4):
-                pieces.append((source, step * long, step * 8 + side * 4 + a * 2))
-                if a == 1:
-                    total += source[step * long + half : step * long + long, :].astype(jnp.float32)
-        for group, side in ((planes[a * 3 : a * 3 + 3], core), (planes[6 + a * 3 : 9 + a * 3], 1 - core)):
-            for flip in range(3):
+                first = step * (half + tail)
+                pieces.append((source, first, step * 8 + side * 4 + a * 2))
+                if tail:
+                    total = add_tile(source, first + half)
+            source = planes[group + a]
+            for flip in range(1, 4):
+                first = (c ^ flip) * (2 * half + tail)
                 for part in range(2):
-                    place = (4 + flip * 2 + part) * 8 + side * 4 + a * 2
-                    pieces.append((group[flip], part * half, place))
-                if a == 1:
-                    total += group[flip][2 * half : 2 * half + TILE, :].astype(jnp.float32)
+                    place = (2 + flip * 2 + part) * 8 + side * 4 + a * 2
+                    pieces.append((source, first + part * half, place))
+                if tail:
+                    total = add_tile(source, first + 2 * half)
     numbers[...] = total[0:8].astype(jnp.int32)
     copy = pltpu.make_async_copy(numbers, pattern, sem)
     copy.start()
@@ -113,7 +134,7 @@
 
     for source, first, place in pieces:
         for b in range(slots):
-            xs[place + b] = source[first + b * size : first + (b + 1) * size, :]
+            xs[place + b] = source[pl.ds(pl.multiple_of(first + b * size, TILE), size), :]
     for number, piece in enumerate((0, 1, 2, 3, 5, 7, 9)):
         for b in range(8):
             xs[80 + number * 8 + b] = xs[piece * 8 + b].T
@@ -221,15 +242,21 @@
     size = values.shape[2]
     band, c = lax.axis_index("row"), lax.axis_index("col")
     z = band // 2
-    lane = lax.broadcasted_iota(jnp.int32, (TILE, size), 1)
-    line_number = lax.broadcasted_iota(jnp.int32, (TILE, size), 0)
-    first = (band * 4 + c) * 4
-    tile = jnp.zeros((TILE, size), jnp.int32)
-    for m in range(4):
-        here = (lane == first + m) & (line_number == 0)
-        tile = jnp.where(here, columns[m // 2, m % 2], tile)
-    halves = values.reshape(2, 2 * size, size)
-    mine = (halves[0], jnp.concatenate([halves[1], tile.astype(jnp.bfloat16)]))
+    origin = jnp.stack([band, c]).astype(jnp.int32)
+    place = ((band * 4 + c) * 4).reshape(1).astype(jnp.int32)
+    mine = pl.pallas_call(
+        make_payloads,
+        out_shape=[
+            jax.ShapeDtypeStruct((2 * size + TILE, size), jnp.bfloat16),
+            jax.ShapeDtypeStruct((2 * size, size), jnp.bfloat16),
+        ],
+        in_specs=[
+            pl.BlockSpec(memory_space=pltpu.SMEM),
+            pl.BlockSpec(memory_space=pltpu.SMEM),
+            pl.BlockSpec(memory_space=pltpu.VMEM),
+        ],
+        out_specs=[pl.BlockSpec(memory_space=pltpu.VMEM)] * 2,
+    )(place, columns, values)
 
     def from_line(line, h):
         return lax.dynamic_index_in_dim(line, (z - h) % 4, axis=0, keepdims=False)
@@ -237,21 +264,22 @@
     lines = [
         jnp.stack([half] + [around(half, step, bands) for step in range(1, 4)]) for half in mine
     ]
-    here, lines_there = [], []
+    here = []
     for a, line in enumerate(lines):
-        tail = [jnp.sum(line[:, 2 * size :], axis=0)] if a else []
-        for flip in range(1, 4):
-            parts = [from_line(line, h)[: 2 * size] for h in (c, c ^ NEXT[flip])]
-            here.append(across(jnp.concatenate(parts + tail), flip))
-        lines_there.append(sibling(line.reshape(-1, size), bands))
+        tail = [] if a else [jnp.sum(line[:, 2 * size :], axis=0)]
+        parts = []
+        for to in range(4):
+            picks = [from_line(line, h)[: 2 * size] for h in (c, c ^ next_flip(c ^ to))]
+            parts.append(jnp.concatenate(picks + tail))
+        here.append(exchange(jnp.stack(parts)).reshape(-1, size))
+    lines = [line.reshape(-1, size) for line in lines]
+    lines_there = [sibling(line, bands) for line in lines]
     there = [sibling(piece, bands) for piece in here]
-    lines = [line.reshape(-1, size) for line in lines]
-    origin = jnp.stack([band, c]).astype(jnp.int32)
     return pl.pallas_call(
         local_iteration,
         out_shape=jax.ShapeDtypeStruct(values.shape, jnp.float32),
         in_specs=[pl.BlockSpec(memory_space=pltpu.SMEM)]
-        + [pl.BlockSpec(memory_space=pltpu.VMEM)] * 16,
+        + [pl.BlockSpec(memory_space=pltpu.VMEM)] * 8,
         out_specs=pl.BlockSpec(memory_space=pltpu.VMEM),
         scratch_shapes=[
             pltpu.VMEM((17 * 8 + 1, size, size), jnp.bfloat16),

time: 47.8 us -> 54.8 us (1.15)
  waiting for transfers between devices: 6.84 us -> 18.3 us
  starting transfers between devices: 21.6 us -> 17.8 us
  Pallas kernels: 13.8 us -> 15.4 us
  local copies, waits for them, and re-layouts: 2.28 us -> 0.94 us
  other arithmetic: 2.94 us -> 2.01 us
    all_to_all x0 -> x2, waiting for transfers between devices: none -> 14.1 us  [exchange(): return lax.all_to_all(array, 'col', 0, 0, tiled=False)]
    ppermute x6 -> x0, starting transfers between devices: 8.09 us -> none  [across(): return lax.ppermute(array, 'col', [(c, c ^ flip) for c in range(4)])]
    all_to_all x0 -> x2, starting transfers between devices: none -> 7.19 us  [exchange(): return lax.all_to_all(array, 'col', 0, 0, tiled=False)]
    ppermute x6 -> x0, waiting for transfers between devices: 5.81 us -> none  [across(): return lax.ppermute(array, 'col', [(c, c ^ flip) for c in range(4)])]
    convert_element_type x1 -> x0, other arithmetic: 2.69 us -> none  [per_device_whole(): mine = (halves[0], jnp.concatenate([halves[1], tile.astype(jnp.bfloat16)]))]
    ppermute x6, waiting for transfers between devices: 0.02 us -> 2.08 us  [around(): lax.ppermute(array, 'row', [(r, (r + 2 * step) % bands) for r in range(ba...]
    ppermute x6, starting transfers between devices: 11.9 us -> 10 us  [around(): lax.ppermute(array, 'row', [(r, (r + 2 * step) % bands) for r in range(ba...]
    another operation x0 -> x4, other arithmetic: none -> 1.86 us  [per_device_whole(): here.append(exchange(jnp.stack(parts)).reshape(-1, size))]
  transfers between devices with their start and end apart: 20 -> 12, of which waited for: 8 -> 4; matrix products, arithmetic and copies ran while one was open for 8% -> 4% of each run, Pallas kernels for 0% -> 0%
where the time goes in v5:
time: 54.8 us; the launch traced here: 54.6 us
  waiting for transfers between devices  18.3 us (33%)
  starting transfers between devices  17.8 us (32%)
  Pallas kernels  15.4 us (28%)
  other arithmetic  2.01 us (4%)
  local copies, waits for them, and re-layouts  0.94 us (2%)
    all_to_all x2, waiting for transfers between devices, exchange(): return lax.all_to_all(array, 'col', 0, 0, tiled=False)  14.1 us
    pallas_call x1, Pallas kernels, per_device_whole(): pl.pallas_call(local_iteration, out_shape=jax.ShapeDtypeStruct(values.sha...  13.9 us
    ppermute x6, starting transfers between devices, around(): lax.ppermute(array, 'row', [(r, (r + 2 * step) % bands) for r in range(ba...  10 us
    all_to_all x2, starting transfers between devices, exchange(): return lax.all_to_all(array, 'col', 0, 0, tiled=False)  7.19 us
    ppermute x4, waiting for transfers between devices, sibling(): return lax.ppermute(array, 'row', [(r, r ^ 1) for r in range(bands)])  2.1 us
    ppermute x6, waiting for transfers between devices, around(): lax.ppermute(array, 'row', [(r, (r + 2 * step) % bands) for r in range(ba...  2.08 us
    another operation x4, other arithmetic, per_device_whole(): here.append(exchange(jnp.stack(parts)).reshape(-1, size))  1.86 us
    pallas_call x1, Pallas kernels, per_device_whole(): pl.pallas_call(make_payloads, out_shape=[jax.ShapeDtypeStruct((2 * size +...  1.57 us
  transfers between devices with their start and end apart: 12, of which 4 were waited for; matrix products, arithmetic and copies ran while one was open for 4% of the time, Pallas kernels for 0%

profile of v5, /device:TPU:0, one launch (start us, length us, event | category | flops | bytes accessed | tf_op | source)
XLA Modules:
  0.0 54.6 jit_solution(6238485198827323223)
XLA Ops:
  0.0 1.6 %shard_map.28 = (bf16[272,128]{1,0:T(8,128)(2,1)}, bf16[256,128]{1,0:T(8,128)(2,1)}) custom-call(s32[1]{0:T(128)} %bitcast.2.place, s32[2,2]{1,0:T(2,128)} %columns.1, bf16[2,2,128,128]{3,2,1,0:T(8,128)(2,1)} %values.1), custom_call_target="tpu_custom_call" | custom-call | tf_op jit(solution)/shard_map/pallas_call | solution.py:247
  1.6 5.0 %collective-permute-start.2 = (bf16[272,128]{1,0:T(8,128)(2,1)}, bf16[272,128]{1,0:T(8,128)(2,1)S(1)}, u32[]{:S(2)}, u32[]{:S(2)}) collective-permute-start(bf16[272,128]{1,0:T(8,128)(2,1)} %get-tuple-element.7), channel_id=1, source_target_pairs={{0,24},{4,28},{8,0},{12,4},{16,8},{20,12},{24,16},{28,20},{1,25},{... | collective-permute-start | bytes 208904 | tf_op jit(solution)/shard_map/ppermute | solution.py:57
  6.6 0.0 collective-permute-start.1
  6.6 1.0 %collective-permute-start = (bf16[272,128]{1,0:T(8,128)(2,1)}, bf16[272,128]{1,0:T(8,128)(2,1)S(1)}, u32[]{:S(2)}, u32[]{:S(2)}) collective-permute-start(bf16[272,128]{1,0:T(8,128)(2,1)} %get-tuple-element.7), channel_id=1, source_target_pairs={{0,8},{4,12},{8,16},{12,20},{16,24},{20,28},{24,0},{28,4},{1,9},{5... | collective-permute-start | bytes 208904 | tf_op jit(solution)/shard_map/ppermute | solution.py:57
  7.6 2.8 %collective-permute-start.5 = (bf16[256,128]{1,0:T(8,128)(2,1)}, bf16[256,128]{1,0:T(8,128)(2,1)S(1)}, u32[]{:S(2)}, u32[]{:S(2)}) collective-permute-start(bf16[256,128]{1,0:T(8,128)(2,1)} %get-tuple-element.8), channel_id=1, source_target_pairs={{0,24},{4,28},{8,0},{12,4},{16,8},{20,12},{24,16},{28,20},{1,25},{... | collective-permute-start | bytes 196616 | tf_op jit(solution)/shard_map/ppermute | solution.py:57
  10.5 1.1 %collective-permute-start.4 = (bf16[256,128]{1,0:T(8,128)(2,1)}, bf16[256,128]{1,0:T(8,128)(2,1)S(1)}, u32[]{:S(2)}, u32[]{:S(2)}) collective-permute-start(bf16[256,128]{1,0:T(8,128)(2,1)} %get-tuple-element.8), channel_id=1, source_target_pairs={{0,16},{4,20},{8,24},{12,28},{16,0},{20,4},{24,8},{28,12},{1,17},{... | collective-permute-start | bytes 196616 | tf_op jit(solution)/shard_map/ppermute | solution.py:57
  11.6 0.0 collective-permute-done.2
  11.6 0.9 %copy-done.1 = bf16[256,128]{1,0:T(8,128)(2,1)S(1)} copy-done((bf16[256,128]{1,0:T(8,128)(2,1)S(1)}, bf16[256,128]{1,0:T(8,128)(2,1)}, u32[]{:S(2)}) %copy-start.1) | copy-done | bytes 65560
  12.5 0.0 collective-permute-start.3
  12.5 2.1 %collective-permute-done.1 = bf16[272,128]{1,0:T(8,128)(2,1)S(1)} collective-permute-done((bf16[272,128]{1,0:T(8,128)(2,1)}, bf16[272,128]{1,0:T(8,128)(2,1)S(1)}, u32[]{:S(2)}, u32[]{:S(2)}) %collective-permute-start.1) | collective-permute-done | bytes 69664 | tf_op jit(solution)/shard_map/ppermute | solution.py:57
  14.5 0.0 collective-permute-done
  14.6 0.1 fusion
  14.7 0.9 %pad_maximum_fusion = bf16[4,528,128]{2,1,0:T(8,128)(2,1)} fusion(bf16[1,528,128]{2,1,0:T(8,128)(2,1)S(1)} %get-tuple-element.22, bf16[1,528,128]{2,1,0:T(8,128)(2,1)S(1)} %get-tuple-element.21, bf16[1,528,128]{2,1,0:T(8,128)(2,1)S(1)} %get-tuple-element.20, bf16[1,528,128]{2,1,0:T(8,128)(2,1)S(1)} %get-tuple-element.19), kind=kLoop, calls=%fused_computation | loop fusion | flops 811008 | bytes 1081344 | tf_op jit(solution)/shard_map/stack | solution.py:274
  15.6 3.7 %all-to-all-start = ((bf16[4,528,128]{2,1,0:T(8,128)(2,1)}), bf16[4,528,128]{2,1,0:T(8,128)(2,1)S(1)}, u32[]{:S(2)}, u32[]{:S(2)}) async-start(bf16[4,528,128]{2,1,0:T(8,128)(2,1)} %pad_maximum_fusion), calls=%async_computation | async-start | bytes 1081344 | tf_op jit(solution)/shard_map/all_to_all | solution.py:61
  19.3 0.0 collective-permute-done.5
  19.3 0.0 collective-permute-done.4
  19.3 0.0 collective-permute-done.3
  19.4 0.1 fusion.4
  19.5 0.9 %pad_maximum_fusion.1 = bf16[4,512,128]{2,1,0:T(8,128)(2,1)} fusion(bf16[1,512,128]{2,1,0:T(8,128)(2,1)S(1)} %get-tuple-element.26, bf16[1,512,128]{2,1,0:T(8,128)(2,1)S(1)} %get-tuple-element.25, bf16[1,512,128]{2,1,0:T(8,128)(2,1)S(1)} %get-tuple-element.24, bf16[1,512,128]{2,1,0:T(8,128)(2,1)S(1)} %get-tuple-element.23), kind=kLoop, calls=%fused_computation.1 | loop fusion | flops 786432 | bytes 1048576 | tf_op jit(solution)/shard_map/stack | solution.py:274
  20.3 7.1 %all-to-all-done = bf16[4,528,128]{2,1,0:T(8,128)(2,1)S(1)} async-done(((bf16[4,528,128]{2,1,0:T(8,128)(2,1)}), bf16[4,528,128]{2,1,0:T(8,128)(2,1)S(1)}, u32[]{:S(2)}, u32[]{:S(2)}) %all-to-all-start) | async-done | bytes 540704 | tf_op jit(solution)/shard_map/all_to_all | solution.py:61
  27.5 3.5 %all-to-all-start.1 = ((bf16[4,512,128]{2,1,0:T(8,128)(2,1)}), bf16[4,512,128]{2,1,0:T(8,128)(2,1)S(1)}, u32[]{:S(2)}, u32[]{:S(2)}) async-start(bf16[4,512,128]{2,1,0:T(8,128)(2,1)} %pad_maximum_fusion.1), calls=%async_computation.1 | async-start | bytes 1048576 | tf_op jit(solution)/shard_map/all_to_all | solution.py:61
  30.9 0.1 collective-permute-start.8
  31.0 7.0 %all-to-all-done.1 = bf16[4,512,128]{2,1,0:T(8,128)(2,1)S(1)} async-done(((bf16[4,512,128]{2,1,0:T(8,128)(2,1)}), bf16[4,512,128]{2,1,0:T(8,128)(2,1)S(1)}, u32[]{:S(2)}, u32[]{:S(2)}) %all-to-all-start.1) | async-done | bytes 524320 | tf_op jit(solution)/shard_map/all_to_all | solution.py:61
  38.0 0.0 collective-permute-start.9
  38.0 0.5 collective-permute-start.6
  38.5 0.0 collective-permute-start.7
  38.5 0.1 pad_add_fusion.origin
  38.6 2.1 %collective-permute-done.7.rest_3_ = bf16[1024,128]{1,0:T(8,128)(2,1)S(1)} collective-permute-done((bf16[1024,128]{1,0:T(8,128)(2,1)S(1)}, bf16[1024,128]{1,0:T(8,128)(2,1)S(1)}, u32[]{:S(2)}, u32[]{:S(2)}) %collective-permute-start.7) | collective-permute-done | bytes 262176 | tf_op jit(solution)/shard_map/ppermute | solution.py:65
  40.7 0.0 collective-permute-done.6.rest_2_
  40.7 0.0 collective-permute-done.9.rest_7_
  40.7 0.0 collective-permute-done.8.rest_6_
  40.7 13.9 %shard_map.29 = f32[2,2,128,128]{3,2,1,0:T(8,128)} custom-call(s32[2]{0:T(128)S(1)} %pad_add_fusion.origin, bf16[1088,128]{1,0:T(8,128)(2,1)S(1)} %bitcast.52, bf16[1024,128]{1,0:T(8,128)(2,1)S(1)} %bitcast.54, bf16[1088,128]{1,0:T(8,128)(2,1)S(1)} %collective-permute-done.6.rest_2_, bf16[1024,128]{1,0:T(8,128)(2,1)S(1)} %collective-permute-done.7.rest_3_, ...), custom_call_target="tpu_custom_call" | custom-call | tf_op jit(solution)/shard_map/pallas_call | solution.py:278
  (8 shorter events, 0.2 us)
Async XLA Ops:
  1.6 10.0 %collective-permute-start.2 = (bf16[272,128]{1,0:T(8,128)(2,1)}, bf16[272,128]{1,0:T(8,128)(2,1)S(1)}, u32[]{:S(2)}, u32[]{:S(2)}) collective-permute-start(bf16[272,128]{1,0:T(8,128)(2,1)} %get-tuple-element.7), channel_id=1, source_target_pairs={{0,24},{4,28},{8,0},{12,4},{16,8},{20,12},{24,16},{28,20},{1,25},{... | collective-permute-start | bytes 208904 | tf_op jit(solution)/shard_map/ppermute | solution.py:57
  6.6 7.9 %collective-permute-start.1 = (bf16[272,128]{1,0:T(8,128)(2,1)}, bf16[272,128]{1,0:T(8,128)(2,1)S(1)}, u32[]{:S(2)}, u32[]{:S(2)}) collective-permute-start(bf16[272,128]{1,0:T(8,128)(2,1)} %get-tuple-element.7), channel_id=1, source_target_pairs={{0,16},{4,20},{8,24},{12,28},{16,0},{20,4},{24,8},{28,12},{1,17},{... | collective-permute-start | bytes 208904 | tf_op jit(solution)/shard_map/ppermute | solution.py:57
  6.6 7.9 %collective-permute-start = (bf16[272,128]{1,0:T(8,128)(2,1)}, bf16[272,128]{1,0:T(8,128)(2,1)S(1)}, u32[]{:S(2)}, u32[]{:S(2)}) collective-permute-start(bf16[272,128]{1,0:T(8,128)(2,1)} %get-tuple-element.7), channel_id=1, source_target_pairs={{0,8},{4,12},{8,16},{12,20},{16,24},{20,28},{24,0},{28,4},{1,9},{5... | collective-permute-start | bytes 208904 | tf_op jit(solution)/shard_map/ppermute | solution.py:57
  7.6 11.7 %collective-permute-start.5 = (bf16[256,128]{1,0:T(8,128)(2,1)}, bf16[256,128]{1,0:T(8,128)(2,1)S(1)}, u32[]{:S(2)}, u32[]{:S(2)}) collective-permute-start(bf16[256,128]{1,0:T(8,128)(2,1)} %get-tuple-element.8), channel_id=1, source_target_pairs={{0,24},{4,28},{8,0},{12,4},{16,8},{20,12},{24,16},{28,20},{1,25},{... | collective-permute-start | bytes 196616 | tf_op jit(solution)/shard_map/ppermute | solution.py:57
  10.5 8.8 %collective-permute-start.4 = (bf16[256,128]{1,0:T(8,128)(2,1)}, bf16[256,128]{1,0:T(8,128)(2,1)S(1)}, u32[]{:S(2)}, u32[]{:S(2)}) collective-permute-start(bf16[256,128]{1,0:T(8,128)(2,1)} %get-tuple-element.8), channel_id=1, source_target_pairs={{0,16},{4,20},{8,24},{12,28},{16,0},{20,4},{24,8},{28,12},{1,17},{... | collective-permute-start | bytes 196616 | tf_op jit(solution)/shard_map/ppermute | solution.py:57
  11.6 0.9 %copy-start.1 = (bf16[256,128]{1,0:T(8,128)(2,1)S(1)}, bf16[256,128]{1,0:T(8,128)(2,1)}, u32[]{:S(2)}) copy-start(bf16[256,128]{1,0:T(8,128)(2,1)} %get-tuple-element.8) | copy-start | bytes 196612
  11.6 3.0 %copy-start = (bf16[272,128]{1,0:T(8,128)(2,1)S(1)}, bf16[272,128]{1,0:T(8,128)(2,1)}, u32[]{:S(2)}) copy-start(bf16[272,128]{1,0:T(8,128)(2,1)} %get-tuple-element.7) | copy-start | bytes 208900
  12.5 6.9 %collective-permute-start.3 = (bf16[256,128]{1,0:T(8,128)(2,1)S(1)}, bf16[256,128]{1,0:T(8,128)(2,1)S(1)}, u32[]{:S(2)}, u32[]{:S(2)}) collective-permute-start(bf16[256,128]{1,0:T(8,128)(2,1)S(1)} %copy-done.1), channel_id=1, source_target_pairs={{0,8},{4,12},{8,16},{12,20},{16,24},{20,28},{24,0},{28,4},{1,9},{5... | collective-permute-start | bytes 196616 | tf_op jit(solution)/shard_map/ppermute | solution.py:57
  15.6 11.9 %all-to-all-start = ((bf16[4,528,128]{2,1,0:T(8,128)(2,1)}), bf16[4,528,128]{2,1,0:T(8,128)(2,1)S(1)}, u32[]{:S(2)}, u32[]{:S(2)}) async-start(bf16[4,528,128]{2,1,0:T(8,128)(2,1)} %pad_maximum_fusion), calls=%async_computation | async-start | bytes 1081344 | tf_op jit(solution)/shard_map/all_to_all | solution.py:61
  27.5 10.5 %all-to-all-start.1 = ((bf16[4,512,128]{2,1,0:T(8,128)(2,1)}), bf16[4,512,128]{2,1,0:T(8,128)(2,1)S(1)}, u32[]{:S(2)}, u32[]{:S(2)}) async-start(bf16[4,512,128]{2,1,0:T(8,128)(2,1)} %pad_maximum_fusion.1), calls=%async_computation.1 | async-start | bytes 1048576 | tf_op jit(solution)/shard_map/all_to_all | solution.py:61
  30.9 9.8 %collective-permute-start.8 = (bf16[2112,128]{1,0:T(8,128)(2,1)S(1)}, bf16[2112,128]{1,0:T(8,128)(2,1)S(1)}, u32[]{:S(2)}, u32[]{:S(2)}) collective-permute-start(bf16[2112,128]{1,0:T(8,128)(2,1)S(1)} %bitcast.55), channel_id=1, source_target_pairs={{0,4},{4,0},{8,12},{12,8},{16,20},{20,16},{24,28},{28,24},{1,5},{5... | collective-permute-start | bytes 1622024 | tf_op jit(solution)/shard_map/ppermute | solution.py:65
  38.0 2.7 %collective-permute-start.9 = (bf16[2048,128]{1,0:T(8,128)(2,1)S(1)}, bf16[2048,128]{1,0:T(8,128)(2,1)S(1)}, u32[]{:S(2)}, u32[]{:S(2)}) collective-permute-start(bf16[2048,128]{1,0:T(8,128)(2,1)S(1)} %bitcast.57), channel_id=1, source_target_pairs={{0,4},{4,0},{8,12},{12,8},{16,20},{20,16},{24,28},{28,24},{1,5},{5... | collective-permute-start | bytes 1572872 | tf_op jit(solution)/shard_map/ppermute | solution.py:65
  38.0 2.7 %collective-permute-start.6 = (bf16[1088,128]{1,0:T(8,128)(2,1)S(1)}, bf16[1088,128]{1,0:T(8,128)(2,1)S(1)}, u32[]{:S(2)}, u32[]{:S(2)}) collective-permute-start(bf16[1088,128]{1,0:T(8,128)(2,1)S(1)} %bitcast.51), channel_id=1, source_target_pairs={{0,4},{4,0},{8,12},{12,8},{16,20},{20,16},{24,28},{28,24},{1,5},{5... | collective-permute-start | bytes 835592 | tf_op jit(solution)/shard_map/ppermute | solution.py:65
  38.5 2.2 %collective-permute-start.7 = (bf16[1024,128]{1,0:T(8,128)(2,1)S(1)}, bf16[1024,128]{1,0:T(8,128)(2,1)S(1)}, u32[]{:S(2)}, u32[]{:S(2)}) collective-permute-start(bf16[1024,128]{1,0:T(8,128)(2,1)S(1)} %bitcast.53), channel_id=1, source_target_pairs={{0,4},{4,0},{8,12},{12,8},{16,20},{20,16},{24,28},{28,24},{1,5},{5... | collective-permute-start | bytes 786440 | tf_op jit(solution)/shard_map/ppermute | solution.py:65

commit v6 on v5

--- a/solution.py
+++ b/solution.py
@@ -57,8 +57,8 @@
     return lax.ppermute(array, "row", [(r, (r + 2 * step) % bands) for r in range(bands)])
 
 
-def exchange(array):
-    return lax.all_to_all(array, "col", 0, 0, tiled=False)
+def across(array, flip):
+    return lax.ppermute(array, "col", [(c, c ^ flip) for c in range(4)])
 
 
 def sibling(array, bands):
@@ -66,7 +66,7 @@
 
 
 def next_flip(flip):
-    return jnp.where(flip == 3, 1, jnp.where(flip == 0, 0, flip + 1))
+    return flip % 3 + 1
 
 
 def make_payloads(place, columns, values, first, second):
@@ -83,47 +83,56 @@
     first[2 * size :, :] = tile.astype(jnp.float32).astype(jnp.bfloat16)
 
 
-def local_iteration(origin, *rest):
-    lines, planes = rest[:4], rest[4:8]
-    out, xs, ys, qs, numbers, pattern, x_table, y_table, near, sem = rest[8:]
+def line_pieces(lines, core, a):
+    skip, long = (4 * (256 + TILE), 256) if a else (0, 256 + TILE)
+    for source, side in zip(lines, (core, 1 - core)):
+        for step in range(4):
+            yield source, skip + step * long, step * 8 + side * 4 + a * 2
+
+
+def plane_pieces(planes, core, a):
+    for source, side in zip(planes, (core, 1 - core)):
+        for flip in range(3):
+            for part in range(2):
+                place = (4 + flip * 2 + part) * 8 + side * 4 + a * 2
+                if a:
+                    yield source[flip], part * 256, place
+                else:
+                    yield source, flip * (512 + TILE) + part * 256, place
+
+
+def put(blocks, source, first, place, piece, mirrors):
+    size = blocks.shape[1]
+    for b in range(2):
+        block = source[first + b * size : first + (b + 1) * size, :]
+        blocks[place + b] = block
+        if piece in mirrors:
+            blocks[80 + mirrors.index(piece) * 8 + place - piece * 8 + b] = block.T
+
+
+MIRRORS = (0, 1, 2, 3, 5, 7, 9)
+
+
+def fold_first(origin, *rest):
+    lines, planes = rest[:2], rest[2:4]
+    blocks, x_table, y_table, near, numbers, pattern, sem = rest[4:]
     rows, kept, slots, size = 16, 8, 2, 128
     band, c = origin[0], origin[1]
     z, core = lax.div(band, 2), lax.rem(band, 2)
-    half = slots * size
-
-    pieces = []
+
     total = jnp.zeros((TILE, size), jnp.float32)
-
-    def add_tile(source, first):
-        rows_at = pl.ds(pl.multiple_of(first, TILE), TILE)
-        return total + source[rows_at, :].astype(jnp.float32)
-
-    for a in range(2):
-        tail = 0 if a else TILE
-        for group, side in ((0, core), (2, 1 - core)):
-            source = lines[group + a]
-            for step in range(4):
-                first = step * (half + tail)
-                pieces.append((source, first, step * 8 + side * 4 + a * 2))
-                if tail:
-                    total = add_tile(source, first + half)
-            source = planes[group + a]
-            for flip in range(1, 4):
-                first = (c ^ flip) * (2 * half + tail)
-                for part in range(2):
-                    place = (2 + flip * 2 + part) * 8 + side * 4 + a * 2
-                    pieces.append((source, first + part * half, place))
-                if tail:
-                    total = add_tile(source, first + 2 * half)
+    for source, first, _ in line_pieces(lines, core, 0):
+        total += source[first + 2 * size : first + 2 * size + TILE, :].astype(jnp.float32)
+    for source in planes:
+        for flip in range(3):
+            end = (flip + 1) * (4 * size + TILE)
+            total += source[end - TILE : end, :].astype(jnp.float32)
     numbers[...] = total[0:8].astype(jnp.int32)
     copy = pltpu.make_async_copy(numbers, pattern, sem)
     copy.start()
 
-    nothing = jnp.zeros((size, size), jnp.bfloat16)
     empty = 17 * 8
-    xs[empty] = nothing
-    ys[rows * kept] = nothing
-    qs[rows * slots] = nothing
+    blocks[empty] = jnp.zeros((size, size), jnp.bfloat16)
 
     def clear(at, carry):
         x_table[at] = empty
@@ -132,12 +141,11 @@
 
     lax.fori_loop(0, rows * rows, clear, 0, unroll=16)
 
-    for source, first, place in pieces:
-        for b in range(slots):
-            xs[place + b] = source[pl.ds(pl.multiple_of(first + b * size, TILE), size), :]
-    for number, piece in enumerate((0, 1, 2, 3, 5, 7, 9)):
-        for b in range(8):
-            xs[80 + number * 8 + b] = xs[piece * 8 + b].T
+    for a in range(2):
+        for number, item in enumerate(line_pieces(lines, core, a)):
+            put(blocks, *item, number % 4, MIRRORS)
+    for number, item in enumerate(plane_pieces(planes, core, 0)):
+        put(blocks, *item, 4 + number % 6, MIRRORS)
     copy.wait()
 
     def entries(h, g):
@@ -153,7 +161,7 @@
             if h == g:
                 base = jnp.where(flip == 0, own, (4 + (flip - 1) * 2) * 8)
             else:
-                straight = (flip == 0) | (((h ^ c) != 0) & (next_flip(flip) == (h ^ g)))
+                straight = (flip == 0) | (((h ^ c) != 0) & (lax.rem(flip, 3) + 1 == (h ^ g)))
                 base = jnp.where(flip == 0, own, (5 + (flip - 1) * 2) * 8)
                 mirror = 80 + jnp.where(flip == 0, own, (3 + flip) * 8)
             for i, j, number, slot in entries(h, g):
@@ -168,6 +176,20 @@
                     for i, j, number, slot in entries(h, g):
                         x_table[i * rows + j] = base + number
                         x_table[j * rows + i] = mirror + number
+
+
+def local_iteration(origin, x_table, y_table, near, blocks, *rest):
+    planes, (out, xs, ys, qs) = (rest[:3], rest[3:6]), rest[6:]
+    rows, kept, slots, size = 16, 8, 2, 128
+    band, c = origin[0], origin[1]
+    core = lax.rem(band, 2)
+    nothing = jnp.zeros((size, size), jnp.bfloat16)
+    ys[rows * kept] = nothing
+    qs[rows * slots] = nothing
+    for at in range(blocks.shape[0]):
+        xs[at] = blocks[at]
+    for number, item in enumerate(plane_pieces(planes, core, 1)):
+        put(xs, *item, 4 + number % 6, MIRRORS)
 
     def wide(parts):
         return jnp.concatenate(parts, axis=1)
@@ -261,39 +283,62 @@
     def from_line(line, h):
         return lax.dynamic_index_in_dim(line, (z - h) % 4, axis=0, keepdims=False)
 
-    lines = [
-        jnp.stack([half] + [around(half, step, bands) for step in range(1, 4)]) for half in mine
-    ]
-    here = []
-    for a, line in enumerate(lines):
-        tail = [] if a else [jnp.sum(line[:, 2 * size :], axis=0)]
-        parts = []
-        for to in range(4):
-            picks = [from_line(line, h)[: 2 * size] for h in (c, c ^ next_flip(c ^ to))]
-            parts.append(jnp.concatenate(picks + tail))
-        here.append(exchange(jnp.stack(parts)).reshape(-1, size))
-    lines = [line.reshape(-1, size) for line in lines]
-    lines_there = [sibling(line, bands) for line in lines]
-    there = [sibling(piece, bands) for piece in here]
+    def col_payloads(line):
+        line = line.reshape(4, -1, size)
+        tail = [jnp.sum(line[:, 2 * size :], axis=0)] if line.shape[1] > 2 * size else []
+        for flip in range(1, 4):
+            parts = [from_line(line, h)[: 2 * size] for h in (c, c ^ next_flip(flip))]
+            yield jnp.concatenate(parts + tail)
+
+    line = [around(mine[0], step, bands) for step in range(1, 4)]
+    later, line[2] = lax.optimization_barrier((mine[1], line[2]))
+    line = jnp.concatenate([mine[0]] + line)
+    later_line = [around(later, step, bands) for step in range(1, 4)]
+    later_line = jnp.concatenate([later] + later_line)
+    first = [across(payload, flip + 1) for flip, payload in enumerate(col_payloads(line))]
+    later_line, first[2] = lax.optimization_barrier((later_line, first[2]))
+    second = [across(payload, flip + 1) for flip, payload in enumerate(col_payloads(later_line))]
+    lines = jnp.concatenate([line, later_line])
+    lines_there = sibling(lines, bands)
+    first = jnp.concatenate(first)
+    first_there = sibling(first, bands)
+    smem, vmem = pl.BlockSpec(memory_space=pltpu.SMEM), pl.BlockSpec(memory_space=pltpu.VMEM)
+    limit = pltpu.CompilerParams(vmem_limit_bytes=32 * 1024 * 1024)
+    count = 17 * 8 + 1
+    blocks, *tables = pl.pallas_call(
+        fold_first,
+        out_shape=[
+            jax.ShapeDtypeStruct((count, size, size), jnp.bfloat16),
+            jax.ShapeDtypeStruct((256,), jnp.int32),
+            jax.ShapeDtypeStruct((256,), jnp.int32),
+            jax.ShapeDtypeStruct((128,), jnp.int32),
+        ],
+        in_specs=[smem] + [vmem] * 4,
+        out_specs=[vmem, smem, smem, smem],
+        scratch_shapes=[
+            pltpu.VMEM((8, size), jnp.int32),
+            pltpu.SMEM((8, size), jnp.int32),
+            pltpu.SemaphoreType.DMA,
+        ],
+        compiler_params=limit,
+        cost_estimate=pl.CostEstimate(
+            flops=100_000_000, bytes_accessed=8_000_000, transcendentals=0
+        ),
+    )(origin, lines, lines_there, first, first_there)
+    blocks, *second = lax.optimization_barrier((blocks, *second))
+    second_there = [sibling(piece, bands) for piece in second]
     return pl.pallas_call(
         local_iteration,
         out_shape=jax.ShapeDtypeStruct(values.shape, jnp.float32),
-        in_specs=[pl.BlockSpec(memory_space=pltpu.SMEM)]
-        + [pl.BlockSpec(memory_space=pltpu.VMEM)] * 8,
-        out_specs=pl.BlockSpec(memory_space=pltpu.VMEM),
+        in_specs=[smem] * 4 + [vmem] * 7,
+        out_specs=vmem,
         scratch_shapes=[
-            pltpu.VMEM((17 * 8 + 1, size, size), jnp.bfloat16),
+            pltpu.VMEM((count, size, size), jnp.bfloat16),
             pltpu.VMEM((129, size, size), jnp.bfloat16),
             pltpu.VMEM((33, size, size), jnp.bfloat16),
-            pltpu.VMEM((8, size), jnp.int32),
-            pltpu.SMEM((8, size), jnp.int32),
-            pltpu.SMEM((256,), jnp.int32),
-            pltpu.SMEM((256,), jnp.int32),
-            pltpu.SMEM((128,), jnp.int32),
-            pltpu.SemaphoreType.DMA,
-        ],
-        compiler_params=pltpu.CompilerParams(vmem_limit_bytes=32 * 1024 * 1024),
-    )(origin, *lines, *lines_there, *here, *there)
+        ],
+        compiler_params=limit,
+    )(origin, *tables, blocks, *second, *second_there)
 
 
 def per_device(values, columns):

time: 54.8 us -> 50.2 us (0.916)
  waiting for transfers between devices: 18.3 us -> 11.9 us
  Pallas kernels: 15.4 us -> 16.9 us
    all_to_all x2 -> x0, waiting for transfers between devices: 14.1 us -> none  [exchange(): return lax.all_to_all(array, 'col', 0, 0, tiled=False)]
    all_to_all x2 -> x0, starting transfers between devices: 7.19 us -> none  [exchange(): return lax.all_to_all(array, 'col', 0, 0, tiled=False)]
    ppermute x0 -> x6, starting transfers between devices: none -> 7.17 us  [across(): return lax.ppermute(array, 'col', [(c, c ^ flip) for c in range(4)])]
    ppermute x0 -> x6, waiting for transfers between devices: none -> 5.98 us  [across(): return lax.ppermute(array, 'col', [(c, c ^ flip) for c in range(4)])]
    pallas_call x0 -> x1, Pallas kernels: none -> 2.73 us  [per_device_whole(): pl.pallas_call(fold_first, out_shape=[jax.ShapeDtypeStruct((count, size,...]
    ppermute x6, waiting for transfers between devices: 2.08 us -> 4.54 us  [around(): lax.ppermute(array, 'row', [(r, (r + 2 * step) % bands) for r in range(ba...]
    another operation x6 -> x0, other arithmetic: 1.93 us -> none  [the longest x4 1.86 us: per_device_whole(): here.append(exchange(jnp.stack(parts)).reshape(-1, size))]
    concatenate x0 -> x4, other arithmetic: none -> 1.82 us  [the longest x1 0.9 us: per_device_whole(): line = jnp.concatenate([mine[0]] + line)]
  transfers between devices with their start and end apart: 12 -> 17, of which waited for: 4 -> 9; matrix products, arithmetic and copies ran while one was open for 4% -> 6% of each run, Pallas kernels for 0% -> 5%
where the time goes in v6:
time: 50.2 us; the launch traced here: 49.9 us
  starting transfers between devices  18 us (36%)
  Pallas kernels  16.9 us (34%)
  waiting for transfers between devices  11.9 us (24%)
  other arithmetic  1.91 us (4%)
  local copies, waits for them, and re-layouts  1.11 us (2%)
    pallas_call x1, Pallas kernels, per_device_whole(): pl.pallas_call(local_iteration, out_shape=jax.ShapeDtypeStruct(values.sha...  12.6 us
    ppermute x6, starting transfers between devices, around(): lax.ppermute(array, 'row', [(r, (r + 2 * step) % bands) for r in range(ba...  10.2 us
    ppermute x6, starting transfers between devices, across(): return lax.ppermute(array, 'col', [(c, c ^ flip) for c in range(4)])  7.17 us
    ppermute x6, waiting for transfers between devices, across(): return lax.ppermute(array, 'col', [(c, c ^ flip) for c in range(4)])  5.98 us
    ppermute x6, waiting for transfers between devices, around(): lax.ppermute(array, 'row', [(r, (r + 2 * step) % bands) for r in range(ba...  4.54 us
    pallas_call x1, Pallas kernels, per_device_whole(): pl.pallas_call(fold_first, out_shape=[jax.ShapeDtypeStruct((count, size,...  2.73 us
    pallas_call x1, Pallas kernels, per_device_whole(): pl.pallas_call(make_payloads, out_shape=[jax.ShapeDtypeStruct((2 * size +...  1.57 us
    ppermute x5, waiting for transfers between devices, sibling(): return lax.ppermute(array, 'row', [(r, r ^ 1) for r in range(bands)])  1.35 us
  transfers between devices with their start and end apart: 17, of which 9 were waited for; matrix products, arithmetic and copies ran while one was open for 6% of the time, Pallas kernels for 5%

profile of v6, /device:TPU:0, one launch (start us, length us, event | category | flops | bytes accessed | tf_op | source)
XLA Modules:
  0.0 49.9 jit_solution(13232243920242417777)
XLA Ops:
  0.0 1.6 %shard_map.28 = (bf16[272,128]{1,0:T(8,128)(2,1)}, bf16[256,128]{1,0:T(8,128)(2,1)}) custom-call(s32[1]{0:T(128)} %bitcast.2.place, s32[2,2]{1,0:T(2,128)} %columns.1, bf16[2,2,128,128]{3,2,1,0:T(8,128)(2,1)} %values.1), custom_call_target="tpu_custom_call" | custom-call | tf_op jit(solution)/shard_map/pallas_call | solution.py:269
  1.6 3.0 %collective-permute-start = (bf16[272,128]{1,0:T(8,128)(2,1)}, bf16[272,128]{1,0:T(8,128)(2,1)S(1)}, u32[]{:S(2)}, u32[]{:S(2)}) collective-permute-start(bf16[272,128]{1,0:T(8,128)(2,1)} %get-tuple-element.19), channel_id=1, source_target_pairs={{0,8},{4,12},{8,16},{12,20},{16,24},{20,28},{24,0},{28,4},{1,9},{5... | collective-permute-start | bytes 208904 | tf_op jit(solution)/shard_map/ppermute | solution.py:57
  4.6 2.6 %collective-permute-start.1 = (bf16[272,128]{1,0:T(8,128)(2,1)}, bf16[272,128]{1,0:T(8,128)(2,1)S(1)}, u32[]{:S(2)}, u32[]{:S(2)}) collective-permute-start(bf16[272,128]{1,0:T(8,128)(2,1)} %get-tuple-element.19), channel_id=1, source_target_pairs={{0,16},{4,20},{8,24},{12,28},{16,0},{20,4},{24,8},{28,12},{1,17},{... | collective-permute-start | bytes 208904 | tf_op jit(solution)/shard_map/ppermute | solution.py:57
  7.2 1.3 %collective-permute-start.2 = (bf16[272,128]{1,0:T(8,128)(2,1)}, bf16[272,128]{1,0:T(8,128)(2,1)S(1)}, u32[]{:S(2)}, u32[]{:S(2)}) collective-permute-start(bf16[272,128]{1,0:T(8,128)(2,1)} %get-tuple-element.19), channel_id=1, source_target_pairs={{0,24},{4,28},{8,0},{12,4},{16,8},{20,12},{24,16},{28,20},{1,25},{... | collective-permute-start | bytes 208904 | tf_op jit(solution)/shard_map/ppermute | solution.py:57
  8.5 0.9 %constant_dynamic-update-slice_fusion.4 = bf16[2112,128]{1,0:T(8,128)(2,1)S(1)} fusion(bf16[272,128]{1,0:T(8,128)(2,1)} %get-tuple-element.19), kind=kLoop, calls=%fused_computation.23 | loop fusion | bytes 139264
  9.5 2.8 %collective-permute-done.2 = bf16[272,128]{1,0:T(8,128)(2,1)S(1)} collective-permute-done((bf16[272,128]{1,0:T(8,128)(2,1)}, bf16[272,128]{1,0:T(8,128)(2,1)S(1)}, u32[]{:S(2)}, u32[]{:S(2)}) %collective-permute-start.2) | collective-permute-done | bytes 69664 | tf_op jit(solution)/shard_map/ppermute | solution.py:57
  12.3 2.6 %collective-permute-start.5 = (bf16[256,128]{1,0:T(8,128)(2,1)}, bf16[256,128]{1,0:T(8,128)(2,1)S(1)}, u32[]{:S(2)}, u32[]{:S(2)}) collective-permute-start(bf16[256,128]{1,0:T(8,128)(2,1)} %get-tuple-element.22), channel_id=1, source_target_pairs={{0,24},{4,28},{8,0},{12,4},{16,8},{20,12},{24,16},{28,20},{1,25},{... | collective-permute-start | bytes 196616 | tf_op jit(solution)/shard_map/ppermute | solution.py:57
  14.9 0.7 %collective-permute-start.4 = (bf16[256,128]{1,0:T(8,128)(2,1)}, bf16[256,128]{1,0:T(8,128)(2,1)S(1)}, u32[]{:S(2)}, u32[]{:S(2)}) collective-permute-start(bf16[256,128]{1,0:T(8,128)(2,1)} %get-tuple-element.22), channel_id=1, source_target_pairs={{0,16},{4,20},{8,24},{12,28},{16,0},{20,4},{24,8},{28,12},{1,17},{... | collective-permute-start | bytes 196616 | tf_op jit(solution)/shard_map/ppermute | solution.py:57
  15.5 0.0 collective-permute-start.3
  15.5 0.9 %pad_maximum_fusion = bf16[1088,128]{1,0:T(8,128)(2,1)S(1)} fusion(bf16[272,128]{1,0:T(8,128)(2,1)S(1)} %collective-permute-done.2, bf16[272,128]{1,0:T(8,128)(2,1)S(1)} %collective-permute-done.1, bf16[272,128]{1,0:T(8,128)(2,1)S(1)} %collective-permute-done, bf16[272,128]{1,0:T(8,128)(2,1)} %get-tuple-element.19), kind=kLoop, calls=%fused_computation | loop fusion | flops 1114112 | bytes 557056 | tf_op jit(solution)/shard_map/concatenate | solution.py:295
  16.5 2.5 %collective-permute-start.6 = (bf16[528,128]{1,0:T(8,128)(2,1)S(1)}, bf16[528,128]{1,0:T(8,128)(2,1)S(1)}, u32[]{:S(2)}, u32[]{:S(2)}) collective-permute-start(bf16[528,128]{1,0:T(8,128)(2,1)S(1)} %get-tuple-element.43), channel_id=1, source_target_pairs={{0,3},{1,2},{2,1},{3,0},{4,7},{5,6},{6,5},{7,4},{8,11},{9,10},{10,... | collective-permute-start | bytes 405512 | tf_op jit(solution)/shard_map/ppermute | solution.py:61
  19.1 0.6 %collective-permute-start.8 = (bf16[528,128]{1,0:T(8,128)(2,1)S(1)}, bf16[528,128]{1,0:T(8,128)(2,1)S(1)}, u32[]{:S(2)}, u32[]{:S(2)}) collective-permute-start(bf16[528,128]{1,0:T(8,128)(2,1)S(1)} %get-tuple-element.42), channel_id=1, source_target_pairs={{0,1},{1,0},{2,3},{3,2},{4,5},{5,4},{6,7},{7,6},{8,9},{9,8},{10,11... | collective-permute-start | bytes 405512 | tf_op jit(solution)/shard_map/ppermute | solution.py:61
  19.7 0.5 %collective-permute-start.9 = (bf16[528,128]{1,0:T(8,128)(2,1)S(1)}, bf16[528,128]{1,0:T(8,128)(2,1)S(1)}, u32[]{:S(2)}, u32[]{:S(2)}) collective-permute-start(bf16[528,128]{1,0:T(8,128)(2,1)S(1)} %get-tuple-element.41), channel_id=1, source_target_pairs={{0,2},{1,3},{2,0},{3,1},{4,6},{5,7},{6,4},{7,5},{8,10},{9,11},{10,... | collective-permute-start | bytes 405512 | tf_op jit(solution)/shard_map/ppermute | solution.py:61
  20.2 1.7 %collective-permute-done.4 = bf16[256,128]{1,0:T(8,128)(2,1)S(1)} collective-permute-done((bf16[256,128]{1,0:T(8,128)(2,1)}, bf16[256,128]{1,0:T(8,128)(2,1)S(1)}, u32[]{:S(2)}, u32[]{:S(2)}) %collective-permute-start.4) | collective-permute-done | bytes 65568 | tf_op jit(solution)/shard_map/ppermute | solution.py:57
  21.9 0.9 %pad_maximum_fusion.1 = bf16[1024,128]{1,0:T(8,128)(2,1)S(1)} fusion(bf16[256,128]{1,0:T(8,128)(2,1)S(1)} %collective-permute-done.5, bf16[256,128]{1,0:T(8,128)(2,1)S(1)} %collective-permute-done.4, bf16[256,128]{1,0:T(8,128)(2,1)S(1)} %collective-permute-done.3, bf16[256,128]{1,0:T(8,128)(2,1)} %get-tuple-element.22), kind=kLoop, calls=%fused_computation.1 | loop fusion | flops 1048576 | bytes 524288 | tf_op jit(solution)/shard_map/concatenate | solution.py:297
  22.8 1.1 %collective-permute-done.6 = bf16[528,128]{1,0:T(8,128)(2,1)S(1)} collective-permute-done((bf16[528,128]{1,0:T(8,128)(2,1)S(1)}, bf16[528,128]{1,0:T(8,128)(2,1)S(1)}, u32[]{:S(2)}, u32[]{:S(2)}) %collective-permute-start.6) | collective-permute-done | bytes 135200 | tf_op jit(solution)/shard_map/ppermute | solution.py:61
  23.9 0.1 collective-permute-start.7
  24.0 1.2 %collective-permute-done.8 = bf16[528,128]{1,0:T(8,128)(2,1)S(1)} collective-permute-done((bf16[528,128]{1,0:T(8,128)(2,1)S(1)}, bf16[528,128]{1,0:T(8,128)(2,1)S(1)}, u32[]{:S(2)}, u32[]{:S(2)}) %collective-permute-start.8) | collective-permute-done | bytes 135200 | tf_op jit(solution)/shard_map/ppermute | solution.py:61
  25.2 0.1 collective-permute-done.9
  25.4 0.1 collective-permute-start.10
  25.5 1.5 %collective-permute-start.11 = (bf16[512,128]{1,0:T(8,128)(2,1)S(1)}, bf16[512,128]{1,0:T(8,128)(2,1)S(1)}, u32[]{:S(2)}, u32[]{:S(2)}) collective-permute-start(bf16[512,128]{1,0:T(8,128)(2,1)S(1)} %get-tuple-element.46), channel_id=1, source_target_pairs={{0,1},{1,0},{2,3},{3,2},{4,5},{5,4},{6,7},{7,6},{8,9},{9,8},{10,11... | collective-permute-start | bytes 393224 | tf_op jit(solution)/shard_map/ppermute | solution.py:61
  27.1 1.3 %collective-permute-start.12 = (bf16[512,128]{1,0:T(8,128)(2,1)S(1)}, bf16[512,128]{1,0:T(8,128)(2,1)S(1)}, u32[]{:S(2)}, u32[]{:S(2)}) collective-permute-start(bf16[512,128]{1,0:T(8,128)(2,1)S(1)} %get-tuple-element.45), channel_id=1, source_target_pairs={{0,2},{1,3},{2,0},{3,1},{4,6},{5,7},{6,4},{7,5},{8,10},{9,11},{10,... | collective-permute-start | bytes 393224 | tf_op jit(solution)/shard_map/ppermute | solution.py:61
  28.4 0.7 %collective-permute-start.13 = (bf16[512,128]{1,0:T(8,128)(2,1)S(1)}, bf16[512,128]{1,0:T(8,128)(2,1)S(1)}, u32[]{:S(2)}, u32[]{:S(2)}) collective-permute-start(bf16[512,128]{1,0:T(8,128)(2,1)S(1)} %get-tuple-element.44), channel_id=1, source_target_pairs={{0,3},{1,2},{2,1},{3,0},{4,7},{5,6},{6,5},{7,4},{8,11},{9,10},{10,... | collective-permute-start | bytes 393224 | tf_op jit(solution)/shard_map/ppermute | solution.py:61
  29.1 0.1 pad_add_fusion.origin
  29.2 2.7 %shard_map.29 = (bf16[137,128,128]{2,1,0:T(8,128)(2,1)S(1)}, s32[256]{0:T(256)S(1)}, s32[256]{0:T(256)S(1)}, s32[128]{0:T(128)S(1)}) custom-call(s32[2]{0:T(128)S(1)} %pad_add_fusion.origin, bf16[2112,128]{1,0:T(8,128)(2,1)S(1)} %constant_dynamic-update-slice_fusion.rest_0_, bf16[2112,128]{1,0:T(8,128)(2,1)S(1)} %collective-permute-done.7.rest_1_, ...), custom_call_target="tpu_custom_call" | custom-call | flops 100000000 | bytes 8000000 | tf_op jit(solution)/shard_map/pallas_call | solution.py:308
  31.9 3.6 %collective-permute-done.12.rest_1_ = bf16[512,128]{1,0:T(8,128)(2,1)S(1)} collective-permute-done((bf16[512,128]{1,0:T(8,128)(2,1)S(1)}, bf16[512,128]{1,0:T(8,128)(2,1)S(1)}, u32[]{:S(2)}, u32[]{:S(2)}) %collective-permute-start.12) | collective-permute-done | bytes 131104 | tf_op jit(solution)/shard_map/ppermute | solution.py:61
  35.5 0.5 %collective-permute-start.15 = (bf16[512,128]{1,0:T(8,128)(2,1)S(1)}, bf16[512,128]{1,0:T(8,128)(2,1)S(1)}, u32[]{:S(2)}, u32[]{:S(2)}) collective-permute-start(bf16[512,128]{1,0:T(8,128)(2,1)S(1)} %collective-permute-done.12.rest_1_), channel_id=1, source_target_pairs={{0,4},{4,0},{8,12},{12,8},{16,20},{20,16},{24,28},{28,24},{1,5},{5... | collective-permute-start | bytes 393224 | tf_op jit(solution)/shard_map/ppermute | solution.py:65
  36.0 0.0 collective-permute-start.16
  36.0 0.8 %collective-permute-done.14.rest_3_ = bf16[512,128]{1,0:T(8,128)(2,1)S(1)} collective-permute-done((bf16[512,128]{1,0:T(8,128)(2,1)S(1)}, bf16[512,128]{1,0:T(8,128)(2,1)S(1)}, u32[]{:S(2)}, u32[]{:S(2)}) %collective-permute-start.14) | collective-permute-done | bytes 131104 | tf_op jit(solution)/shard_map/ppermute | solution.py:65
  36.8 0.2 collective-permute-done.15.rest_4_
  37.0 0.3 collective-permute-done.16.rest_5_
  37.3 12.6 %shard_map.30 = f32[2,2,128,128]{3,2,1,0:T(8,128)} custom-call(s32[2]{0:T(128)S(1)} %pad_add_fusion.origin, s32[256]{0:T(256)S(1)} %get-tuple-element.25.x_table, s32[256]{0:T(256)S(1)} %get-tuple-element.26.y_table, s32[128]{0:T(128)S(1)} %get-tuple-element.27.near, bf16[137,128,128]{2,1,0:T(8,128)(2,1)S(1)} %get-tuple-element.29.blocks, ...), custom_call_target="tpu_custom_call" | custom-call | tf_op jit(solution)/shard_map/pallas_call | solution.py:330
  (21 shorter events, 0.3 us)
Async XLA Ops:
  1.6 13.9 %collective-permute-start = (bf16[272,128]{1,0:T(8,128)(2,1)}, bf16[272,128]{1,0:T(8,128)(2,1)S(1)}, u32[]{:S(2)}, u32[]{:S(2)}) collective-permute-start(bf16[272,128]{1,0:T(8,128)(2,1)} %get-tuple-element.19), channel_id=1, source_target_pairs={{0,8},{4,12},{8,16},{12,20},{16,24},{20,28},{24,0},{28,4},{1,9},{5... | collective-permute-start | bytes 208904 | tf_op jit(solution)/shard_map/ppermute | solution.py:57
  4.6 10.9 %collective-permute-start.1 = (bf16[272,128]{1,0:T(8,128)(2,1)}, bf16[272,128]{1,0:T(8,128)(2,1)S(1)}, u32[]{:S(2)}, u32[]{:S(2)}) collective-permute-start(bf16[272,128]{1,0:T(8,128)(2,1)} %get-tuple-element.19), channel_id=1, source_target_pairs={{0,16},{4,20},{8,24},{12,28},{16,0},{20,4},{24,8},{28,12},{1,17},{... | collective-permute-start | bytes 208904 | tf_op jit(solution)/shard_map/ppermute | solution.py:57
  7.2 5.1 %collective-permute-start.2 = (bf16[272,128]{1,0:T(8,128)(2,1)}, bf16[272,128]{1,0:T(8,128)(2,1)S(1)}, u32[]{:S(2)}, u32[]{:S(2)}) collective-permute-start(bf16[272,128]{1,0:T(8,128)(2,1)} %get-tuple-element.19), channel_id=1, source_target_pairs={{0,24},{4,28},{8,0},{12,4},{16,8},{20,12},{24,16},{28,20},{1,25},{... | collective-permute-start | bytes 208904 | tf_op jit(solution)/shard_map/ppermute | solution.py:57
  12.3 7.4 %collective-permute-start.5 = (bf16[256,128]{1,0:T(8,128)(2,1)}, bf16[256,128]{1,0:T(8,128)(2,1)S(1)}, u32[]{:S(2)}, u32[]{:S(2)}) collective-permute-start(bf16[256,128]{1,0:T(8,128)(2,1)} %get-tuple-element.22), channel_id=1, source_target_pairs={{0,24},{4,28},{8,0},{12,4},{16,8},{20,12},{24,16},{28,20},{1,25},{... | collective-permute-start | bytes 196616 | tf_op jit(solution)/shard_map/ppermute | solution.py:57
  14.9 7.1 %collective-permute-start.4 = (bf16[256,128]{1,0:T(8,128)(2,1)}, bf16[256,128]{1,0:T(8,128)(2,1)S(1)}, u32[]{:S(2)}, u32[]{:S(2)}) collective-permute-start(bf16[256,128]{1,0:T(8,128)(2,1)} %get-tuple-element.22), channel_id=1, source_target_pairs={{0,16},{4,20},{8,24},{12,28},{16,0},{20,4},{24,8},{28,12},{1,17},{... | collective-permute-start | bytes 196616 | tf_op jit(solution)/shard_map/ppermute | solution.py:57
  15.5 6.4 %collective-permute-start.3 = (bf16[256,128]{1,0:T(8,128)(2,1)}, bf16[256,128]{1,0:T(8,128)(2,1)S(1)}, u32[]{:S(2)}, u32[]{:S(2)}) collective-permute-start(bf16[256,128]{1,0:T(8,128)(2,1)} %get-tuple-element.22), channel_id=1, source_target_pairs={{0,8},{4,12},{8,16},{12,20},{16,24},{20,28},{24,0},{28,4},{1,9},{5... | collective-permute-start | bytes 196616 | tf_op jit(solution)/shard_map/ppermute | solution.py:57
  16.5 7.4 %collective-permute-start.6 = (bf16[528,128]{1,0:T(8,128)(2,1)S(1)}, bf16[528,128]{1,0:T(8,128)(2,1)S(1)}, u32[]{:S(2)}, u32[]{:S(2)}) collective-permute-start(bf16[528,128]{1,0:T(8,128)(2,1)S(1)} %get-tuple-element.43), channel_id=1, source_target_pairs={{0,3},{1,2},{2,1},{3,0},{4,7},{5,6},{6,5},{7,4},{8,11},{9,10},{10,... | collective-permute-start | bytes 405512 | tf_op jit(solution)/shard_map/ppermute | solution.py:61
  19.1 6.1 %collective-permute-start.8 = (bf16[528,128]{1,0:T(8,128)(2,1)S(1)}, bf16[528,128]{1,0:T(8,128)(2,1)S(1)}, u32[]{:S(2)}, u32[]{:S(2)}) collective-permute-start(bf16[528,128]{1,0:T(8,128)(2,1)S(1)} %get-tuple-element.42), channel_id=1, source_target_pairs={{0,1},{1,0},{2,3},{3,2},{4,5},{5,4},{6,7},{7,6},{8,9},{9,8},{10,11... | collective-permute-start | bytes 405512 | tf_op jit(solution)/shard_map/ppermute | solution.py:61
  19.7 5.6 %collective-permute-start.9 = (bf16[528,128]{1,0:T(8,128)(2,1)S(1)}, bf16[528,128]{1,0:T(8,128)(2,1)S(1)}, u32[]{:S(2)}, u32[]{:S(2)}) collective-permute-start(bf16[528,128]{1,0:T(8,128)(2,1)S(1)} %get-tuple-element.41), channel_id=1, source_target_pairs={{0,2},{1,3},{2,0},{3,1},{4,6},{5,7},{6,4},{7,5},{8,10},{9,11},{10,... | collective-permute-start | bytes 405512 | tf_op jit(solution)/shard_map/ppermute | solution.py:61
  23.9 5.2 %collective-permute-start.7 = (bf16[2112,128]{1,0:T(8,128)(2,1)S(1)}, bf16[2112,128]{1,0:T(8,128)(2,1)S(1)}, u32[]{:S(2)}, u32[]{:S(2)}) collective-permute-start(bf16[2112,128]{1,0:T(8,128)(2,1)S(1)} %constant_dynamic-update-slice_fusion.rest_0_), channel_id=1, source_target_pairs={{0,4},{4,0},{8,12},{12,8},{16,20},{20,16},{24,28},{28,24},{1,5},{5... | collective-permute-start | bytes 1622024 | tf_op jit(solution)/shard_map/ppermute | solution.py:65
  25.4 3.8 %collective-permute-start.10 = (bf16[1584,128]{1,0:T(8,128)(2,1)S(1)}, bf16[1584,128]{1,0:T(8,128)(2,1)S(1)}, u32[]{:S(2)}, u32[]{:S(2)}) collective-permute-start(bf16[1584,128]{1,0:T(8,128)(2,1)S(1)} %constant_dynamic-update-slice_fusion.5.rest_2_), channel_id=1, source_target_pairs={{0,4},{4,0},{8,12},{12,8},{16,20},{20,16},{24,28},{28,24},{1,5},{5... | collective-permute-start | bytes 1216520 | tf_op jit(solution)/shard_map/ppermute | solution.py:65
  25.5 6.4 %collective-permute-start.11 = (bf16[512,128]{1,0:T(8,128)(2,1)S(1)}, bf16[512,128]{1,0:T(8,128)(2,1)S(1)}, u32[]{:S(2)}, u32[]{:S(2)}) collective-permute-start(bf16[512,128]{1,0:T(8,128)(2,1)S(1)} %get-tuple-element.46), channel_id=1, source_target_pairs={{0,1},{1,0},{2,3},{3,2},{4,5},{5,4},{6,7},{7,6},{8,9},{9,8},{10,11... | collective-permute-start | bytes 393224 | tf_op jit(solution)/shard_map/ppermute | solution.py:61
  27.1 8.4 %collective-permute-start.12 = (bf16[512,128]{1,0:T(8,128)(2,1)S(1)}, bf16[512,128]{1,0:T(8,128)(2,1)S(1)}, u32[]{:S(2)}, u32[]{:S(2)}) collective-permute-start(bf16[512,128]{1,0:T(8,128)(2,1)S(1)} %get-tuple-element.45), channel_id=1, source_target_pairs={{0,2},{1,3},{2,0},{3,1},{4,6},{5,7},{6,4},{7,5},{8,10},{9,11},{10,... | collective-permute-start | bytes 393224 | tf_op jit(solution)/shard_map/ppermute | solution.py:61
  28.4 7.1 %collective-permute-start.13 = (bf16[512,128]{1,0:T(8,128)(2,1)S(1)}, bf16[512,128]{1,0:T(8,128)(2,1)S(1)}, u32[]{:S(2)}, u32[]{:S(2)}) collective-permute-start(bf16[512,128]{1,0:T(8,128)(2,1)S(1)} %get-tuple-element.44), channel_id=1, source_target_pairs={{0,3},{1,2},{2,1},{3,0},{4,7},{5,6},{6,5},{7,4},{8,11},{9,10},{10,... | collective-permute-start | bytes 393224 | tf_op jit(solution)/shard_map/ppermute | solution.py:61
  35.5 1.3 %collective-permute-start.14 = (bf16[512,128]{1,0:T(8,128)(2,1)S(1)}, bf16[512,128]{1,0:T(8,128)(2,1)S(1)}, u32[]{:S(2)}, u32[]{:S(2)}) collective-permute-start(bf16[512,128]{1,0:T(8,128)(2,1)S(1)} %collective-permute-done.11.rest_0_), channel_id=1, source_target_pairs={{0,4},{4,0},{8,12},{12,8},{16,20},{20,16},{24,28},{28,24},{1,5},{5... | collective-permute-start | bytes 393224 | tf_op jit(solution)/shard_map/ppermute | solution.py:65
  35.5 1.5 %collective-permute-start.15 = (bf16[512,128]{1,0:T(8,128)(2,1)S(1)}, bf16[512,128]{1,0:T(8,128)(2,1)S(1)}, u32[]{:S(2)}, u32[]{:S(2)}) collective-permute-start(bf16[512,128]{1,0:T(8,128)(2,1)S(1)} %collective-permute-done.12.rest_1_), channel_id=1, source_target_pairs={{0,4},{4,0},{8,12},{12,8},{16,20},{20,16},{24,28},{28,24},{1,5},{5... | collective-permute-start | bytes 393224 | tf_op jit(solution)/shard_map/ppermute | solution.py:65
  36.0 1.3 %collective-permute-start.16 = (bf16[512,128]{1,0:T(8,128)(2,1)S(1)}, bf16[512,128]{1,0:T(8,128)(2,1)S(1)}, u32[]{:S(2)}, u32[]{:S(2)}) collective-permute-start(bf16[512,128]{1,0:T(8,128)(2,1)S(1)} %collective-permute-done.13.rest_2_), channel_id=1, source_target_pairs={{0,4},{4,0},{8,12},{12,8},{16,20},{20,16},{24,28},{28,24},{1,5},{5... | collective-permute-start | bytes 393224 | tf_op jit(solution)/shard_map/ppermute | solution.py:65

commit v7 on v4

--- a/solution.py
+++ b/solution.py
@@ -70,6 +70,20 @@
     return jnp.where(flip == 3, 1, flip + 1)
 
 
+def make_payloads(place, columns, values, first, second):
+    size = values.shape[2]
+    lane = lax.broadcasted_iota(jnp.int32, (TILE, size), 1)
+    line = lax.broadcasted_iota(jnp.int32, (TILE, size), 0)
+    tile = jnp.zeros((TILE, size), jnp.int32)
+    for m in range(4):
+        here = (lane == place[0] + m) & (line == 0)
+        tile = jnp.where(here, columns[m // 2, m % 2], tile)
+    for t in range(2):
+        first[t * size : (t + 1) * size, :] = values[0, t]
+        second[t * size : (t + 1) * size, :] = values[1, t]
+    second[2 * size :, :] = tile.astype(jnp.float32).astype(jnp.bfloat16)
+
+
 def local_iteration(origin, *rest):
     lines, planes = rest[:4], rest[4:16]
     out, xs, ys, qs, numbers, pattern, x_table, y_table, near, sem = rest[16:]
@@ -178,7 +192,7 @@
                     ys[y_at(j, i)] = block.T
             return carry
 
-        lax.fori_loop(home * 4, home * 4 + 4, square, 0)
+        lax.fori_loop(home * 4, home * 4 + 4, square, 0, unroll=2)
 
     eye = (
         lax.broadcasted_iota(jnp.int32, (size, size), 0)
@@ -198,7 +212,7 @@
             qs[i * slots + t] = value.astype(jnp.bfloat16)
         return carry
 
-    lax.fori_loop(0, rows, polynomial, 0)
+    lax.fori_loop(0, rows, polynomial, 0, unroll=4)
 
     for a in range(2):
         i = band * 2 + a
@@ -221,15 +235,20 @@
     size = values.shape[2]
     band, c = lax.axis_index("row"), lax.axis_index("col")
     z = band // 2
-    lane = lax.broadcasted_iota(jnp.int32, (TILE, size), 1)
-    line_number = lax.broadcasted_iota(jnp.int32, (TILE, size), 0)
-    first = (band * 4 + c) * 4
-    tile = jnp.zeros((TILE, size), jnp.int32)
-    for m in range(4):
-        here = (lane == first + m) & (line_number == 0)
-        tile = jnp.where(here, columns[m // 2, m % 2], tile)
-    halves = values.reshape(2, 2 * size, size)
-    mine = (halves[0], jnp.concatenate([halves[1], tile.astype(jnp.bfloat16)]))
+    place = ((band * 4 + c) * 4).reshape(1).astype(jnp.int32)
+    mine = pl.pallas_call(
+        make_payloads,
+        out_shape=[
+            jax.ShapeDtypeStruct((2 * size, size), jnp.bfloat16),
+            jax.ShapeDtypeStruct((2 * size + TILE, size), jnp.bfloat16),
+        ],
+        in_specs=[
+            pl.BlockSpec(memory_space=pltpu.SMEM),
+            pl.BlockSpec(memory_space=pltpu.SMEM),
+            pl.BlockSpec(memory_space=pltpu.VMEM),
+        ],
+        out_specs=[pl.BlockSpec(memory_space=pltpu.VMEM)] * 2,
+    )(place, columns, values)
 
     def from_line(line, h):
         return lax.dynamic_index_in_dim(line, (z - h) % 4, axis=0, keepdims=False)

time: 47.8 us -> 44.2 us (0.925)
  waiting for transfers between devices: 6.84 us -> 11.2 us
  other arithmetic: 2.94 us -> 0.22 us
  starting transfers between devices: 21.6 us -> 19.7 us
  Pallas kernels: 13.8 us -> 11.9 us
  local copies, waits for them, and re-layouts: 2.28 us -> 0.97 us
    ppermute x6, waiting for transfers between devices: 0.02 us -> 3.69 us  [around(): lax.ppermute(array, 'row', [(r, (r + 2 * step) % bands) for r in range(ba...]
    pallas_call x1, Pallas kernels: 13.8 us -> 10.4 us  [per_device_whole(): pl.pallas_call(local_iteration, out_shape=jax.ShapeDtypeStruct(values.sha...]
    convert_element_type x1 -> x0, other arithmetic: 2.69 us -> none  [per_device_whole(): mine = (halves[0], jnp.concatenate([halves[1], tile.astype(jnp.bfloat16)]))]
    ppermute x6, starting transfers between devices: 11.9 us -> 10 us  [around(): lax.ppermute(array, 'row', [(r, (r + 2 * step) % bands) for r in range(ba...]
    pallas_call x0 -> x1, Pallas kernels: none -> 1.57 us  [per_device_whole(): pl.pallas_call(make_payloads, out_shape=[jax.ShapeDtypeStruct((2 * size,...]
    slice x2 -> x0, local copies, waits for them, and re-layouts: 1.55 us -> none  [the longest x1 0.88 us: per_device_whole(): mine = (halves[0], jnp.concatenate([halves[1], tile.astype(jnp.bfloat16)]))]
    ppermute x6, waiting for transfers between devices: 5.81 us -> 6.45 us  [across(): return lax.ppermute(array, 'col', [(c, c ^ flip) for c in range(4)])]
  transfers between devices with their start and end apart: 20 -> 20, of which waited for: 8 -> 9; matrix products, arithmetic and copies ran while one was open for 8% -> 1% of each run, Pallas kernels for 0% -> 0%
where the time goes in v7:
time: 44.2 us; the launch traced here: 44 us
  starting transfers between devices  19.7 us (45%)
  Pallas kernels  11.9 us (27%)
  waiting for transfers between devices  11.2 us (25%)
  local copies, waits for them, and re-layouts  0.97 us (2%)
    pallas_call x1, Pallas kernels, per_device_whole(): pl.pallas_call(local_iteration, out_shape=jax.ShapeDtypeStruct(values.sha...  10.4 us
    ppermute x6, starting transfers between devices, around(): lax.ppermute(array, 'row', [(r, (r + 2 * step) % bands) for r in range(ba...  10 us
    ppermute x6, starting transfers between devices, across(): return lax.ppermute(array, 'col', [(c, c ^ flip) for c in range(4)])  8.06 us
    ppermute x6, waiting for transfers between devices, across(): return lax.ppermute(array, 'col', [(c, c ^ flip) for c in range(4)])  6.45 us
    ppermute x6, waiting for transfers between devices, around(): lax.ppermute(array, 'row', [(r, (r + 2 * step) % bands) for r in range(ba...  3.69 us
    ppermute x8, starting transfers between devices, sibling(): return lax.ppermute(array, 'row', [(r, r ^ 1) for r in range(bands)])  1.6 us
    pallas_call x1, Pallas kernels, per_device_whole(): pl.pallas_call(make_payloads, out_shape=[jax.ShapeDtypeStruct((2 * size,...  1.57 us
    ppermute x8, waiting for transfers between devices, sibling(): return lax.ppermute(array, 'row', [(r, r ^ 1) for r in range(bands)])  1.02 us
  transfers between devices with their start and end apart: 20, of which 9 were waited for; matrix products, arithmetic and copies ran while one was open for 1% of the time, Pallas kernels for 0%

profile of v7, /device:TPU:0, one launch (start us, length us, event | category | flops | bytes accessed | tf_op | source)
XLA Modules:
  0.0 44.0 jit_solution(7541192344749624609)
XLA Ops:
  0.0 1.6 %shard_map.28 = (bf16[256,128]{1,0:T(8,128)(2,1)}, bf16[272,128]{1,0:T(8,128)(2,1)}) custom-call(s32[1]{0:T(128)} %bitcast.2.place, s32[2,2]{1,0:T(2,128)} %columns.1, bf16[2,2,128,128]{3,2,1,0:T(8,128)(2,1)} %values.1), custom_call_target="tpu_custom_call" | custom-call | tf_op jit(solution)/shard_map/pallas_call | solution.py:239
  1.6 5.0 %collective-permute-start.2 = (bf16[256,128]{1,0:T(8,128)(2,1)}, bf16[256,128]{1,0:T(8,128)(2,1)S(1)}, u32[]{:S(2)}, u32[]{:S(2)}) collective-permute-start(bf16[256,128]{1,0:T(8,128)(2,1)} %get-tuple-element.7), channel_id=1, source_target_pairs={{0,24},{4,28},{8,0},{12,4},{16,8},{20,12},{24,16},{28,20},{1,25},{... | collective-permute-start | bytes 196616 | tf_op jit(solution)/shard_map/ppermute | solution.py:58
  6.6 0.0 collective-permute-start.1
  6.6 1.0 %collective-permute-start = (bf16[256,128]{1,0:T(8,128)(2,1)}, bf16[256,128]{1,0:T(8,128)(2,1)S(1)}, u32[]{:S(2)}, u32[]{:S(2)}) collective-permute-start(bf16[256,128]{1,0:T(8,128)(2,1)} %get-tuple-element.7), channel_id=1, source_target_pairs={{0,8},{4,12},{8,16},{12,20},{16,24},{20,28},{24,0},{28,4},{1,9},{5... | collective-permute-start | bytes 196616 | tf_op jit(solution)/shard_map/ppermute | solution.py:58
  7.6 2.8 %collective-permute-start.5 = (bf16[272,128]{1,0:T(8,128)(2,1)}, bf16[272,128]{1,0:T(8,128)(2,1)S(1)}, u32[]{:S(2)}, u32[]{:S(2)}) collective-permute-start(bf16[272,128]{1,0:T(8,128)(2,1)} %get-tuple-element.8), channel_id=1, source_target_pairs={{0,24},{4,28},{8,0},{12,4},{16,8},{20,12},{24,16},{28,20},{1,25},{... | collective-permute-start | bytes 208904 | tf_op jit(solution)/shard_map/ppermute | solution.py:58
  10.4 1.1 %collective-permute-start.4 = (bf16[272,128]{1,0:T(8,128)(2,1)}, bf16[272,128]{1,0:T(8,128)(2,1)S(1)}, u32[]{:S(2)}, u32[]{:S(2)}) collective-permute-start(bf16[272,128]{1,0:T(8,128)(2,1)} %get-tuple-element.8), channel_id=1, source_target_pairs={{0,16},{4,20},{8,24},{12,28},{16,0},{20,4},{24,8},{28,12},{1,17},{... | collective-permute-start | bytes 208904 | tf_op jit(solution)/shard_map/ppermute | solution.py:58
  11.6 0.0 collective-permute-done.2
  11.6 0.9 %copy-done = bf16[272,128]{1,0:T(8,128)(2,1)S(1)} copy-done((bf16[272,128]{1,0:T(8,128)(2,1)S(1)}, bf16[272,128]{1,0:T(8,128)(2,1)}, u32[]{:S(2)}) %copy-start) | copy-done | bytes 69656
  12.5 0.0 collective-permute-start.3
  12.5 1.9 %collective-permute-done.1 = bf16[256,128]{1,0:T(8,128)(2,1)S(1)} collective-permute-done((bf16[256,128]{1,0:T(8,128)(2,1)}, bf16[256,128]{1,0:T(8,128)(2,1)S(1)}, u32[]{:S(2)}, u32[]{:S(2)}) %collective-permute-start.1) | collective-permute-done | bytes 65568 | tf_op jit(solution)/shard_map/ppermute | solution.py:58
  14.5 2.5 %collective-permute-start.10 = (bf16[512,128]{1,0:T(8,128)(2,1)S(1)}, bf16[512,128]{1,0:T(8,128)(2,1)S(1)}, u32[]{:S(2)}, u32[]{:S(2)}) collective-permute-start(bf16[512,128]{1,0:T(8,128)(2,1)S(1)} %get-tuple-element.20), channel_id=1, source_target_pairs={{0,3},{1,2},{2,1},{3,0},{4,7},{5,6},{6,5},{7,4},{8,11},{9,10},{10,... | collective-permute-start | bytes 393224 | tf_op jit(solution)/shard_map/ppermute | solution.py:62
  17.0 0.5 %collective-permute-start.9 = (bf16[512,128]{1,0:T(8,128)(2,1)S(1)}, bf16[512,128]{1,0:T(8,128)(2,1)S(1)}, u32[]{:S(2)}, u32[]{:S(2)}) collective-permute-start(bf16[512,128]{1,0:T(8,128)(2,1)S(1)} %get-tuple-element.21), channel_id=1, source_target_pairs={{0,2},{1,3},{2,0},{3,1},{4,6},{5,7},{6,4},{7,5},{8,10},{9,11},{10,... | collective-permute-start | bytes 393224 | tf_op jit(solution)/shard_map/ppermute | solution.py:62
  17.5 1.8 %collective-permute-done.4 = bf16[272,128]{1,0:T(8,128)(2,1)S(1)} collective-permute-done((bf16[272,128]{1,0:T(8,128)(2,1)}, bf16[272,128]{1,0:T(8,128)(2,1)S(1)}, u32[]{:S(2)}, u32[]{:S(2)}) %collective-permute-start.4) | collective-permute-done | bytes 69664 | tf_op jit(solution)/shard_map/ppermute | solution.py:58
  19.3 0.0 collective-permute-done.3
  19.5 2.5 %collective-permute-start.13 = (bf16[528,128]{1,0:T(8,128)(2,1)S(1)}, bf16[528,128]{1,0:T(8,128)(2,1)S(1)}, u32[]{:S(2)}, u32[]{:S(2)}) collective-permute-start(bf16[528,128]{1,0:T(8,128)(2,1)S(1)} %get-tuple-element.17), channel_id=1, source_target_pairs={{0,3},{1,2},{2,1},{3,0},{4,7},{5,6},{6,5},{7,4},{8,11},{9,10},{10,... | collective-permute-start | bytes 405512 | tf_op jit(solution)/shard_map/ppermute | solution.py:62
  22.0 0.5 %collective-permute-start.12 = (bf16[528,128]{1,0:T(8,128)(2,1)S(1)}, bf16[528,128]{1,0:T(8,128)(2,1)S(1)}, u32[]{:S(2)}, u32[]{:S(2)}) collective-permute-start(bf16[528,128]{1,0:T(8,128)(2,1)S(1)} %get-tuple-element.18), channel_id=1, source_target_pairs={{0,2},{1,3},{2,0},{3,1},{4,6},{5,7},{6,4},{7,5},{8,10},{9,11},{10,... | collective-permute-start | bytes 405512 | tf_op jit(solution)/shard_map/ppermute | solution.py:62
  22.5 0.5 %collective-permute-start.8 = (bf16[512,128]{1,0:T(8,128)(2,1)S(1)}, bf16[512,128]{1,0:T(8,128)(2,1)S(1)}, u32[]{:S(2)}, u32[]{:S(2)}) collective-permute-start(bf16[512,128]{1,0:T(8,128)(2,1)S(1)} %get-tuple-element.22), channel_id=1, source_target_pairs={{0,1},{1,0},{2,3},{3,2},{4,5},{5,4},{6,7},{7,6},{8,9},{9,8},{10,11... | collective-permute-start | bytes 393224 | tf_op jit(solution)/shard_map/ppermute | solution.py:62
  23.0 1.5 %collective-permute-start.11 = (bf16[528,128]{1,0:T(8,128)(2,1)S(1)}, bf16[528,128]{1,0:T(8,128)(2,1)S(1)}, u32[]{:S(2)}, u32[]{:S(2)}) collective-permute-start(bf16[528,128]{1,0:T(8,128)(2,1)S(1)} %get-tuple-element.19), channel_id=1, source_target_pairs={{0,1},{1,0},{2,3},{3,2},{4,5},{5,4},{6,7},{7,6},{8,9},{9,8},{10,11... | collective-permute-start | bytes 405512 | tf_op jit(solution)/shard_map/ppermute | solution.py:62
  24.5 1.8 %collective-permute-done.9.rest_5_ = bf16[512,128]{1,0:T(8,128)(2,1)S(1)} collective-permute-done((bf16[512,128]{1,0:T(8,128)(2,1)S(1)}, bf16[512,128]{1,0:T(8,128)(2,1)S(1)}, u32[]{:S(2)}, u32[]{:S(2)}) %collective-permute-start.9) | collective-permute-done | bytes 131104 | tf_op jit(solution)/shard_map/ppermute | solution.py:62
  26.3 3.5 %collective-permute-done.8.rest_4_ = bf16[512,128]{1,0:T(8,128)(2,1)S(1)} collective-permute-done((bf16[512,128]{1,0:T(8,128)(2,1)S(1)}, bf16[512,128]{1,0:T(8,128)(2,1)S(1)}, u32[]{:S(2)}, u32[]{:S(2)}) %collective-permute-start.8) | collective-permute-done | bytes 131104 | tf_op jit(solution)/shard_map/ppermute | solution.py:62
  29.8 0.5 %collective-permute-start.15 = (bf16[512,128]{1,0:T(8,128)(2,1)S(1)}, bf16[512,128]{1,0:T(8,128)(2,1)S(1)}, u32[]{:S(2)}, u32[]{:S(2)}) collective-permute-start(bf16[512,128]{1,0:T(8,128)(2,1)S(1)} %collective-permute-done.9.rest_5_), channel_id=1, source_target_pairs={{0,4},{4,0},{8,12},{12,8},{16,20},{20,16},{24,28},{28,24},{1,5},{5... | collective-permute-start | bytes 393224 | tf_op jit(solution)/shard_map/ppermute | solution.py:66
  30.3 0.1 collective-permute-start.14
  30.3 1.2 %collective-permute-done.11.rest_7_ = bf16[528,128]{1,0:T(8,128)(2,1)S(1)} collective-permute-done((bf16[528,128]{1,0:T(8,128)(2,1)S(1)}, bf16[528,128]{1,0:T(8,128)(2,1)S(1)}, u32[]{:S(2)}, u32[]{:S(2)}) %collective-permute-start.11) | collective-permute-done | bytes 135200 | tf_op jit(solution)/shard_map/ppermute | solution.py:62
  31.5 0.5 %collective-permute-start.19 = (bf16[528,128]{1,0:T(8,128)(2,1)S(1)}, bf16[528,128]{1,0:T(8,128)(2,1)S(1)}, u32[]{:S(2)}, u32[]{:S(2)}) collective-permute-start(bf16[528,128]{1,0:T(8,128)(2,1)S(1)} %collective-permute-done.13.rest_9_), channel_id=1, source_target_pairs={{0,4},{4,0},{8,12},{12,8},{16,20},{20,16},{24,28},{28,24},{1,5},{5... | collective-permute-start | bytes 405512 | tf_op jit(solution)/shard_map/ppermute | solution.py:66
  32.1 0.1 collective-permute-start.18
  32.1 0.4 %collective-permute-start.17 = (bf16[528,128]{1,0:T(8,128)(2,1)S(1)}, bf16[528,128]{1,0:T(8,128)(2,1)S(1)}, u32[]{:S(2)}, u32[]{:S(2)}) collective-permute-start(bf16[528,128]{1,0:T(8,128)(2,1)S(1)} %collective-permute-done.11.rest_7_), channel_id=1, source_target_pairs={{0,4},{4,0},{8,12},{12,8},{16,20},{20,16},{24,28},{28,24},{1,5},{5... | collective-permute-start | bytes 405512 | tf_op jit(solution)/shard_map/ppermute | solution.py:66
  32.6 0.1 pad_add_fusion.origin
  32.6 0.4 collective-permute-done.6.rest_2_
  33.1 0.2 collective-permute-done.19.rest_15_
  33.3 0.2 collective-permute-done.18.rest_14_
  33.5 0.2 collective-permute-done.17.rest_13_
  33.7 10.4 %shard_map.29 = f32[2,2,128,128]{3,2,1,0:T(8,128)} custom-call(s32[2]{0:T(128)S(1)} %pad_add_fusion.origin, bf16[1024,128]{1,0:T(8,128)(2,1)S(1)} %bitcast.32, bf16[1088,128]{1,0:T(8,128)(2,1)S(1)} %bitcast.30, bf16[1024,128]{1,0:T(8,128)(2,1)S(1)} %collective-permute-done.6.rest_2_, bf16[1088,128]{1,0:T(8,128)(2,1)S(1)} %collective-permute-done.7.rest_3_, ...), custom_call_target="tpu_custom_call" | custom-call | tf_op jit(solution)/shard_map/pallas_call | solution.py:269
  (22 shorter events, 0.2 us)
Async XLA Ops:
  1.6 10.0 %collective-permute-start.2 = (bf16[256,128]{1,0:T(8,128)(2,1)}, bf16[256,128]{1,0:T(8,128)(2,1)S(1)}, u32[]{:S(2)}, u32[]{:S(2)}) collective-permute-start(bf16[256,128]{1,0:T(8,128)(2,1)} %get-tuple-element.7), channel_id=1, source_target_pairs={{0,24},{4,28},{8,0},{12,4},{16,8},{20,12},{24,16},{28,20},{1,25},{... | collective-permute-start | bytes 196616 | tf_op jit(solution)/shard_map/ppermute | solution.py:58
  6.6 7.8 %collective-permute-start.1 = (bf16[256,128]{1,0:T(8,128)(2,1)}, bf16[256,128]{1,0:T(8,128)(2,1)S(1)}, u32[]{:S(2)}, u32[]{:S(2)}) collective-permute-start(bf16[256,128]{1,0:T(8,128)(2,1)} %get-tuple-element.7), channel_id=1, source_target_pairs={{0,16},{4,20},{8,24},{12,28},{16,0},{20,4},{24,8},{28,12},{1,17},{... | collective-permute-start | bytes 196616 | tf_op jit(solution)/shard_map/ppermute | solution.py:58
  6.6 7.8 %collective-permute-start = (bf16[256,128]{1,0:T(8,128)(2,1)}, bf16[256,128]{1,0:T(8,128)(2,1)S(1)}, u32[]{:S(2)}, u32[]{:S(2)}) collective-permute-start(bf16[256,128]{1,0:T(8,128)(2,1)} %get-tuple-element.7), channel_id=1, source_target_pairs={{0,8},{4,12},{8,16},{12,20},{16,24},{20,28},{24,0},{28,4},{1,9},{5... | collective-permute-start | bytes 196616 | tf_op jit(solution)/shard_map/ppermute | solution.py:58
  7.6 9.9 %collective-permute-start.5 = (bf16[272,128]{1,0:T(8,128)(2,1)}, bf16[272,128]{1,0:T(8,128)(2,1)S(1)}, u32[]{:S(2)}, u32[]{:S(2)}) collective-permute-start(bf16[272,128]{1,0:T(8,128)(2,1)} %get-tuple-element.8), channel_id=1, source_target_pairs={{0,24},{4,28},{8,0},{12,4},{16,8},{20,12},{24,16},{28,20},{1,25},{... | collective-permute-start | bytes 208904 | tf_op jit(solution)/shard_map/ppermute | solution.py:58
  10.4 8.9 %collective-permute-start.4 = (bf16[272,128]{1,0:T(8,128)(2,1)}, bf16[272,128]{1,0:T(8,128)(2,1)S(1)}, u32[]{:S(2)}, u32[]{:S(2)}) collective-permute-start(bf16[272,128]{1,0:T(8,128)(2,1)} %get-tuple-element.8), channel_id=1, source_target_pairs={{0,16},{4,20},{8,24},{12,28},{16,0},{20,4},{24,8},{28,12},{1,17},{... | collective-permute-start | bytes 208904 | tf_op jit(solution)/shard_map/ppermute | solution.py:58
  11.6 0.9 %copy-start = (bf16[272,128]{1,0:T(8,128)(2,1)S(1)}, bf16[272,128]{1,0:T(8,128)(2,1)}, u32[]{:S(2)}) copy-start(bf16[272,128]{1,0:T(8,128)(2,1)} %get-tuple-element.8) | copy-start | bytes 208900
  11.6 2.8 %copy-start.1 = (bf16[256,128]{1,0:T(8,128)(2,1)S(1)}, bf16[256,128]{1,0:T(8,128)(2,1)}, u32[]{:S(2)}) copy-start(bf16[256,128]{1,0:T(8,128)(2,1)} %get-tuple-element.7) | copy-start | bytes 196612
  12.5 6.8 %collective-permute-start.3 = (bf16[272,128]{1,0:T(8,128)(2,1)S(1)}, bf16[272,128]{1,0:T(8,128)(2,1)S(1)}, u32[]{:S(2)}, u32[]{:S(2)}) collective-permute-start(bf16[272,128]{1,0:T(8,128)(2,1)S(1)} %copy-done), channel_id=1, source_target_pairs={{0,8},{4,12},{8,16},{12,20},{16,24},{20,28},{24,0},{28,4},{1,9},{5... | collective-permute-start | bytes 208904 | tf_op jit(solution)/shard_map/ppermute | solution.py:58
  14.5 8.5 %collective-permute-start.10 = (bf16[512,128]{1,0:T(8,128)(2,1)S(1)}, bf16[512,128]{1,0:T(8,128)(2,1)S(1)}, u32[]{:S(2)}, u32[]{:S(2)}) collective-permute-start(bf16[512,128]{1,0:T(8,128)(2,1)S(1)} %get-tuple-element.20), channel_id=1, source_target_pairs={{0,3},{1,2},{2,1},{3,0},{4,7},{5,6},{6,5},{7,4},{8,11},{9,10},{10,... | collective-permute-start | bytes 393224 | tf_op jit(solution)/shard_map/ppermute | solution.py:62
  17.0 9.3 %collective-permute-start.9 = (bf16[512,128]{1,0:T(8,128)(2,1)S(1)}, bf16[512,128]{1,0:T(8,128)(2,1)S(1)}, u32[]{:S(2)}, u32[]{:S(2)}) collective-permute-start(bf16[512,128]{1,0:T(8,128)(2,1)S(1)} %get-tuple-element.21), channel_id=1, source_target_pairs={{0,2},{1,3},{2,0},{3,1},{4,6},{5,7},{6,4},{7,5},{8,10},{9,11},{10,... | collective-permute-start | bytes 393224 | tf_op jit(solution)/shard_map/ppermute | solution.py:62
  19.5 10.3 %collective-permute-start.13 = (bf16[528,128]{1,0:T(8,128)(2,1)S(1)}, bf16[528,128]{1,0:T(8,128)(2,1)S(1)}, u32[]{:S(2)}, u32[]{:S(2)}) collective-permute-start(bf16[528,128]{1,0:T(8,128)(2,1)S(1)} %get-tuple-element.17), channel_id=1, source_target_pairs={{0,3},{1,2},{2,1},{3,0},{4,7},{5,6},{6,5},{7,4},{8,11},{9,10},{10,... | collective-permute-start | bytes 405512 | tf_op jit(solution)/shard_map/ppermute | solution.py:62
  22.0 8.3 %collective-permute-start.12 = (bf16[528,128]{1,0:T(8,128)(2,1)S(1)}, bf16[528,128]{1,0:T(8,128)(2,1)S(1)}, u32[]{:S(2)}, u32[]{:S(2)}) collective-permute-start(bf16[528,128]{1,0:T(8,128)(2,1)S(1)} %get-tuple-element.18), channel_id=1, source_target_pairs={{0,2},{1,3},{2,0},{3,1},{4,6},{5,7},{6,4},{7,5},{8,10},{9,11},{10,... | collective-permute-start | bytes 405512 | tf_op jit(solution)/shard_map/ppermute | solution.py:62
  22.5 7.3 %collective-permute-start.8 = (bf16[512,128]{1,0:T(8,128)(2,1)S(1)}, bf16[512,128]{1,0:T(8,128)(2,1)S(1)}, u32[]{:S(2)}, u32[]{:S(2)}) collective-permute-start(bf16[512,128]{1,0:T(8,128)(2,1)S(1)} %get-tuple-element.22), channel_id=1, source_target_pairs={{0,1},{1,0},{2,3},{3,2},{4,5},{5,4},{6,7},{7,6},{8,9},{9,8},{10,11... | collective-permute-start | bytes 393224 | tf_op jit(solution)/shard_map/ppermute | solution.py:62
  23.0 8.5 %collective-permute-start.11 = (bf16[528,128]{1,0:T(8,128)(2,1)S(1)}, bf16[528,128]{1,0:T(8,128)(2,1)S(1)}, u32[]{:S(2)}, u32[]{:S(2)}) collective-permute-start(bf16[528,128]{1,0:T(8,128)(2,1)S(1)} %get-tuple-element.19), channel_id=1, source_target_pairs={{0,1},{1,0},{2,3},{3,2},{4,5},{5,4},{6,7},{7,6},{8,9},{9,8},{10,11... | collective-permute-start | bytes 405512 | tf_op jit(solution)/shard_map/ppermute | solution.py:62
  26.3 7.4 %collective-permute-start.7 = (bf16[1088,128]{1,0:T(8,128)(2,1)S(1)}, bf16[1088,128]{1,0:T(8,128)(2,1)S(1)}, u32[]{:S(2)}, u32[]{:S(2)}) collective-permute-start(bf16[1088,128]{1,0:T(8,128)(2,1)S(1)} %bitcast.29), channel_id=1, source_target_pairs={{0,4},{4,0},{8,12},{12,8},{16,20},{20,16},{24,28},{28,24},{1,5},{5... | collective-permute-start | bytes 835592 | tf_op jit(solution)/shard_map/ppermute | solution.py:66
  29.8 1.8 %collective-permute-start.16 = (bf16[512,128]{1,0:T(8,128)(2,1)S(1)}, bf16[512,128]{1,0:T(8,128)(2,1)S(1)}, u32[]{:S(2)}, u32[]{:S(2)}) collective-permute-start(bf16[512,128]{1,0:T(8,128)(2,1)S(1)} %collective-permute-done.10.rest_6_), channel_id=1, source_target_pairs={{0,4},{4,0},{8,12},{12,8},{16,20},{20,16},{24,28},{28,24},{1,5},{5... | collective-permute-start | bytes 393224 | tf_op jit(solution)/shard_map/ppermute | solution.py:66
  29.8 2.3 %collective-permute-start.15 = (bf16[512,128]{1,0:T(8,128)(2,1)S(1)}, bf16[512,128]{1,0:T(8,128)(2,1)S(1)}, u32[]{:S(2)}, u32[]{:S(2)}) collective-permute-start(bf16[512,128]{1,0:T(8,128)(2,1)S(1)} %collective-permute-done.9.rest_5_), channel_id=1, source_target_pairs={{0,4},{4,0},{8,12},{12,8},{16,20},{20,16},{24,28},{28,24},{1,5},{5... | collective-permute-start | bytes 393224 | tf_op jit(solution)/shard_map/ppermute | solution.py:66
  30.3 1.9 %collective-permute-start.14 = (bf16[512,128]{1,0:T(8,128)(2,1)S(1)}, bf16[512,128]{1,0:T(8,128)(2,1)S(1)}, u32[]{:S(2)}, u32[]{:S(2)}) collective-permute-start(bf16[512,128]{1,0:T(8,128)(2,1)S(1)} %collective-permute-done.8.rest_4_), channel_id=1, source_target_pairs={{0,4},{4,0},{8,12},{12,8},{16,20},{20,16},{24,28},{28,24},{1,5},{5... | collective-permute-start | bytes 393224 | tf_op jit(solution)/shard_map/ppermute | solution.py:66
  31.5 1.5 %collective-permute-start.6 = (bf16[1024,128]{1,0:T(8,128)(2,1)S(1)}, bf16[1024,128]{1,0:T(8,128)(2,1)S(1)}, u32[]{:S(2)}, u32[]{:S(2)}) collective-permute-start(bf16[1024,128]{1,0:T(8,128)(2,1)S(1)} %bitcast.31), channel_id=1, source_target_pairs={{0,4},{4,0},{8,12},{12,8},{16,20},{20,16},{24,28},{28,24},{1,5},{5... | collective-permute-start | bytes 786440 | tf_op jit(solution)/shard_map/ppermute | solution.py:66
  31.5 1.7 %collective-permute-start.19 = (bf16[528,128]{1,0:T(8,128)(2,1)S(1)}, bf16[528,128]{1,0:T(8,128)(2,1)S(1)}, u32[]{:S(2)}, u32[]{:S(2)}) collective-permute-start(bf16[528,128]{1,0:T(8,128)(2,1)S(1)} %collective-permute-done.13.rest_9_), channel_id=1, source_target_pairs={{0,4},{4,0},{8,12},{12,8},{16,20},{20,16},{24,28},{28,24},{1,5},{5... | collective-permute-start | bytes 405512 | tf_op jit(solution)/shard_map/ppermute | solution.py:66
  32.1 1.4 %collective-permute-start.18 = (bf16[528,128]{1,0:T(8,128)(2,1)S(1)}, bf16[528,128]{1,0:T(8,128)(2,1)S(1)}, u32[]{:S(2)}, u32[]{:S(2)}) collective-permute-start(bf16[528,128]{1,0:T(8,128)(2,1)S(1)} %collective-permute-done.12.rest_8_), channel_id=1, source_target_pairs={{0,4},{4,0},{8,12},{12,8},{16,20},{20,16},{24,28},{28,24},{1,5},{5... | collective-permute-start | bytes 405512 | tf_op jit(solution)/shard_map/ppermute | solution.py:66
  32.1 1.5 %collective-permute-start.17 = (bf16[528,128]{1,0:T(8,128)(2,1)S(1)}, bf16[528,128]{1,0:T(8,128)(2,1)S(1)}, u32[]{:S(2)}, u32[]{:S(2)}) collective-permute-start(bf16[528,128]{1,0:T(8,128)(2,1)S(1)} %collective-permute-done.11.rest_7_), channel_id=1, source_target_pairs={{0,4},{4,0},{8,12},{12,8},{16,20},{20,16},{24,28},{28,24},{1,5},{5... | collective-permute-start | bytes 405512 | tf_op jit(solution)/shard_map/ppermute | solution.py:66

commit v8 on v4

--- a/solution.py
+++ b/solution.py
@@ -70,30 +70,35 @@
     return jnp.where(flip == 3, 1, flip + 1)
 
 
+def make_tile(place, columns, out):
+    lane = lax.broadcasted_iota(jnp.int32, out.shape, 1)
+    line = lax.broadcasted_iota(jnp.int32, out.shape, 0)
+    tile = jnp.zeros(out.shape, jnp.int32)
+    for m in range(4):
+        here = (lane == place[0] + m) & (line == 0)
+        tile = jnp.where(here, columns[m // 2, m % 2], tile)
+    out[...] = tile.astype(jnp.float32).astype(jnp.bfloat16)
+
+
 def local_iteration(origin, *rest):
-    lines, planes = rest[:4], rest[4:16]
-    out, xs, ys, qs, numbers, pattern, x_table, y_table, near, sem = rest[16:]
+    lines, planes = rest[:2], (rest[2:5], rest[5:8])
+    out, xs, ys, qs, numbers, pattern, x_table, y_table, near, sem = rest[8:]
     rows, kept, slots, size = 16, 8, 2, 128
     band, c = origin[0], origin[1]
     z, core = lax.div(band, 2), lax.rem(band, 2)
-    half = slots * size
+    part_rows = 4 * size
 
     pieces = []
     total = jnp.zeros((TILE, size), jnp.float32)
-    for a in range(2):
-        long = half + a * TILE
-        for source, side in ((lines[a], core), (lines[2 + a], 1 - core)):
-            for step in range(4):
-                pieces.append((source, step * long, step * 8 + side * 4 + a * 2))
-                if a == 1:
-                    total += source[step * long + half : step * long + long, :].astype(jnp.float32)
-        for group, side in ((planes[a * 3 : a * 3 + 3], core), (planes[6 + a * 3 : 9 + a * 3], 1 - core)):
-            for flip in range(3):
-                for part in range(2):
-                    place = (4 + flip * 2 + part) * 8 + side * 4 + a * 2
-                    pieces.append((group[flip], part * half, place))
-                if a == 1:
-                    total += group[flip][2 * half : 2 * half + TILE, :].astype(jnp.float32)
+    for line, group, side in zip(lines, planes, (core, 1 - core)):
+        for step in range(4):
+            pieces.append((line, step * part_rows, step * 8 + side * 4))
+        total += line[4 * part_rows :, :].astype(jnp.float32)
+        for flip in range(3):
+            for part in range(2):
+                place = (4 + flip * 2 + part) * 8 + side * 4
+                pieces.append((group[flip], part * part_rows, place))
+            total += group[flip][2 * part_rows :, :].astype(jnp.float32)
     numbers[...] = total[0:8].astype(jnp.int32)
     copy = pltpu.make_async_copy(numbers, pattern, sem)
     copy.start()
@@ -112,7 +117,7 @@
     lax.fori_loop(0, rows * rows, clear, 0, unroll=16)
 
     for source, first, place in pieces:
-        for b in range(slots):
+        for b in range(4):
             xs[place + b] = source[first + b * size : first + (b + 1) * size, :]
     for number, piece in enumerate((0, 1, 2, 3, 5, 7, 9)):
         for b in range(8):
@@ -178,7 +183,7 @@
                     ys[y_at(j, i)] = block.T
             return carry
 
-        lax.fori_loop(home * 4, home * 4 + 4, square, 0)
+        lax.fori_loop(home * 4, home * 4 + 4, square, 0, unroll=4)
 
     eye = (
         lax.broadcasted_iota(jnp.int32, (size, size), 0)
@@ -198,7 +203,7 @@
             qs[i * slots + t] = value.astype(jnp.bfloat16)
         return carry
 
-    lax.fori_loop(0, rows, polynomial, 0)
+    lax.fori_loop(0, rows, polynomial, 0, unroll=8)
 
     for a in range(2):
         i = band * 2 + a
@@ -221,38 +226,35 @@
     size = values.shape[2]
     band, c = lax.axis_index("row"), lax.axis_index("col")
     z = band // 2
-    lane = lax.broadcasted_iota(jnp.int32, (TILE, size), 1)
-    line_number = lax.broadcasted_iota(jnp.int32, (TILE, size), 0)
-    first = (band * 4 + c) * 4
-    tile = jnp.zeros((TILE, size), jnp.int32)
-    for m in range(4):
-        here = (lane == first + m) & (line_number == 0)
-        tile = jnp.where(here, columns[m // 2, m % 2], tile)
-    halves = values.reshape(2, 2 * size, size)
-    mine = (halves[0], jnp.concatenate([halves[1], tile.astype(jnp.bfloat16)]))
-
-    def from_line(line, h):
-        return lax.dynamic_index_in_dim(line, (z - h) % 4, axis=0, keepdims=False)
-
-    lines = [
-        jnp.stack([half] + [around(half, step, bands) for step in range(1, 4)]) for half in mine
-    ]
-    here, lines_there = [], []
-    for a, line in enumerate(lines):
-        tail = [jnp.sum(line[:, 2 * size :], axis=0)] if a else []
-        for flip in range(1, 4):
-            parts = [from_line(line, h)[: 2 * size] for h in (c, c ^ NEXT[flip])]
-            here.append(across(jnp.concatenate(parts + tail), flip))
-        lines_there.append(sibling(line.reshape(-1, size), bands))
+    place = ((band * 4 + c) * 4).reshape(1).astype(jnp.int32)
+    smem, vmem = pl.BlockSpec(memory_space=pltpu.SMEM), pl.BlockSpec(memory_space=pltpu.VMEM)
+    mine = values.reshape(4 * size, size)
+    line = [mine] + [around(mine, step, bands) for step in range(1, 4)]
+    tile = pl.pallas_call(
+        make_tile,
+        out_shape=jax.ShapeDtypeStruct((TILE, size), jnp.bfloat16),
+        in_specs=[smem, smem],
+        out_specs=vmem,
+    )(place, columns)
+    tile = tile + sum(around(tile, step, bands) for step in range(1, 4))
+    stacked = jnp.stack(line)
+
+    def from_line(h):
+        return lax.dynamic_index_in_dim(stacked, (z - h) % 4, axis=0, keepdims=False)
+
+    here = []
+    for flip in range(1, 4):
+        parts = [from_line(h) for h in (c, c ^ NEXT[flip])]
+        here.append(across(jnp.concatenate(parts + [tile]), flip))
+    line = jnp.concatenate(line + [tile])
+    line_there = sibling(line, bands)
     there = [sibling(piece, bands) for piece in here]
-    lines = [line.reshape(-1, size) for line in lines]
     origin = jnp.stack([band, c]).astype(jnp.int32)
     return pl.pallas_call(
         local_iteration,
         out_shape=jax.ShapeDtypeStruct(values.shape, jnp.float32),
-        in_specs=[pl.BlockSpec(memory_space=pltpu.SMEM)]
-        + [pl.BlockSpec(memory_space=pltpu.VMEM)] * 16,
-        out_specs=pl.BlockSpec(memory_space=pltpu.VMEM),
+        in_specs=[smem] + [vmem] * 8,
+        out_specs=vmem,
         scratch_shapes=[
             pltpu.VMEM((17 * 8 + 1, size, size), jnp.bfloat16),
             pltpu.VMEM((129, size, size), jnp.bfloat16),
@@ -265,7 +267,7 @@
             pltpu.SemaphoreType.DMA,
         ],
         compiler_params=pltpu.CompilerParams(vmem_limit_bytes=32 * 1024 * 1024),
-    )(origin, *lines, *lines_there, *here, *there)
+    )(origin, line, line_there, *here, *there)
 
 
 def per_device(values, columns):

time: 47.8 us -> 42.1 us (0.88)
  waiting for transfers between devices: 6.84 us -> 16.8 us
  starting transfers between devices: 21.6 us -> 14.1 us
  Pallas kernels: 13.8 us -> 9.95 us
  other arithmetic: 2.94 us -> 0.22 us
  local copies, waits for them, and re-layouts: 2.28 us -> 0.81 us
    pallas_call x1, Pallas kernels: 13.8 us -> 8.66 us  [per_device_whole(): pl.pallas_call(local_iteration, out_shape=jax.ShapeDtypeStruct(values.sha...]
    ppermute x6, waiting for transfers between devices: 0.02 us -> 5.18 us  [around(): lax.ppermute(array, 'row', [(r, (r + 2 * step) % bands) for r in range(ba...]
    ppermute x6 -> x3, starting transfers between devices: 8.09 us -> 3.55 us  [across(): return lax.ppermute(array, 'col', [(c, c ^ flip) for c in range(4)])]
    ppermute x6 -> x3, waiting for transfers between devices: 5.81 us -> 10.3 us  [across(): return lax.ppermute(array, 'col', [(c, c ^ flip) for c in range(4)])]
    convert_element_type x1 -> x0, other arithmetic: 2.69 us -> none  [per_device_whole(): mine = (halves[0], jnp.concatenate([halves[1], tile.astype(jnp.bfloat16)]))]
    ppermute x6, starting transfers between devices: 11.9 us -> 10 us  [around(): lax.ppermute(array, 'row', [(r, (r + 2 * step) % bands) for r in range(ba...]
    slice x3 -> x0, local copies, waits for them, and re-layouts: 1.58 us -> none  [the longest x1 0.88 us: per_device_whole(): mine = (halves[0], jnp.concatenate([halves[1], tile.astype(jnp.bfloat16)]))]
    pallas_call x0 -> x1, Pallas kernels: none -> 1.29 us  [per_device_whole(): pl.pallas_call(make_tile, out_shape=jax.ShapeDtypeStruct((TILE, size), jn...]
  transfers between devices with their start and end apart: 20 -> 13, of which waited for: 8 -> 6; matrix products, arithmetic and copies ran while one was open for 8% -> 1% of each run, Pallas kernels for 0% -> 3%
where the time goes in v8:
time: 42.1 us; the launch traced here: 41.9 us
  waiting for transfers between devices  16.8 us (40%)
  starting transfers between devices  14.1 us (33%)
  Pallas kernels  9.95 us (24%)
  local copies, waits for them, and re-layouts  0.81 us (2%)
    ppermute x3, waiting for transfers between devices, across(): return lax.ppermute(array, 'col', [(c, c ^ flip) for c in range(4)])  10.3 us
    ppermute x6, starting transfers between devices, around(): lax.ppermute(array, 'row', [(r, (r + 2 * step) % bands) for r in range(ba...  10 us
    pallas_call x1, Pallas kernels, per_device_whole(): pl.pallas_call(local_iteration, out_shape=jax.ShapeDtypeStruct(values.sha...  8.66 us
    ppermute x6, waiting for transfers between devices, around(): lax.ppermute(array, 'row', [(r, (r + 2 * step) % bands) for r in range(ba...  5.18 us
    ppermute x3, starting transfers between devices, across(): return lax.ppermute(array, 'col', [(c, c ^ flip) for c in range(4)])  3.55 us
    ppermute x4, waiting for transfers between devices, sibling(): return lax.ppermute(array, 'row', [(r, r ^ 1) for r in range(bands)])  1.33 us
    pallas_call x1, Pallas kernels, per_device_whole(): pl.pallas_call(make_tile, out_shape=jax.ShapeDtypeStruct((TILE, size), jn...  1.29 us
  transfers between devices with their start and end apart: 13, of which 6 were waited for; matrix products, arithmetic and copies ran while one was open for 1% of the time, Pallas kernels for 3%

profile of v8, /device:TPU:0, one launch (start us, length us, event | category | flops | bytes accessed | tf_op | source)
XLA Modules:
  0.0 41.9 jit_solution(15596127892766229039)
XLA Ops:
  0.0 5.0 %collective-permute-start.2 = (bf16[512,128]{1,0:T(8,128)(2,1)}, bf16[512,128]{1,0:T(8,128)(2,1)S(1)}, u32[]{:S(2)}, u32[]{:S(2)}) collective-permute-start(bf16[512,128]{1,0:T(8,128)(2,1)} %bitcast.16), channel_id=1, source_target_pairs={{0,24},{4,28},{8,0},{12,4},{16,8},{20,12},{24,16},{28,20},{1,25},{... | collective-permute-start | bytes 393224 | tf_op jit(solution)/shard_map/ppermute | solution.py:58
  5.1 0.0 collective-permute-start.1
  5.1 1.0 %collective-permute-start = (bf16[512,128]{1,0:T(8,128)(2,1)}, bf16[512,128]{1,0:T(8,128)(2,1)S(1)}, u32[]{:S(2)}, u32[]{:S(2)}) collective-permute-start(bf16[512,128]{1,0:T(8,128)(2,1)} %bitcast.18), channel_id=1, source_target_pairs={{0,8},{4,12},{8,16},{12,20},{16,24},{20,28},{24,0},{28,4},{1,9},{5... | collective-permute-start | bytes 393224 | tf_op jit(solution)/shard_map/ppermute | solution.py:58
  6.1 1.3 %shard_map.28 = bf16[16,128]{1,0:T(8,128)(2,1)} custom-call(s32[1]{0:T(128)} %bitcast.3.place, s32[2,2]{1,0:T(2,128)} %columns.1), custom_call_target="tpu_custom_call" | custom-call | tf_op jit(solution)/shard_map/pallas_call | solution.py:233
  7.4 2.8 %collective-permute-start.5 = (bf16[16,128]{1,0:T(8,128)(2,1)}, bf16[16,128]{1,0:T(8,128)(2,1)S(1)}, u32[]{:S(2)}, u32[]{:S(2)}) collective-permute-start(bf16[16,128]{1,0:T(8,128)(2,1)} %shard_map.28), channel_id=1, source_target_pairs={{0,24},{4,28},{8,0},{12,4},{16,8},{20,12},{24,16},{28,20},{1,25},{... | collective-permute-start | bytes 12296 | tf_op jit(solution)/shard_map/ppermute | solution.py:58
  10.2 1.1 %collective-permute-start.4 = (bf16[16,128]{1,0:T(8,128)(2,1)}, bf16[16,128]{1,0:T(8,128)(2,1)S(1)}, u32[]{:S(2)}, u32[]{:S(2)}) collective-permute-start(bf16[16,128]{1,0:T(8,128)(2,1)} %shard_map.28), channel_id=1, source_target_pairs={{0,16},{4,20},{8,24},{12,28},{16,0},{20,4},{24,8},{28,12},{1,17},{... | collective-permute-start | bytes 12296 | tf_op jit(solution)/shard_map/ppermute | solution.py:58
  11.3 0.0 collective-permute-done.2
  11.3 0.7 %copy-done.1 = bf16[16,128]{1,0:T(8,128)(2,1)S(1)} copy-done((bf16[16,128]{1,0:T(8,128)(2,1)S(1)}, bf16[16,128]{1,0:T(8,128)(2,1)}, u32[]{:S(2)}) %copy-start.1) | copy-done | bytes 4120
  12.0 0.0 collective-permute-start.3
  12.0 4.7 %collective-permute-done.1 = bf16[512,128]{1,0:T(8,128)(2,1)S(1)} collective-permute-done((bf16[512,128]{1,0:T(8,128)(2,1)}, bf16[512,128]{1,0:T(8,128)(2,1)S(1)}, u32[]{:S(2)}, u32[]{:S(2)}) %collective-permute-start.1) | collective-permute-done | bytes 131104 | tf_op jit(solution)/shard_map/ppermute | solution.py:58
  16.7 0.0 collective-permute-done
  16.7 0.1 pad_maximum_fusion
  16.9 0.0 collective-permute-done.5
  16.9 0.0 collective-permute-done.4
  16.9 0.5 %collective-permute-done.3 = bf16[16,128]{1,0:T(8,128)(2,1)S(1)} collective-permute-done((bf16[16,128]{1,0:T(8,128)(2,1)S(1)}, bf16[16,128]{1,0:T(8,128)(2,1)S(1)}, u32[]{:S(2)}, u32[]{:S(2)}) %collective-permute-start.3) | collective-permute-done | bytes 4128 | tf_op jit(solution)/shard_map/ppermute | solution.py:58
  17.4 0.1 pad_maximum_fusion.1
  17.5 2.5 %collective-permute-start.9 = (bf16[1040,128]{1,0:T(8,128)(2,1)S(1)}, bf16[1040,128]{1,0:T(8,128)(2,1)S(1)}, u32[]{:S(2)}, u32[]{:S(2)}) collective-permute-start(bf16[1040,128]{1,0:T(8,128)(2,1)S(1)} %get-tuple-element.11), channel_id=1, source_target_pairs={{0,3},{1,2},{2,1},{3,0},{4,7},{5,6},{6,5},{7,4},{8,11},{9,10},{10,... | collective-permute-start | bytes 798728 | tf_op jit(solution)/shard_map/ppermute | solution.py:62
  20.0 0.5 %collective-permute-start.7 = (bf16[1040,128]{1,0:T(8,128)(2,1)S(1)}, bf16[1040,128]{1,0:T(8,128)(2,1)S(1)}, u32[]{:S(2)}, u32[]{:S(2)}) collective-permute-start(bf16[1040,128]{1,0:T(8,128)(2,1)S(1)} %get-tuple-element.12), channel_id=1, source_target_pairs={{0,1},{1,0},{2,3},{3,2},{4,5},{5,4},{6,7},{7,6},{8,9},{9,8},{10,11... | collective-permute-start | bytes 798728 | tf_op jit(solution)/shard_map/ppermute | solution.py:62
  20.5 0.5 %collective-permute-start.8 = (bf16[1040,128]{1,0:T(8,128)(2,1)S(1)}, bf16[1040,128]{1,0:T(8,128)(2,1)S(1)}, u32[]{:S(2)}, u32[]{:S(2)}) collective-permute-start(bf16[1040,128]{1,0:T(8,128)(2,1)S(1)} %get-tuple-element.13), channel_id=1, source_target_pairs={{0,2},{1,3},{2,0},{3,1},{4,6},{5,7},{6,4},{7,5},{8,10},{9,11},{10,... | collective-permute-start | bytes 798728 | tf_op jit(solution)/shard_map/ppermute | solution.py:62
  21.1 0.0 collective-permute-start.6
  21.1 6.8 %collective-permute-done.9.rest_4_ = bf16[1040,128]{1,0:T(8,128)(2,1)S(1)} collective-permute-done((bf16[1040,128]{1,0:T(8,128)(2,1)S(1)}, bf16[1040,128]{1,0:T(8,128)(2,1)S(1)}, u32[]{:S(2)}, u32[]{:S(2)}) %collective-permute-start.9) | collective-permute-done | bytes 266272 | tf_op jit(solution)/shard_map/ppermute | solution.py:62
  27.8 0.0 collective-permute-start.12
  27.8 3.5 %collective-permute-done.7.rest_2_ = bf16[1040,128]{1,0:T(8,128)(2,1)S(1)} collective-permute-done((bf16[1040,128]{1,0:T(8,128)(2,1)S(1)}, bf16[1040,128]{1,0:T(8,128)(2,1)S(1)}, u32[]{:S(2)}, u32[]{:S(2)}) %collective-permute-start.7) | collective-permute-done | bytes 266272 | tf_op jit(solution)/shard_map/ppermute | solution.py:62
  31.3 0.0 collective-permute-start.10
  31.4 0.0 collective-permute-done.8.rest_3_
  31.4 0.5 %collective-permute-start.11 = (bf16[1040,128]{1,0:T(8,128)(2,1)S(1)}, bf16[1040,128]{1,0:T(8,128)(2,1)S(1)}, u32[]{:S(2)}, u32[]{:S(2)}) collective-permute-start(bf16[1040,128]{1,0:T(8,128)(2,1)S(1)} %collective-permute-done.8.rest_3_), channel_id=1, source_target_pairs={{0,4},{4,0},{8,12},{12,8},{16,20},{20,16},{24,28},{28,24},{1,5},{5... | collective-permute-start | bytes 798728 | tf_op jit(solution)/shard_map/ppermute | solution.py:66
  31.9 0.1 pad_add_fusion.origin
  31.9 0.0 collective-permute-done.6.rest_1_
  31.9 0.0 collective-permute-done.12.rest_7_
  31.9 0.9 %collective-permute-done.10.rest_5_ = bf16[1040,128]{1,0:T(8,128)(2,1)S(1)} collective-permute-done((bf16[1040,128]{1,0:T(8,128)(2,1)S(1)}, bf16[1040,128]{1,0:T(8,128)(2,1)S(1)}, u32[]{:S(2)}, u32[]{:S(2)}) %collective-permute-start.10) | collective-permute-done | bytes 266272 | tf_op jit(solution)/shard_map/ppermute | solution.py:66
  32.9 0.4 collective-permute-done.11.rest_6_
  33.3 8.7 %shard_map.29 = f32[2,2,128,128]{3,2,1,0:T(8,128)} custom-call(s32[2]{0:T(128)S(1)} %pad_add_fusion.origin, bf16[2064,128]{1,0:T(8,128)(2,1)S(1)} %get-tuple-element.5.rest_0_, bf16[2064,128]{1,0:T(8,128)(2,1)S(1)} %collective-permute-done.6.rest_1_, bf16[1040,128]{1,0:T(8,128)(2,1)S(1)} %collective-permute-done.7.rest_2_, ...), custom_call_target="tpu_custom_call" | custom-call | tf_op jit(solution)/shard_map/pallas_call | solution.py:253
  (9 shorter events, 0.1 us)
Async XLA Ops:
  0.0 11.3 %copy-start = (bf16[2,2,128,128]{3,2,1,0:T(8,128)(2,1)S(1)}, bf16[2,2,128,128]{3,2,1,0:T(8,128)(2,1)}, u32[]{:S(2)}) copy-start(bf16[2,2,128,128]{3,2,1,0:T(8,128)(2,1)} %param.2) | copy-start | bytes 393220
  0.0 11.3 %collective-permute-start.2 = (bf16[512,128]{1,0:T(8,128)(2,1)}, bf16[512,128]{1,0:T(8,128)(2,1)S(1)}, u32[]{:S(2)}, u32[]{:S(2)}) collective-permute-start(bf16[512,128]{1,0:T(8,128)(2,1)} %bitcast.16), channel_id=1, source_target_pairs={{0,24},{4,28},{8,0},{12,4},{16,8},{20,12},{24,16},{28,20},{1,25},{... | collective-permute-start | bytes 393224 | tf_op jit(solution)/shard_map/ppermute | solution.py:58
  5.1 11.6 %collective-permute-start.1 = (bf16[512,128]{1,0:T(8,128)(2,1)}, bf16[512,128]{1,0:T(8,128)(2,1)S(1)}, u32[]{:S(2)}, u32[]{:S(2)}) collective-permute-start(bf16[512,128]{1,0:T(8,128)(2,1)} %bitcast.17), channel_id=1, source_target_pairs={{0,16},{4,20},{8,24},{12,28},{16,0},{20,4},{24,8},{28,12},{1,17},{... | collective-permute-start | bytes 393224 | tf_op jit(solution)/shard_map/ppermute | solution.py:58
  5.1 11.6 %collective-permute-start = (bf16[512,128]{1,0:T(8,128)(2,1)}, bf16[512,128]{1,0:T(8,128)(2,1)S(1)}, u32[]{:S(2)}, u32[]{:S(2)}) collective-permute-start(bf16[512,128]{1,0:T(8,128)(2,1)} %bitcast.18), channel_id=1, source_target_pairs={{0,8},{4,12},{8,16},{12,20},{16,24},{20,28},{24,0},{28,4},{1,9},{5... | collective-permute-start | bytes 393224 | tf_op jit(solution)/shard_map/ppermute | solution.py:58
  7.4 9.5 %collective-permute-start.5 = (bf16[16,128]{1,0:T(8,128)(2,1)}, bf16[16,128]{1,0:T(8,128)(2,1)S(1)}, u32[]{:S(2)}, u32[]{:S(2)}) collective-permute-start(bf16[16,128]{1,0:T(8,128)(2,1)} %shard_map.28), channel_id=1, source_target_pairs={{0,24},{4,28},{8,0},{12,4},{16,8},{20,12},{24,16},{28,20},{1,25},{... | collective-permute-start | bytes 12296 | tf_op jit(solution)/shard_map/ppermute | solution.py:58
  10.2 6.7 %collective-permute-start.4 = (bf16[16,128]{1,0:T(8,128)(2,1)}, bf16[16,128]{1,0:T(8,128)(2,1)S(1)}, u32[]{:S(2)}, u32[]{:S(2)}) collective-permute-start(bf16[16,128]{1,0:T(8,128)(2,1)} %shard_map.28), channel_id=1, source_target_pairs={{0,16},{4,20},{8,24},{12,28},{16,0},{20,4},{24,8},{28,12},{1,17},{... | collective-permute-start | bytes 12296 | tf_op jit(solution)/shard_map/ppermute | solution.py:58
  11.3 0.7 %copy-start.1 = (bf16[16,128]{1,0:T(8,128)(2,1)S(1)}, bf16[16,128]{1,0:T(8,128)(2,1)}, u32[]{:S(2)}) copy-start(bf16[16,128]{1,0:T(8,128)(2,1)} %shard_map.28) | copy-start | bytes 12292
  12.0 5.4 %collective-permute-start.3 = (bf16[16,128]{1,0:T(8,128)(2,1)S(1)}, bf16[16,128]{1,0:T(8,128)(2,1)S(1)}, u32[]{:S(2)}, u32[]{:S(2)}) collective-permute-start(bf16[16,128]{1,0:T(8,128)(2,1)S(1)} %copy-done.1), channel_id=1, source_target_pairs={{0,8},{4,12},{8,16},{12,20},{16,24},{20,28},{24,0},{28,4},{1,9},{5... | collective-permute-start | bytes 12296 | tf_op jit(solution)/shard_map/ppermute | solution.py:58
  17.5 10.3 %collective-permute-start.9 = (bf16[1040,128]{1,0:T(8,128)(2,1)S(1)}, bf16[1040,128]{1,0:T(8,128)(2,1)S(1)}, u32[]{:S(2)}, u32[]{:S(2)}) collective-permute-start(bf16[1040,128]{1,0:T(8,128)(2,1)S(1)} %get-tuple-element.11), channel_id=1, source_target_pairs={{0,3},{1,2},{2,1},{3,0},{4,7},{5,6},{6,5},{7,4},{8,11},{9,10},{10,... | collective-permute-start | bytes 798728 | tf_op jit(solution)/shard_map/ppermute | solution.py:62
  20.0 11.3 %collective-permute-start.7 = (bf16[1040,128]{1,0:T(8,128)(2,1)S(1)}, bf16[1040,128]{1,0:T(8,128)(2,1)S(1)}, u32[]{:S(2)}, u32[]{:S(2)}) collective-permute-start(bf16[1040,128]{1,0:T(8,128)(2,1)S(1)} %get-tuple-element.12), channel_id=1, source_target_pairs={{0,1},{1,0},{2,3},{3,2},{4,5},{5,4},{6,7},{7,6},{8,9},{9,8},{10,11... | collective-permute-start | bytes 798728 | tf_op jit(solution)/shard_map/ppermute | solution.py:62
  20.5 10.8 %collective-permute-start.8 = (bf16[1040,128]{1,0:T(8,128)(2,1)S(1)}, bf16[1040,128]{1,0:T(8,128)(2,1)S(1)}, u32[]{:S(2)}, u32[]{:S(2)}) collective-permute-start(bf16[1040,128]{1,0:T(8,128)(2,1)S(1)} %get-tuple-element.13), channel_id=1, source_target_pairs={{0,2},{1,3},{2,0},{3,1},{4,6},{5,7},{6,4},{7,5},{8,10},{9,11},{10,... | collective-permute-start | bytes 798728 | tf_op jit(solution)/shard_map/ppermute | solution.py:62
  21.1 10.9 %collective-permute-start.6 = (bf16[2064,128]{1,0:T(8,128)(2,1)S(1)}, bf16[2064,128]{1,0:T(8,128)(2,1)S(1)}, u32[]{:S(2)}, u32[]{:S(2)}) collective-permute-start(bf16[2064,128]{1,0:T(8,128)(2,1)S(1)} %get-tuple-element.5.rest_0_), channel_id=1, source_target_pairs={{0,4},{4,0},{8,12},{12,8},{16,20},{20,16},{24,28},{28,24},{1,5},{5... | collective-permute-start | bytes 1585160 | tf_op jit(solution)/shard_map/ppermute | solution.py:66
  27.8 4.1 %collective-permute-start.12 = (bf16[1040,128]{1,0:T(8,128)(2,1)S(1)}, bf16[1040,128]{1,0:T(8,128)(2,1)S(1)}, u32[]{:S(2)}, u32[]{:S(2)}) collective-permute-start(bf16[1040,128]{1,0:T(8,128)(2,1)S(1)} %collective-permute-done.9.rest_4_), channel_id=1, source_target_pairs={{0,4},{4,0},{8,12},{12,8},{16,20},{20,16},{24,28},{28,24},{1,5},{5... | collective-permute-start | bytes 798728 | tf_op jit(solution)/shard_map/ppermute | solution.py:66
  31.3 1.5 %collective-permute-start.10 = (bf16[1040,128]{1,0:T(8,128)(2,1)S(1)}, bf16[1040,128]{1,0:T(8,128)(2,1)S(1)}, u32[]{:S(2)}, u32[]{:S(2)}) collective-permute-start(bf16[1040,128]{1,0:T(8,128)(2,1)S(1)} %collective-permute-done.7.rest_2_), channel_id=1, source_target_pairs={{0,4},{4,0},{8,12},{12,8},{16,20},{20,16},{24,28},{28,24},{1,5},{5... | collective-permute-start | bytes 798728 | tf_op jit(solution)/shard_map/ppermute | solution.py:66
  31.4 1.9 %collective-permute-start.11 = (bf16[1040,128]{1,0:T(8,128)(2,1)S(1)}, bf16[1040,128]{1,0:T(8,128)(2,1)S(1)}, u32[]{:S(2)}, u32[]{:S(2)}) collective-permute-start(bf16[1040,128]{1,0:T(8,128)(2,1)S(1)} %collective-permute-done.8.rest_3_), channel_id=1, source_target_pairs={{0,4},{4,0},{8,12},{12,8},{16,20},{20,16},{24,28},{28,24},{1,5},{5... | collective-permute-start | bytes 798728 | tf_op jit(solution)/shard_map/ppermute | solution.py:66

commit v9 on v8

--- a/solution.py
+++ b/solution.py
@@ -119,9 +119,6 @@
     for source, first, place in pieces:
         for b in range(4):
             xs[place + b] = source[first + b * size : first + (b + 1) * size, :]
-    for number, piece in enumerate((0, 1, 2, 3, 5, 7, 9)):
-        for b in range(8):
-            xs[80 + number * 8 + b] = xs[piece * 8 + b].T
     copy.wait()
 
     def entries(h, g):
@@ -146,12 +143,14 @@
                 if h == g:
                     x_table[i * rows + j] = base + number
             if h != g:
-
-                @pl.when(straight)
-                def _():
-                    for i, j, number, slot in entries(h, g):
-                        x_table[i * rows + j] = base + number
-                        x_table[j * rows + i] = mirror + number
+                unused = jnp.where(straight, 0, rows * rows)
+                for i, j, number, slot in entries(h, g):
+                    x_table[unused + i * rows + j] = base + number
+                    x_table[unused + j * rows + i] = mirror + number
+
+    for number, piece in enumerate((0, 1, 2, 3, 5, 7, 9)):
+        for b in range(8):
+            xs[80 + number * 8 + b] = xs[piece * 8 + b].T
 
     def wide(parts):
         return jnp.concatenate(parts, axis=1)
@@ -203,7 +202,7 @@
             qs[i * slots + t] = value.astype(jnp.bfloat16)
         return carry
 
-    lax.fori_loop(0, rows, polynomial, 0, unroll=8)
+    lax.fori_loop(0, rows, polynomial, 0, unroll=16)
 
     for a in range(2):
         i = band * 2 + a
@@ -261,7 +260,7 @@
             pltpu.VMEM((33, size, size), jnp.bfloat16),
             pltpu.VMEM((8, size), jnp.int32),
             pltpu.SMEM((8, size), jnp.int32),
-            pltpu.SMEM((256,), jnp.int32),
+            pltpu.SMEM((512,), jnp.int32),
             pltpu.SMEM((256,), jnp.int32),
             pltpu.SMEM((128,), jnp.int32),
             pltpu.SemaphoreType.DMA,

time: 42.1 us -> 41.3 us (0.981)
  Pallas kernels: 9.95 us -> 9.12 us
    pallas_call x1, Pallas kernels: 8.66 us -> 7.83 us  [per_device_whole(): pl.pallas_call(local_iteration, out_shape=jax.ShapeDtypeStruct(values.sha...]
where the time goes in v9:
time: 41.3 us; the launch traced here: 41.1 us
  waiting for transfers between devices  16.8 us (41%)
  starting transfers between devices  14.1 us (34%)
  Pallas kernels  9.12 us (22%)
  local copies, waits for them, and re-layouts  0.81 us (2%)
    ppermute x3, waiting for transfers between devices, across(): return lax.ppermute(array, 'col', [(c, c ^ flip) for c in range(4)])  10.3 us
    ppermute x6, starting transfers between devices, around(): lax.ppermute(array, 'row', [(r, (r + 2 * step) % bands) for r in range(ba...  10 us
    pallas_call x1, Pallas kernels, per_device_whole(): pl.pallas_call(local_iteration, out_shape=jax.ShapeDtypeStruct(values.sha...  7.83 us
    ppermute x6, waiting for transfers between devices, around(): lax.ppermute(array, 'row', [(r, (r + 2 * step) % bands) for r in range(ba...  5.18 us
    ppermute x3, starting transfers between devices, across(): return lax.ppermute(array, 'col', [(c, c ^ flip) for c in range(4)])  3.55 us
    ppermute x4, waiting for transfers between devices, sibling(): return lax.ppermute(array, 'row', [(r, r ^ 1) for r in range(bands)])  1.33 us
    pallas_call x1, Pallas kernels, per_device_whole(): pl.pallas_call(make_tile, out_shape=jax.ShapeDtypeStruct((TILE, size), jn...  1.29 us
  transfers between devices with their start and end apart: 13, of which 6 were waited for; matrix products, arithmetic and copies ran while one was open for 1% of the time, Pallas kernels for 3%

profile of v9, /device:TPU:0, one launch (start us, length us, event | category | flops | bytes accessed | tf_op | source)
XLA Modules:
  0.0 41.1 jit_solution(5632626157757267586)
XLA Ops:
  0.0 5.0 %collective-permute-start.2 = (bf16[512,128]{1,0:T(8,128)(2,1)}, bf16[512,128]{1,0:T(8,128)(2,1)S(1)}, u32[]{:S(2)}, u32[]{:S(2)}) collective-permute-start(bf16[512,128]{1,0:T(8,128)(2,1)} %bitcast.16), channel_id=1, source_target_pairs={{0,24},{4,28},{8,0},{12,4},{16,8},{20,12},{24,16},{28,20},{1,25},{... | collective-permute-start | bytes 393224 | tf_op jit(solution)/shard_map/ppermute | solution.py:58
  5.1 0.0 collective-permute-start.1
  5.1 1.0 %collective-permute-start = (bf16[512,128]{1,0:T(8,128)(2,1)}, bf16[512,128]{1,0:T(8,128)(2,1)S(1)}, u32[]{:S(2)}, u32[]{:S(2)}) collective-permute-start(bf16[512,128]{1,0:T(8,128)(2,1)} %bitcast.18), channel_id=1, source_target_pairs={{0,8},{4,12},{8,16},{12,20},{16,24},{20,28},{24,0},{28,4},{1,9},{5... | collective-permute-start | bytes 393224 | tf_op jit(solution)/shard_map/ppermute | solution.py:58
  6.1 1.3 %shard_map.28 = bf16[16,128]{1,0:T(8,128)(2,1)} custom-call(s32[1]{0:T(128)} %bitcast.3.place, s32[2,2]{1,0:T(2,128)} %columns.1), custom_call_target="tpu_custom_call" | custom-call | tf_op jit(solution)/shard_map/pallas_call | solution.py:232
  7.4 2.8 %collective-permute-start.5 = (bf16[16,128]{1,0:T(8,128)(2,1)}, bf16[16,128]{1,0:T(8,128)(2,1)S(1)}, u32[]{:S(2)}, u32[]{:S(2)}) collective-permute-start(bf16[16,128]{1,0:T(8,128)(2,1)} %shard_map.28), channel_id=1, source_target_pairs={{0,24},{4,28},{8,0},{12,4},{16,8},{20,12},{24,16},{28,20},{1,25},{... | collective-permute-start | bytes 12296 | tf_op jit(solution)/shard_map/ppermute | solution.py:58
  10.2 1.1 %collective-permute-start.4 = (bf16[16,128]{1,0:T(8,128)(2,1)}, bf16[16,128]{1,0:T(8,128)(2,1)S(1)}, u32[]{:S(2)}, u32[]{:S(2)}) collective-permute-start(bf16[16,128]{1,0:T(8,128)(2,1)} %shard_map.28), channel_id=1, source_target_pairs={{0,16},{4,20},{8,24},{12,28},{16,0},{20,4},{24,8},{28,12},{1,17},{... | collective-permute-start | bytes 12296 | tf_op jit(solution)/shard_map/ppermute | solution.py:58
  11.3 0.0 collective-permute-done.2
  11.3 0.7 %copy-done.1 = bf16[16,128]{1,0:T(8,128)(2,1)S(1)} copy-done((bf16[16,128]{1,0:T(8,128)(2,1)S(1)}, bf16[16,128]{1,0:T(8,128)(2,1)}, u32[]{:S(2)}) %copy-start.1) | copy-done | bytes 4120
  12.0 0.0 collective-permute-start.3
  12.0 4.7 %collective-permute-done.1 = bf16[512,128]{1,0:T(8,128)(2,1)S(1)} collective-permute-done((bf16[512,128]{1,0:T(8,128)(2,1)}, bf16[512,128]{1,0:T(8,128)(2,1)S(1)}, u32[]{:S(2)}, u32[]{:S(2)}) %collective-permute-start.1) | collective-permute-done | bytes 131104 | tf_op jit(solution)/shard_map/ppermute | solution.py:58
  16.7 0.0 collective-permute-done
  16.7 0.1 pad_maximum_fusion
  16.9 0.0 collective-permute-done.5
  16.9 0.0 collective-permute-done.4
  16.9 0.5 %collective-permute-done.3 = bf16[16,128]{1,0:T(8,128)(2,1)S(1)} collective-permute-done((bf16[16,128]{1,0:T(8,128)(2,1)S(1)}, bf16[16,128]{1,0:T(8,128)(2,1)S(1)}, u32[]{:S(2)}, u32[]{:S(2)}) %collective-permute-start.3) | collective-permute-done | bytes 4128 | tf_op jit(solution)/shard_map/ppermute | solution.py:58
  17.4 0.1 pad_maximum_fusion.1
  17.5 2.5 %collective-permute-start.9 = (bf16[1040,128]{1,0:T(8,128)(2,1)S(1)}, bf16[1040,128]{1,0:T(8,128)(2,1)S(1)}, u32[]{:S(2)}, u32[]{:S(2)}) collective-permute-start(bf16[1040,128]{1,0:T(8,128)(2,1)S(1)} %get-tuple-element.11), channel_id=1, source_target_pairs={{0,3},{1,2},{2,1},{3,0},{4,7},{5,6},{6,5},{7,4},{8,11},{9,10},{10,... | collective-permute-start | bytes 798728 | tf_op jit(solution)/shard_map/ppermute | solution.py:62
  20.0 0.5 %collective-permute-start.7 = (bf16[1040,128]{1,0:T(8,128)(2,1)S(1)}, bf16[1040,128]{1,0:T(8,128)(2,1)S(1)}, u32[]{:S(2)}, u32[]{:S(2)}) collective-permute-start(bf16[1040,128]{1,0:T(8,128)(2,1)S(1)} %get-tuple-element.12), channel_id=1, source_target_pairs={{0,1},{1,0},{2,3},{3,2},{4,5},{5,4},{6,7},{7,6},{8,9},{9,8},{10,11... | collective-permute-start | bytes 798728 | tf_op jit(solution)/shard_map/ppermute | solution.py:62
  20.5 0.5 %collective-permute-start.8 = (bf16[1040,128]{1,0:T(8,128)(2,1)S(1)}, bf16[1040,128]{1,0:T(8,128)(2,1)S(1)}, u32[]{:S(2)}, u32[]{:S(2)}) collective-permute-start(bf16[1040,128]{1,0:T(8,128)(2,1)S(1)} %get-tuple-element.13), channel_id=1, source_target_pairs={{0,2},{1,3},{2,0},{3,1},{4,6},{5,7},{6,4},{7,5},{8,10},{9,11},{10,... | collective-permute-start | bytes 798728 | tf_op jit(solution)/shard_map/ppermute | solution.py:62
  21.1 0.0 collective-permute-start.6
  21.1 6.8 %collective-permute-done.9.rest_4_ = bf16[1040,128]{1,0:T(8,128)(2,1)S(1)} collective-permute-done((bf16[1040,128]{1,0:T(8,128)(2,1)S(1)}, bf16[1040,128]{1,0:T(8,128)(2,1)S(1)}, u32[]{:S(2)}, u32[]{:S(2)}) %collective-permute-start.9) | collective-permute-done | bytes 266272 | tf_op jit(solution)/shard_map/ppermute | solution.py:62
  27.8 0.0 collective-permute-start.12
  27.8 3.5 %collective-permute-done.7.rest_2_ = bf16[1040,128]{1,0:T(8,128)(2,1)S(1)} collective-permute-done((bf16[1040,128]{1,0:T(8,128)(2,1)S(1)}, bf16[1040,128]{1,0:T(8,128)(2,1)S(1)}, u32[]{:S(2)}, u32[]{:S(2)}) %collective-permute-start.7) | collective-permute-done | bytes 266272 | tf_op jit(solution)/shard_map/ppermute | solution.py:62
  31.3 0.0 collective-permute-start.10
  31.4 0.0 collective-permute-done.8.rest_3_
  31.4 0.5 %collective-permute-start.11 = (bf16[1040,128]{1,0:T(8,128)(2,1)S(1)}, bf16[1040,128]{1,0:T(8,128)(2,1)S(1)}, u32[]{:S(2)}, u32[]{:S(2)}) collective-permute-start(bf16[1040,128]{1,0:T(8,128)(2,1)S(1)} %collective-permute-done.8.rest_3_), channel_id=1, source_target_pairs={{0,4},{4,0},{8,12},{12,8},{16,20},{20,16},{24,28},{28,24},{1,5},{5... | collective-permute-start | bytes 798728 | tf_op jit(solution)/shard_map/ppermute | solution.py:66
  31.9 0.1 pad_add_fusion.origin
  31.9 0.0 collective-permute-done.6.rest_1_
  31.9 0.0 collective-permute-done.12.rest_7_
  31.9 0.9 %collective-permute-done.10.rest_5_ = bf16[1040,128]{1,0:T(8,128)(2,1)S(1)} collective-permute-done((bf16[1040,128]{1,0:T(8,128)(2,1)S(1)}, bf16[1040,128]{1,0:T(8,128)(2,1)S(1)}, u32[]{:S(2)}, u32[]{:S(2)}) %collective-permute-start.10) | collective-permute-done | bytes 266272 | tf_op jit(solution)/shard_map/ppermute | solution.py:66
  32.9 0.4 collective-permute-done.11.rest_6_
  33.3 7.8 %shard_map.29 = f32[2,2,128,128]{3,2,1,0:T(8,128)} custom-call(s32[2]{0:T(128)S(1)} %pad_add_fusion.origin, bf16[2064,128]{1,0:T(8,128)(2,1)S(1)} %get-tuple-element.5.rest_0_, bf16[2064,128]{1,0:T(8,128)(2,1)S(1)} %collective-permute-done.6.rest_1_, bf16[1040,128]{1,0:T(8,128)(2,1)S(1)} %collective-permute-done.7.rest_2_, ...), custom_call_target="tpu_custom_call" | custom-call | tf_op jit(solution)/shard_map/pallas_call | solution.py:252
  (9 shorter events, 0.1 us)
Async XLA Ops:
  0.0 11.3 %copy-start = (bf16[2,2,128,128]{3,2,1,0:T(8,128)(2,1)S(1)}, bf16[2,2,128,128]{3,2,1,0:T(8,128)(2,1)}, u32[]{:S(2)}) copy-start(bf16[2,2,128,128]{3,2,1,0:T(8,128)(2,1)} %param.2) | copy-start | bytes 393220
  0.0 11.3 %collective-permute-start.2 = (bf16[512,128]{1,0:T(8,128)(2,1)}, bf16[512,128]{1,0:T(8,128)(2,1)S(1)}, u32[]{:S(2)}, u32[]{:S(2)}) collective-permute-start(bf16[512,128]{1,0:T(8,128)(2,1)} %bitcast.16), channel_id=1, source_target_pairs={{0,24},{4,28},{8,0},{12,4},{16,8},{20,12},{24,16},{28,20},{1,25},{... | collective-permute-start | bytes 393224 | tf_op jit(solution)/shard_map/ppermute | solution.py:58
  5.1 11.6 %collective-permute-start.1 = (bf16[512,128]{1,0:T(8,128)(2,1)}, bf16[512,128]{1,0:T(8,128)(2,1)S(1)}, u32[]{:S(2)}, u32[]{:S(2)}) collective-permute-start(bf16[512,128]{1,0:T(8,128)(2,1)} %bitcast.17), channel_id=1, source_target_pairs={{0,16},{4,20},{8,24},{12,28},{16,0},{20,4},{24,8},{28,12},{1,17},{... | collective-permute-start | bytes 393224 | tf_op jit(solution)/shard_map/ppermute | solution.py:58
  5.1 11.6 %collective-permute-start = (bf16[512,128]{1,0:T(8,128)(2,1)}, bf16[512,128]{1,0:T(8,128)(2,1)S(1)}, u32[]{:S(2)}, u32[]{:S(2)}) collective-permute-start(bf16[512,128]{1,0:T(8,128)(2,1)} %bitcast.18), channel_id=1, source_target_pairs={{0,8},{4,12},{8,16},{12,20},{16,24},{20,28},{24,0},{28,4},{1,9},{5... | collective-permute-start | bytes 393224 | tf_op jit(solution)/shard_map/ppermute | solution.py:58
  7.4 9.5 %collective-permute-start.5 = (bf16[16,128]{1,0:T(8,128)(2,1)}, bf16[16,128]{1,0:T(8,128)(2,1)S(1)}, u32[]{:S(2)}, u32[]{:S(2)}) collective-permute-start(bf16[16,128]{1,0:T(8,128)(2,1)} %shard_map.28), channel_id=1, source_target_pairs={{0,24},{4,28},{8,0},{12,4},{16,8},{20,12},{24,16},{28,20},{1,25},{... | collective-permute-start | bytes 12296 | tf_op jit(solution)/shard_map/ppermute | solution.py:58
  10.2 6.7 %collective-permute-start.4 = (bf16[16,128]{1,0:T(8,128)(2,1)}, bf16[16,128]{1,0:T(8,128)(2,1)S(1)}, u32[]{:S(2)}, u32[]{:S(2)}) collective-permute-start(bf16[16,128]{1,0:T(8,128)(2,1)} %shard_map.28), channel_id=1, source_target_pairs={{0,16},{4,20},{8,24},{12,28},{16,0},{20,4},{24,8},{28,12},{1,17},{... | collective-permute-start | bytes 12296 | tf_op jit(solution)/shard_map/ppermute | solution.py:58
  11.3 0.7 %copy-start.1 = (bf16[16,128]{1,0:T(8,128)(2,1)S(1)}, bf16[16,128]{1,0:T(8,128)(2,1)}, u32[]{:S(2)}) copy-start(bf16[16,128]{1,0:T(8,128)(2,1)} %shard_map.28) | copy-start | bytes 12292
  12.0 5.4 %collective-permute-start.3 = (bf16[16,128]{1,0:T(8,128)(2,1)S(1)}, bf16[16,128]{1,0:T(8,128)(2,1)S(1)}, u32[]{:S(2)}, u32[]{:S(2)}) collective-permute-start(bf16[16,128]{1,0:T(8,128)(2,1)S(1)} %copy-done.1), channel_id=1, source_target_pairs={{0,8},{4,12},{8,16},{12,20},{16,24},{20,28},{24,0},{28,4},{1,9},{5... | collective-permute-start | bytes 12296 | tf_op jit(solution)/shard_map/ppermute | solution.py:58
  17.5 10.3 %collective-permute-start.9 = (bf16[1040,128]{1,0:T(8,128)(2,1)S(1)}, bf16[1040,128]{1,0:T(8,128)(2,1)S(1)}, u32[]{:S(2)}, u32[]{:S(2)}) collective-permute-start(bf16[1040,128]{1,0:T(8,128)(2,1)S(1)} %get-tuple-element.11), channel_id=1, source_target_pairs={{0,3},{1,2},{2,1},{3,0},{4,7},{5,6},{6,5},{7,4},{8,11},{9,10},{10,... | collective-permute-start | bytes 798728 | tf_op jit(solution)/shard_map/ppermute | solution.py:62
  20.0 11.3 %collective-permute-start.7 = (bf16[1040,128]{1,0:T(8,128)(2,1)S(1)}, bf16[1040,128]{1,0:T(8,128)(2,1)S(1)}, u32[]{:S(2)}, u32[]{:S(2)}) collective-permute-start(bf16[1040,128]{1,0:T(8,128)(2,1)S(1)} %get-tuple-element.12), channel_id=1, source_target_pairs={{0,1},{1,0},{2,3},{3,2},{4,5},{5,4},{6,7},{7,6},{8,9},{9,8},{10,11... | collective-permute-start | bytes 798728 | tf_op jit(solution)/shard_map/ppermute | solution.py:62
  20.5 10.8 %collective-permute-start.8 = (bf16[1040,128]{1,0:T(8,128)(2,1)S(1)}, bf16[1040,128]{1,0:T(8,128)(2,1)S(1)}, u32[]{:S(2)}, u32[]{:S(2)}) collective-permute-start(bf16[1040,128]{1,0:T(8,128)(2,1)S(1)} %get-tuple-element.13), channel_id=1, source_target_pairs={{0,2},{1,3},{2,0},{3,1},{4,6},{5,7},{6,4},{7,5},{8,10},{9,11},{10,... | collective-permute-start | bytes 798728 | tf_op jit(solution)/shard_map/ppermute | solution.py:62
  21.1 10.9 %collective-permute-start.6 = (bf16[2064,128]{1,0:T(8,128)(2,1)S(1)}, bf16[2064,128]{1,0:T(8,128)(2,1)S(1)}, u32[]{:S(2)}, u32[]{:S(2)}) collective-permute-start(bf16[2064,128]{1,0:T(8,128)(2,1)S(1)} %get-tuple-element.5.rest_0_), channel_id=1, source_target_pairs={{0,4},{4,0},{8,12},{12,8},{16,20},{20,16},{24,28},{28,24},{1,5},{5... | collective-permute-start | bytes 1585160 | tf_op jit(solution)/shard_map/ppermute | solution.py:66
  27.8 4.1 %collective-permute-start.12 = (bf16[1040,128]{1,0:T(8,128)(2,1)S(1)}, bf16[1040,128]{1,0:T(8,128)(2,1)S(1)}, u32[]{:S(2)}, u32[]{:S(2)}) collective-permute-start(bf16[1040,128]{1,0:T(8,128)(2,1)S(1)} %collective-permute-done.9.rest_4_), channel_id=1, source_target_pairs={{0,4},{4,0},{8,12},{12,8},{16,20},{20,16},{24,28},{28,24},{1,5},{5... | collective-permute-start | bytes 798728 | tf_op jit(solution)/shard_map/ppermute | solution.py:66
  31.3 1.5 %collective-permute-start.10 = (bf16[1040,128]{1,0:T(8,128)(2,1)S(1)}, bf16[1040,128]{1,0:T(8,128)(2,1)S(1)}, u32[]{:S(2)}, u32[]{:S(2)}) collective-permute-start(bf16[1040,128]{1,0:T(8,128)(2,1)S(1)} %collective-permute-done.7.rest_2_), channel_id=1, source_target_pairs={{0,4},{4,0},{8,12},{12,8},{16,20},{20,16},{24,28},{28,24},{1,5},{5... | collective-permute-start | bytes 798728 | tf_op jit(solution)/shard_map/ppermute | solution.py:66
  31.4 1.9 %collective-permute-start.11 = (bf16[1040,128]{1,0:T(8,128)(2,1)S(1)}, bf16[1040,128]{1,0:T(8,128)(2,1)S(1)}, u32[]{:S(2)}, u32[]{:S(2)}) collective-permute-start(bf16[1040,128]{1,0:T(8,128)(2,1)S(1)} %collective-permute-done.8.rest_3_), channel_id=1, source_target_pairs={{0,4},{4,0},{8,12},{12,8},{16,20},{20,16},{24,28},{28,24},{1,5},{5... | collective-permute-start | bytes 798728 | tf_op jit(solution)/shard_map/ppermute | solution.py:66

commit v10 on v9

--- a/solution.py
+++ b/solution.py
@@ -80,9 +80,17 @@
     out[...] = tile.astype(jnp.float32).astype(jnp.bfloat16)
 
 
+def mirror_line(line, out):
+    size = out.shape[1]
+    for step in range(4):
+        for b in range(4):
+            out[step * 4 + b] = line[step, b * size : (b + 1) * size, :].T
+
+
 def local_iteration(origin, *rest):
     lines, planes = rest[:2], (rest[2:5], rest[5:8])
-    out, xs, ys, qs, numbers, pattern, x_table, y_table, near, sem = rest[8:]
+    out, xs, ys, qs, numbers, pattern, x_table, y_table, near, sem = rest[9:]
+    mirrored = rest[8]
     rows, kept, slots, size = 16, 8, 2, 128
     band, c = origin[0], origin[1]
     z, core = lax.div(band, 2), lax.rem(band, 2)
@@ -148,9 +156,14 @@
                     x_table[unused + i * rows + j] = base + number
                     x_table[unused + j * rows + i] = mirror + number
 
-    for number, piece in enumerate((0, 1, 2, 3, 5, 7, 9)):
+    for step in range(4):
+        for b in range(4):
+            first = step * part_rows + b * size
+            xs[80 + step * 8 + core * 4 + b] = mirrored[step * 4 + b]
+            xs[80 + step * 8 + (1 - core) * 4 + b] = lines[1][first : first + size, :].T
+    for number, piece in enumerate((5, 7, 9)):
         for b in range(8):
-            xs[80 + number * 8 + b] = xs[piece * 8 + b].T
+            xs[112 + number * 8 + b] = xs[piece * 8 + b].T
 
     def wide(parts):
         return jnp.concatenate(parts, axis=1)
@@ -247,12 +260,19 @@
         here.append(across(jnp.concatenate(parts + [tile]), flip))
     line = jnp.concatenate(line + [tile])
     line_there = sibling(line, bands)
+    mirrored = pl.pallas_call(
+        mirror_line,
+        out_shape=jax.ShapeDtypeStruct((16, size, size), jnp.bfloat16),
+        in_specs=[vmem],
+        out_specs=vmem,
+    )(stacked)
+    mirrored, *here = lax.optimization_barrier((mirrored, *here))
     there = [sibling(piece, bands) for piece in here]
     origin = jnp.stack([band, c]).astype(jnp.int32)
     return pl.pallas_call(
         local_iteration,
         out_shape=jax.ShapeDtypeStruct(values.shape, jnp.float32),
-        in_specs=[smem] + [vmem] * 8,
+        in_specs=[smem] + [vmem] * 9,
         out_specs=vmem,
         scratch_shapes=[
             pltpu.VMEM((17 * 8 + 1, size, size), jnp.bfloat16),
@@ -266,7 +286,7 @@
             pltpu.SemaphoreType.DMA,
         ],
         compiler_params=pltpu.CompilerParams(vmem_limit_bytes=32 * 1024 * 1024),
-    )(origin, line, line_there, *here, *there)
+    )(origin, line, line_there, *here, *there, mirrored)
 
 
 def per_device(values, columns):

time: 41.3 us -> 43.7 us (1.058)
  Pallas kernels: 9.12 us -> 11.3 us
  local copies, waits for them, and re-layouts: 0.81 us -> 2.59 us
  waiting for transfers between devices: 16.8 us -> 15.1 us
    pallas_call x0 -> x1, Pallas kernels: none -> 2.03 us  [per_device_whole(): pl.pallas_call(mirror_line, out_shape=jax.ShapeDtypeStruct((16, size, siz...]
    unnamed x8 -> x12, local copies, waits for them, and re-layouts: 0.77 us -> 2.54 us
    ppermute x3, waiting for transfers between devices: 10.3 us -> 8.75 us  [across(): return lax.ppermute(array, 'col', [(c, c ^ flip) for c in range(4)])]
    ppermute x6, waiting for transfers between devices: 5.18 us -> 4.68 us  [around(): lax.ppermute(array, 'row', [(r, (r + 2 * step) % bands) for r in range(ba...]
  transfers between devices with their start and end apart: 13 -> 13, of which waited for: 6 -> 6; matrix products, arithmetic and copies ran while one was open for 1% -> 1% of each run, Pallas kernels for 3% -> 8%
where the time goes in v10:
time: 43.7 us; the launch traced here: 43.4 us
  waiting for transfers between devices  15.1 us (35%)
  starting transfers between devices  14.1 us (32%)
  Pallas kernels  11.3 us (26%)
  local copies, waits for them, and re-layouts  2.59 us (6%)
    ppermute x6, starting transfers between devices, around(): lax.ppermute(array, 'row', [(r, (r + 2 * step) % bands) for r in range(ba...  10 us
    ppermute x3, waiting for transfers between devices, across(): return lax.ppermute(array, 'col', [(c, c ^ flip) for c in range(4)])  8.75 us
    pallas_call x1, Pallas kernels, per_device_whole(): pl.pallas_call(local_iteration, out_shape=jax.ShapeDtypeStruct(values.sha...  8 us
    ppermute x6, waiting for transfers between devices, around(): lax.ppermute(array, 'row', [(r, (r + 2 * step) % bands) for r in range(ba...  4.68 us
    ppermute x3, starting transfers between devices, across(): return lax.ppermute(array, 'col', [(c, c ^ flip) for c in range(4)])  3.55 us
    unnamed x12, local copies, waits for them, and re-layouts  2.54 us
    pallas_call x1, Pallas kernels, per_device_whole(): pl.pallas_call(mirror_line, out_shape=jax.ShapeDtypeStruct((16, size, siz...  2.03 us
    ppermute x4, waiting for transfers between devices, sibling(): return lax.ppermute(array, 'row', [(r, r ^ 1) for r in range(bands)])  1.71 us
  transfers between devices with their start and end apart: 13, of which 6 were waited for; matrix products, arithmetic and copies ran while one was open for 1% of the time, Pallas kernels for 8%

profile of v10, /device:TPU:0, one launch (start us, length us, event | category | flops | bytes accessed | tf_op | source)
XLA Modules:
  0.0 43.4 jit_solution(4492020256295729205)
XLA Ops:
  0.0 5.0 %collective-permute-start.2 = (bf16[512,128]{1,0:T(8,128)(2,1)}, bf16[512,128]{1,0:T(8,128)(2,1)S(1)}, u32[]{:S(2)}, u32[]{:S(2)}) collective-permute-start(bf16[512,128]{1,0:T(8,128)(2,1)} %bitcast.16), channel_id=1, source_target_pairs={{0,24},{4,28},{8,0},{12,4},{16,8},{20,12},{24,16},{28,20},{1,25},{... | collective-permute-start | bytes 393224 | tf_op jit(solution)/shard_map/ppermute | solution.py:58
  5.1 0.0 collective-permute-start.1
  5.1 1.0 %collective-permute-start = (bf16[512,128]{1,0:T(8,128)(2,1)}, bf16[512,128]{1,0:T(8,128)(2,1)S(1)}, u32[]{:S(2)}, u32[]{:S(2)}) collective-permute-start(bf16[512,128]{1,0:T(8,128)(2,1)} %bitcast.18), channel_id=1, source_target_pairs={{0,8},{4,12},{8,16},{12,20},{16,24},{20,28},{24,0},{28,4},{1,9},{5... | collective-permute-start | bytes 393224 | tf_op jit(solution)/shard_map/ppermute | solution.py:58
  6.1 1.3 %shard_map.28 = bf16[16,128]{1,0:T(8,128)(2,1)} custom-call(s32[1]{0:T(128)} %bitcast.3.place, s32[2,2]{1,0:T(2,128)} %columns.1), custom_call_target="tpu_custom_call" | custom-call | tf_op jit(solution)/shard_map/pallas_call | solution.py:245
  7.4 2.8 %collective-permute-start.5 = (bf16[16,128]{1,0:T(8,128)(2,1)}, bf16[16,128]{1,0:T(8,128)(2,1)S(1)}, u32[]{:S(2)}, u32[]{:S(2)}) collective-permute-start(bf16[16,128]{1,0:T(8,128)(2,1)} %shard_map.28), channel_id=1, source_target_pairs={{0,24},{4,28},{8,0},{12,4},{16,8},{20,12},{24,16},{28,20},{1,25},{... | collective-permute-start | bytes 12296 | tf_op jit(solution)/shard_map/ppermute | solution.py:58
  10.2 1.1 %collective-permute-start.4 = (bf16[16,128]{1,0:T(8,128)(2,1)}, bf16[16,128]{1,0:T(8,128)(2,1)S(1)}, u32[]{:S(2)}, u32[]{:S(2)}) collective-permute-start(bf16[16,128]{1,0:T(8,128)(2,1)} %shard_map.28), channel_id=1, source_target_pairs={{0,16},{4,20},{8,24},{12,28},{16,0},{20,4},{24,8},{28,12},{1,17},{... | collective-permute-start | bytes 12296 | tf_op jit(solution)/shard_map/ppermute | solution.py:58
  11.3 0.0 collective-permute-done.2
  11.3 0.7 %copy-done.3 = bf16[16,128]{1,0:T(8,128)(2,1)S(1)} copy-done((bf16[16,128]{1,0:T(8,128)(2,1)S(1)}, bf16[16,128]{1,0:T(8,128)(2,1)}, u32[]{:S(2)}) %copy-start.3) | copy-done | bytes 4120
  12.0 0.0 collective-permute-start.3
  12.0 4.7 %collective-permute-done.1 = bf16[512,128]{1,0:T(8,128)(2,1)S(1)} collective-permute-done((bf16[512,128]{1,0:T(8,128)(2,1)}, bf16[512,128]{1,0:T(8,128)(2,1)S(1)}, u32[]{:S(2)}, u32[]{:S(2)}) %collective-permute-start.1) | collective-permute-done | bytes 131104 | tf_op jit(solution)/shard_map/ppermute | solution.py:58
  16.7 0.0 collective-permute-done
  16.7 0.1 pad_maximum_fusion.line
  16.8 0.7 %copy-done.1 = bf16[4,512,128]{2,1,0:T(8,128)(2,1)} copy-done((bf16[4,512,128]{2,1,0:T(8,128)(2,1)}, bf16[4,512,128]{2,1,0:T(8,128)(2,1)S(1)}, u32[]{:S(2)}) %copy-start.1) | copy-done | bytes 524312
  17.6 0.0 collective-permute-done.4
  17.7 0.0 collective-permute-done.3
  17.7 0.1 pad_maximum_fusion.1
  17.8 2.5 %collective-permute-start.9 = (bf16[1040,128]{1,0:T(8,128)(2,1)S(1)}, bf16[1040,128]{1,0:T(8,128)(2,1)S(1)}, u32[]{:S(2)}, u32[]{:S(2)}) collective-permute-start(bf16[1040,128]{1,0:T(8,128)(2,1)S(1)} %get-tuple-element.19), channel_id=1, source_target_pairs={{0,3},{1,2},{2,1},{3,0},{4,7},{5,6},{6,5},{7,4},{8,11},{9,10},{10,... | collective-permute-start | bytes 798728 | tf_op jit(solution)/shard_map/ppermute | solution.py:62
  20.3 0.5 %collective-permute-start.7 = (bf16[1040,128]{1,0:T(8,128)(2,1)S(1)}, bf16[1040,128]{1,0:T(8,128)(2,1)S(1)}, u32[]{:S(2)}, u32[]{:S(2)}) collective-permute-start(bf16[1040,128]{1,0:T(8,128)(2,1)S(1)} %get-tuple-element.20), channel_id=1, source_target_pairs={{0,1},{1,0},{2,3},{3,2},{4,5},{5,4},{6,7},{7,6},{8,9},{9,8},{10,11... | collective-permute-start | bytes 798728 | tf_op jit(solution)/shard_map/ppermute | solution.py:62
  20.8 0.5 %collective-permute-start.8 = (bf16[1040,128]{1,0:T(8,128)(2,1)S(1)}, bf16[1040,128]{1,0:T(8,128)(2,1)S(1)}, u32[]{:S(2)}, u32[]{:S(2)}) collective-permute-start(bf16[1040,128]{1,0:T(8,128)(2,1)S(1)} %get-tuple-element.21), channel_id=1, source_target_pairs={{0,2},{1,3},{2,0},{3,1},{4,6},{5,7},{6,4},{7,5},{8,10},{9,11},{10,... | collective-permute-start | bytes 798728 | tf_op jit(solution)/shard_map/ppermute | solution.py:62
  21.3 2.0 %shard_map.29.rest_8_ = bf16[16,128,128]{2,1,0:T(8,128)(2,1)} custom-call(bf16[4,512,128]{2,1,0:T(8,128)(2,1)} %copy-done.1), custom_call_target="tpu_custom_call" | custom-call | tf_op jit(solution)/shard_map/pallas_call | solution.py:263
  23.3 4.8 %collective-permute-done.9.rest_4_ = bf16[1040,128]{1,0:T(8,128)(2,1)S(1)} collective-permute-done((bf16[1040,128]{1,0:T(8,128)(2,1)S(1)}, bf16[1040,128]{1,0:T(8,128)(2,1)S(1)}, u32[]{:S(2)}, u32[]{:S(2)}) %collective-permute-start.9) | collective-permute-done | bytes 266272 | tf_op jit(solution)/shard_map/ppermute | solution.py:62
  28.1 4.0 %collective-permute-done.7.rest_2_ = bf16[1040,128]{1,0:T(8,128)(2,1)S(1)} collective-permute-done((bf16[1040,128]{1,0:T(8,128)(2,1)S(1)}, bf16[1040,128]{1,0:T(8,128)(2,1)S(1)}, u32[]{:S(2)}, u32[]{:S(2)}) %collective-permute-start.7) | collective-permute-done | bytes 266272 | tf_op jit(solution)/shard_map/ppermute | solution.py:62
  32.1 0.0 collective-permute-done.8.rest_3_
  32.1 0.0 collective-permute-start.10
  32.1 0.5 %collective-permute-start.11 = (bf16[1040,128]{1,0:T(8,128)(2,1)S(1)}, bf16[1040,128]{1,0:T(8,128)(2,1)S(1)}, u32[]{:S(2)}, u32[]{:S(2)}) collective-permute-start(bf16[1040,128]{1,0:T(8,128)(2,1)S(1)} %collective-permute-done.8.rest_3_), channel_id=1, source_target_pairs={{0,4},{4,0},{8,12},{12,8},{16,20},{20,16},{24,28},{28,24},{1,5},{5... | collective-permute-start | bytes 798728 | tf_op jit(solution)/shard_map/ppermute | solution.py:66
  32.6 0.0 collective-permute-start.12
  32.6 0.1 pad_add_fusion.origin
  32.7 0.9 %collective-permute-done.10.rest_5_ = bf16[1040,128]{1,0:T(8,128)(2,1)S(1)} collective-permute-done((bf16[1040,128]{1,0:T(8,128)(2,1)S(1)}, bf16[1040,128]{1,0:T(8,128)(2,1)S(1)}, u32[]{:S(2)}, u32[]{:S(2)}) %collective-permute-start.10) | collective-permute-done | bytes 266272 | tf_op jit(solution)/shard_map/ppermute | solution.py:66
  33.6 0.4 collective-permute-done.11.rest_6_
  34.0 0.4 collective-permute-done.12.rest_7_
  34.4 1.0 %copy-done = bf16[16,128,128]{2,1,0:T(8,128)(2,1)S(1)} copy-done((bf16[16,128,128]{2,1,0:T(8,128)(2,1)S(1)}, bf16[16,128,128]{2,1,0:T(8,128)(2,1)}, u32[]{:S(2)}) %copy-start) | copy-done | bytes 524312
  35.4 8.0 %shard_map.30 = f32[2,2,128,128]{3,2,1,0:T(8,128)} custom-call(s32[2]{0:T(128)S(1)} %pad_add_fusion.origin, bf16[2064,128]{1,0:T(8,128)(2,1)S(1)} %get-tuple-element.13.rest_0_, bf16[2064,128]{1,0:T(8,128)(2,1)S(1)} %collective-permute-done.6.rest_1_, bf16[1040,128]{1,0:T(8,128)(2,1)S(1)} %collective-permute-done.7.rest_2_, ...), custom_call_target="tpu_custom_call" | custom-call | tf_op jit(solution)/shard_map/pallas_call | solution.py:272
  (14 shorter events, 0.1 us)
Async XLA Ops:
  0.0 11.3 %copy-start.2 = (bf16[2,2,128,128]{3,2,1,0:T(8,128)(2,1)S(1)}, bf16[2,2,128,128]{3,2,1,0:T(8,128)(2,1)}, u32[]{:S(2)}) copy-start(bf16[2,2,128,128]{3,2,1,0:T(8,128)(2,1)} %param.2) | copy-start | bytes 393220
  0.0 11.3 %collective-permute-start.2 = (bf16[512,128]{1,0:T(8,128)(2,1)}, bf16[512,128]{1,0:T(8,128)(2,1)S(1)}, u32[]{:S(2)}, u32[]{:S(2)}) collective-permute-start(bf16[512,128]{1,0:T(8,128)(2,1)} %bitcast.16), channel_id=1, source_target_pairs={{0,24},{4,28},{8,0},{12,4},{16,8},{20,12},{24,16},{28,20},{1,25},{... | collective-permute-start | bytes 393224 | tf_op jit(solution)/shard_map/ppermute | solution.py:58
  5.1 11.6 %collective-permute-start.1 = (bf16[512,128]{1,0:T(8,128)(2,1)}, bf16[512,128]{1,0:T(8,128)(2,1)S(1)}, u32[]{:S(2)}, u32[]{:S(2)}) collective-permute-start(bf16[512,128]{1,0:T(8,128)(2,1)} %bitcast.17), channel_id=1, source_target_pairs={{0,16},{4,20},{8,24},{12,28},{16,0},{20,4},{24,8},{28,12},{1,17},{... | collective-permute-start | bytes 393224 | tf_op jit(solution)/shard_map/ppermute | solution.py:58
  5.1 11.6 %collective-permute-start = (bf16[512,128]{1,0:T(8,128)(2,1)}, bf16[512,128]{1,0:T(8,128)(2,1)S(1)}, u32[]{:S(2)}, u32[]{:S(2)}) collective-permute-start(bf16[512,128]{1,0:T(8,128)(2,1)} %bitcast.18), channel_id=1, source_target_pairs={{0,8},{4,12},{8,16},{12,20},{16,24},{20,28},{24,0},{28,4},{1,9},{5... | collective-permute-start | bytes 393224 | tf_op jit(solution)/shard_map/ppermute | solution.py:58
  7.4 10.3 %collective-permute-start.5 = (bf16[16,128]{1,0:T(8,128)(2,1)}, bf16[16,128]{1,0:T(8,128)(2,1)S(1)}, u32[]{:S(2)}, u32[]{:S(2)}) collective-permute-start(bf16[16,128]{1,0:T(8,128)(2,1)} %shard_map.28), channel_id=1, source_target_pairs={{0,24},{4,28},{8,0},{12,4},{16,8},{20,12},{24,16},{28,20},{1,25},{... | collective-permute-start | bytes 12296 | tf_op jit(solution)/shard_map/ppermute | solution.py:58
  10.2 7.5 %collective-permute-start.4 = (bf16[16,128]{1,0:T(8,128)(2,1)}, bf16[16,128]{1,0:T(8,128)(2,1)S(1)}, u32[]{:S(2)}, u32[]{:S(2)}) collective-permute-start(bf16[16,128]{1,0:T(8,128)(2,1)} %shard_map.28), channel_id=1, source_target_pairs={{0,16},{4,20},{8,24},{12,28},{16,0},{20,4},{24,8},{28,12},{1,17},{... | collective-permute-start | bytes 12296 | tf_op jit(solution)/shard_map/ppermute | solution.py:58
  11.3 0.7 %copy-start.3 = (bf16[16,128]{1,0:T(8,128)(2,1)S(1)}, bf16[16,128]{1,0:T(8,128)(2,1)}, u32[]{:S(2)}) copy-start(bf16[16,128]{1,0:T(8,128)(2,1)} %shard_map.28) | copy-start | bytes 12292
  12.0 5.6 %collective-permute-start.3 = (bf16[16,128]{1,0:T(8,128)(2,1)S(1)}, bf16[16,128]{1,0:T(8,128)(2,1)S(1)}, u32[]{:S(2)}, u32[]{:S(2)}) collective-permute-start(bf16[16,128]{1,0:T(8,128)(2,1)S(1)} %copy-done.3), channel_id=1, source_target_pairs={{0,8},{4,12},{8,16},{12,20},{16,24},{20,28},{24,0},{28,4},{1,9},{5... | collective-permute-start | bytes 12296 | tf_op jit(solution)/shard_map/ppermute | solution.py:58
  16.8 0.8 %copy-start.1 = (bf16[4,512,128]{2,1,0:T(8,128)(2,1)}, bf16[4,512,128]{2,1,0:T(8,128)(2,1)S(1)}, u32[]{:S(2)}) copy-start(bf16[4,512,128]{2,1,0:T(8,128)(2,1)S(1)} %pad_maximum_fusion.line) | copy-start | bytes 1572868
  17.8 10.3 %collective-permute-start.9 = (bf16[1040,128]{1,0:T(8,128)(2,1)S(1)}, bf16[1040,128]{1,0:T(8,128)(2,1)S(1)}, u32[]{:S(2)}, u32[]{:S(2)}) collective-permute-start(bf16[1040,128]{1,0:T(8,128)(2,1)S(1)} %get-tuple-element.19), channel_id=1, source_target_pairs={{0,3},{1,2},{2,1},{3,0},{4,7},{5,6},{6,5},{7,4},{8,11},{9,10},{10,... | collective-permute-start | bytes 798728 | tf_op jit(solution)/shard_map/ppermute | solution.py:62
  20.3 11.8 %collective-permute-start.7 = (bf16[1040,128]{1,0:T(8,128)(2,1)S(1)}, bf16[1040,128]{1,0:T(8,128)(2,1)S(1)}, u32[]{:S(2)}, u32[]{:S(2)}) collective-permute-start(bf16[1040,128]{1,0:T(8,128)(2,1)S(1)} %get-tuple-element.20), channel_id=1, source_target_pairs={{0,1},{1,0},{2,3},{3,2},{4,5},{5,4},{6,7},{7,6},{8,9},{9,8},{10,11... | collective-permute-start | bytes 798728 | tf_op jit(solution)/shard_map/ppermute | solution.py:62
  20.8 11.3 %collective-permute-start.8 = (bf16[1040,128]{1,0:T(8,128)(2,1)S(1)}, bf16[1040,128]{1,0:T(8,128)(2,1)S(1)}, u32[]{:S(2)}, u32[]{:S(2)}) collective-permute-start(bf16[1040,128]{1,0:T(8,128)(2,1)S(1)} %get-tuple-element.21), channel_id=1, source_target_pairs={{0,2},{1,3},{2,0},{3,1},{4,6},{5,7},{6,4},{7,5},{8,10},{9,11},{10,... | collective-permute-start | bytes 798728 | tf_op jit(solution)/shard_map/ppermute | solution.py:62
  21.3 11.4 %collective-permute-start.6 = (bf16[2064,128]{1,0:T(8,128)(2,1)S(1)}, bf16[2064,128]{1,0:T(8,128)(2,1)S(1)}, u32[]{:S(2)}, u32[]{:S(2)}) collective-permute-start(bf16[2064,128]{1,0:T(8,128)(2,1)S(1)} %get-tuple-element.13.rest_0_), channel_id=1, source_target_pairs={{0,4},{4,0},{8,12},{12,8},{16,20},{20,16},{24,28},{28,24},{1,5},{5... | collective-permute-start | bytes 1585160 | tf_op jit(solution)/shard_map/ppermute | solution.py:66
  32.1 1.5 %collective-permute-start.10 = (bf16[1040,128]{1,0:T(8,128)(2,1)S(1)}, bf16[1040,128]{1,0:T(8,128)(2,1)S(1)}, u32[]{:S(2)}, u32[]{:S(2)}) collective-permute-start(bf16[1040,128]{1,0:T(8,128)(2,1)S(1)} %collective-permute-done.7.rest_2_), channel_id=1, source_target_pairs={{0,4},{4,0},{8,12},{12,8},{16,20},{20,16},{24,28},{28,24},{1,5},{5... | collective-permute-start | bytes 798728 | tf_op jit(solution)/shard_map/ppermute | solution.py:66
  32.1 1.9 %collective-permute-start.11 = (bf16[1040,128]{1,0:T(8,128)(2,1)S(1)}, bf16[1040,128]{1,0:T(8,128)(2,1)S(1)}, u32[]{:S(2)}, u32[]{:S(2)}) collective-permute-start(bf16[1040,128]{1,0:T(8,128)(2,1)S(1)} %collective-permute-done.8.rest_3_), channel_id=1, source_target_pairs={{0,4},{4,0},{8,12},{12,8},{16,20},{20,16},{24,28},{28,24},{1,5},{5... | collective-permute-start | bytes 798728 | tf_op jit(solution)/shard_map/ppermute | solution.py:66
  32.6 1.8 %collective-permute-start.12 = (bf16[1040,128]{1,0:T(8,128)(2,1)S(1)}, bf16[1040,128]{1,0:T(8,128)(2,1)S(1)}, u32[]{:S(2)}, u32[]{:S(2)}) collective-permute-start(bf16[1040,128]{1,0:T(8,128)(2,1)S(1)} %collective-permute-done.9.rest_4_), channel_id=1, source_target_pairs={{0,4},{4,0},{8,12},{12,8},{16,20},{20,16},{24,28},{28,24},{1,5},{5... | collective-permute-start | bytes 798728 | tf_op jit(solution)/shard_map/ppermute | solution.py:66
  34.4 1.0 %copy-start = (bf16[16,128,128]{2,1,0:T(8,128)(2,1)S(1)}, bf16[16,128,128]{2,1,0:T(8,128)(2,1)}, u32[]{:S(2)}) copy-start(bf16[16,128,128]{2,1,0:T(8,128)(2,1)} %shard_map.29.rest_8_) | copy-start | bytes 1572868
